TPU v7x, 32 devices: a whole 2x2x4 slice. The times are simulated.
32 devices in a mesh: row: 4 (over x, core), col: 8 (over z, y).
Axes of the slice: x: 2, y: 2, z: 4, core: 2. Of those that a mesh axis runs over, the one named last changes fastest.
Arguments:
- test_points: float32 [3, 512], P(None, ('row', 'col')), may hold values from 0 to 1
- src_points: float32 [3, 32768], P(None, ('row', 'col')), may hold values from 0 to 1
- currents: float32 [2, 32768], P(None, ('row', 'col')), may hold values from -6 to 6
- near_blocks: float32 [256, 2, 16, 128], P(('row', 'col')), may hold values from -0.3 to 0.3
- near_dest: int32 [256, 1], P(('row', 'col')), may hold values from 0 to 7; in each aligned block of 8 rows (0 to 7, 8 to 15, ...) at most 2 rows name the same one
- near_tile: int32 [256, 1], P(('row', 'col')), may hold values from 0 to 7
Outputs:
- field: float32 [2, 512], P(None, ('row', 'col'))
Inputs may be any that keep to these rules, and one draw needn't show every extreme that they name: `near_dest`: among the 8 blocks held by one device, at most 2 name the same column index; some device reaches 2 in every draw.
All inputs are finite; a program needn't handle non-finite values.
Results may differ from a plain program's by a relative error of at most 0.0003.
Values sent between devices are 32-bit elements; how exact they have to be, the bound alone decides.
No kernel may reach another device: no remote copies, remote signals or barrier semaphores. Data moves between devices by JAX's collectives and lax.ppermute only.
A program may use at most 64 MiB of HBM per device.

v0:
```python
import functools
import math

import jax
import jax.numpy as jnp
import numpy as np
from jax import lax
from jax.experimental import pallas as pl
from jax.experimental.pallas import tpu as pltpu
from jax.sharding import PartitionSpec as P

WAVENUMBER = 40.0
SOFTENING = 0.01
TURNS = WAVENUMBER / (2.0 * math.pi)
LANES = 128
SUB = 8


def even_fit(function, terms, reach):
    nodes = np.cos((np.arange(400) + 0.5) * np.pi / 400)
    squares = (nodes + 1) * 0.5 * reach * reach
    fit = np.polynomial.chebyshev.Chebyshev.fit(squares, function(np.sqrt(squares)), terms - 1)
    return [float(value) for value in fit.convert(kind=np.polynomial.Polynomial).coef]


ROOT2 = math.sqrt(2.0)
SINE = even_fit(lambda u: ROOT2 * math.pi * np.sinc(u), 5, 0.5)
COSINE = even_fit(lambda u: -ROOT2 * np.cos(np.pi * u), 5, 0.5)
ROUNDER = 1.5 * 2.0**23


def horner(coefficients, x):
    total = coefficients[-1] * x + coefficients[-2]
    for value in coefficients[-3::-1]:
        total = total * x + value
    return total


def lane_repeat(x, period):
    width = period
    lane = lax.broadcasted_iota(jnp.int32, x.shape, 1)
    while width < LANES:
        x = jnp.where(lane < width, x, pltpu.roll(x, width, 1))
        width *= 2
    return x


def field_kernel(
    columns, dest_ref, tile_ref, tests_ref, src_ref, cur_ref, blocks_hbm, out_ref,
    source_rows, near_rows, start, padded, tests_wide, blocks_ref, blocks_sem
):
    devices, _, row_dev = tests_ref.shape
    width = src_ref.shape[1]
    items = blocks_ref.shape[0]
    per_row = LANES // row_dev
    tiles = width // LANES
    gain = TURNS / math.sqrt(width * devices)
    lane = lax.broadcasted_iota(jnp.int32, (SUB, LANES), 1)
    sub = lax.broadcasted_iota(jnp.int32, (SUB, LANES), 0)

    blocks_copy = pltpu.make_async_copy(blocks_hbm, blocks_ref, blocks_sem)
    blocks_copy.start()

    padded[0:3, :] = src_ref[...] * TURNS
    cr = cur_ref[0:1, :]
    ci = cur_ref[1:2, :]
    padded[3:4, :] = jnp.sqrt(cr * cr + ci * ci) * gain
    padded[4:5, :] = jnp.arctan2(ci, cr) * (0.5 / math.pi)
    padded[5:8, :] = jnp.zeros((3, width), jnp.float32)
    pick = lane // row_dev
    for tile in range(tiles):
        x = padded[:, pl.ds(tile * LANES, LANES)]
        for j in range(row_dev):
            source_rows[tile * row_dev + j] = jnp.take_along_axis(x, pick + j * per_row, axis=1)

    blocks_copy.wait()
    start[...] = jnp.zeros_like(start)
    row_base = lax.axis_index("row") * columns
    for group in range(items // per_row):
        owner = jnp.zeros((SUB, LANES), jnp.int32)
        for k in range(per_row):
            block = group * per_row + k
            tile = pl.multiple_of(tile_ref[block] * LANES, LANES)
            cr = cur_ref[0:1, pl.ds(tile, LANES)]
            ci = cur_ref[1:2, pl.ds(tile, LANES)]
            br = blocks_ref[block, 0]
            bi = blocks_ref[block, 1]
            near_rows[0, pl.ds(k * row_dev, row_dev), :] = br * cr - bi * ci
            near_rows[1, pl.ds(k * row_dev, row_dev), :] = br * ci + bi * cr
            owner = jnp.where(lane // row_dev == k, dest_ref[block], owner)
        ones = jnp.ones((SUB, LANES), jnp.float32)
        for part in range(2):
            term = lax.dot_general(
                ones, near_rows[part], (((1,), (1,)), ((), ())),
                precision=lax.Precision.HIGHEST, preferred_element_type=jnp.float32,
            )
            for block in range(columns // SUB):
                place = pl.ds(pl.multiple_of(row_base + block * SUB, SUB), SUB)
                start[part, place, :] += jnp.where(owner == sub + block * SUB, term, 0.0)

    for group in range(devices // SUB):
        for c in range(3):
            points = tests_ref[pl.ds(group * SUB, SUB), c, :] * TURNS
            points = jnp.concatenate([points, jnp.zeros((SUB, LANES - row_dev), jnp.float32)], axis=1)
            tests_wide[c, pl.ds(group * SUB, SUB), :] = lane_repeat(points, row_dev)

    chunk = min(4, devices // SUB)
    soft = (SOFTENING * TURNS) ** 2

    def far(block, _):
        places = [pl.ds(pl.multiple_of((block * chunk + g) * SUB, SUB), SUB) for g in range(chunk)]
        tests = [[tests_wide[c, place, :] for c in range(3)] for place in places]

        def step(r, sums):
            sx, sy, sz, size, turn = [
                jnp.broadcast_to(source_rows[r, c : c + 1, :], (SUB, LANES)) for c in range(5)
            ]
            new = []
            for (tx, ty, tz), (re, im) in zip(tests, sums):
                dx = tx - sx
                dy = ty - sy
                dz = tz - sz
                square = dx * dx + dy * dy + (dz * dz + soft)
                inverse = lax.rsqrt(square)
                t = square * inverse - turn
                u = t - ((t + ROUNDER) - ROUNDER)
                u2 = u * u
                s = u * horner(SINE, u2)
                c = horner(COSINE, u2)
                a = inverse * size
                new.append((re + a * (1.0 - s * s), im + a * (s * c)))
            return tuple(new)

        sums = tuple((start[0, place, :], start[1, place, :]) for place in places)
        sums = lax.fori_loop(0, width // per_row, step, sums, unroll=2)
        for place, (re, im) in zip(places, sums):
            shift = LANES // 2
            while shift >= row_dev:
                re = re + pltpu.roll(re, shift, 1)
                im = im + pltpu.roll(im, shift, 1)
                shift //= 2
            out_ref[place, 0, :] = re[:, :row_dev]
            out_ref[place, 1, :] = im[:, :row_dev]
        return 0

    lax.fori_loop(0, devices // (SUB * chunk), far, 0)


def local(test_points, src_points, currents, near_blocks, near_dest, near_tile):
    row_dev = test_points.shape[1]
    width = src_points.shape[1]
    columns = lax.axis_size("col")
    devices = lax.axis_size("row") * columns
    copies = jnp.broadcast_to(test_points[None], (devices, 3, row_dev))
    tests = lax.all_to_all(copies, ("row", "col"), split_axis=0, concat_axis=0, tiled=True)
    vmem = pl.BlockSpec(memory_space=pltpu.VMEM)
    smem = pl.BlockSpec(memory_space=pltpu.SMEM)
    partial = pl.pallas_call(
        functools.partial(field_kernel, columns),
        out_shape=jax.ShapeDtypeStruct((devices, 2, row_dev), jnp.float32),
        in_specs=[smem, smem, vmem, vmem, vmem, pl.BlockSpec(memory_space=pl.ANY)],
        out_specs=vmem,
        scratch_shapes=[
            pltpu.VMEM((width * row_dev // LANES, SUB, LANES), jnp.float32),
            pltpu.VMEM((2, LANES, LANES), jnp.float32),
            pltpu.VMEM((2, devices, LANES), jnp.float32),
            pltpu.VMEM((SUB, width), jnp.float32),
            pltpu.VMEM((3, devices, LANES), jnp.float32),
            pltpu.VMEM(near_blocks.shape, jnp.float32),
            pltpu.SemaphoreType.DMA,
        ],
        compiler_params=pltpu.CompilerParams(vmem_limit_bytes=24 << 20),
    )(near_dest.reshape(-1), near_tile.reshape(-1), tests, src_points, currents, near_blocks)
    parts = lax.all_to_all(partial, ("row", "col"), split_axis=0, concat_axis=0, tiled=True)
    return parts.sum(axis=0)


def solution(mesh):
    in_specs = (
        P(None, ("row", "col")),
        P(None, ("row", "col")),
        P(None, ("row", "col")),
        P(("row", "col"), None, None, None),
        P(("row", "col"), None),
        P(("row", "col"), None),
    )
    out_specs = P(None, ("row", "col"))
    return jax.shard_map(local, mesh=mesh, in_specs=in_specs, out_specs=out_specs, check_vma=False)
```

profile of v0, /device:TPU:0, one launch (start us, length us, event | category | flops | bytes accessed | tf_op | source)
XLA Modules:
  0.0 30.5 jit_solution(17585341954917554843)
XLA Ops:
  0.0 0.0 copy-start
  0.0 0.7 %broadcast_in_dim.2 = f32[32,3,16]{2,1,0:T(4,128)S(1)} broadcast(f32[3,16]{1,0:T(4,128)} %param.6), dimensions={1,2} | broadcast | bytes 6336 | tf_op jit(solution)/shard_map/broadcast_in_dim | solution.py:154
  0.7 0.0 copy-start.1
  0.7 0.0 copy-start.2
  0.8 14.4 %all_to_all.10.tests_ref = f32[32,3,16]{2,1,0:T(4,128)S(1)} all-to-all(f32[32,3,16]{2,1,0:T(4,128)S(1)} %broadcast_in_dim.2), channel_id=1, replica_groups=mesh['row'=4,'col'=8] {'row','col'}, dimensions={0} | all-to-all | bytes 12288 | tf_op jit(solution)/shard_map/all_to_all | solution.py:155
  15.1 0.0 copy-start.3
  15.1 0.0 copy-start.4
  15.1 0.0 copy-done
  15.1 0.0 copy-done.1
  15.2 0.0 copy-done.2
  15.2 0.6 %copy-done.3 = s32[8,1]{0,1:T(1,128)S(1)} copy-done((s32[8,1]{0,1:T(1,128)S(1)}, s32[8,1]{0,1:T(1,128)}, u32[]{:S(2)}) %copy-start.3) | copy-done | bytes 56
  15.8 0.0 copy-done.4
  15.8 5.2 %shard_map.64 = f32[32,2,16]{2,1,0:T(2,128)S(1)} custom-call(s32[8]{0:T(128)S(1)} %bitcast.2, s32[8]{0:T(128)S(1)} %bitcast.3, f32[32,3,16]{2,1,0:T(4,128)S(1)} %all_to_all.10.tests_ref, f32[3,1024]{1,0:T(4,128)S(1)} %copy-done.1, f32[2,1024]{1,0:T(2,128)S(1)} %copy-done.2, f32[8,2,16,128]{3,2,1,0:T(8,128)S(1)} %copy-done), custom_call_target="tpu_custom_call" | custom-call | tf_op jit(solution)/shard_map/pallas_call | solution.py:158
  21.0 8.9 %all_to_all.11 = f32[32,2,16]{2,1,0:T(2,128)S(1)} all-to-all(f32[32,2,16]{2,1,0:T(2,128)S(1)} %shard_map.64), channel_id=1, replica_groups=mesh['row'=4,'col'=8] {'row','col'}, dimensions={0} | all-to-all | bytes 8192 | tf_op jit(solution)/shard_map/all_to_all | solution.py:174
  29.9 0.6 %reduce_sum.9 = f32[2,16]{1,0:T(2,128)} reduce(f32[32,2,16]{2,1,0:T(2,128)S(1)} %all_to_all.11, f32[]{:T(128)} %constant.0.clone.1), dimensions={0}, to_apply=%region_0.0 | reduce | flops 992 | bytes 4228 | tf_op jit(solution)/shard_map/reduce_sum | solution.py:175
Async XLA Ops:
  0.0 15.1 %copy-start = (f32[8,2,16,128]{3,2,1,0:T(8,128)S(1)}, f32[8,2,16,128]{3,2,1,0:T(8,128)}, u32[]{:S(2)}) copy-start(f32[8,2,16,128]{3,2,1,0:T(8,128)} %blocks_hbm.1) | copy-start | bytes 393220
  0.7 14.4 %copy-start.1 = (f32[3,1024]{1,0:T(4,128)S(1)}, f32[3,1024]{1,0:T(4,128)}, u32[]{:S(2)}) copy-start(f32[3,1024]{1,0:T(4,128)} %src_ref.1) | copy-start | bytes 36868
  0.7 14.4 %copy-start.2 = (f32[2,1024]{1,0:T(2,128)S(1)}, f32[2,1024]{1,0:T(2,128)}, u32[]{:S(2)}) copy-start(f32[2,1024]{1,0:T(2,128)} %cur_ref.1) | copy-start | bytes 24580
  15.1 0.7 %copy-start.3 = (s32[8,1]{0,1:T(1,128)S(1)}, s32[8,1]{0,1:T(1,128)}, u32[]{:S(2)}) copy-start(s32[8,1]{0,1:T(1,128)} %param.10) | copy-start | bytes 100
  15.1 0.7 %copy-start.4 = (s32[8,1]{0,1:T(1,128)S(1)}, s32[8,1]{0,1:T(1,128)}, u32[]{:S(2)}) copy-start(s32[8,1]{0,1:T(1,128)} %param.11) | copy-start | bytes 100
where the time goes:
time: 30.7 us; the launch traced here: 30.5 us
  blocking collectives  23.3 us (76%)
  Pallas kernels  5.17 us (17%)
  local copies, waits for them, and re-layouts  1.39 us (5%)
  other arithmetic  0.6 us (2%)
    all_to_all x1, blocking collectives, local(): lax.all_to_all(copies, ('row', 'col'), split_axis=0, concat_axis=0, tiled...  14.4 us
    all_to_all x1, blocking collectives, local(): lax.all_to_all(partial, ('row', 'col'), split_axis=0, concat_axis=0, tile...  8.88 us
    pallas_call x1, Pallas kernels, local(): pl.pallas_call(functools.partial(field_kernel, columns), out_shape=jax.Sh...  5.17 us
    broadcast_in_dim x1, local copies, waits for them, and re-layouts, local(): copies = jnp.broadcast_to(test_points[None], (devices, 3, row_dev))  0.73 us
    unnamed x10, local copies, waits for them, and re-layouts  0.67 us

commit v1 on v0

--- a/solution.py
+++ b/solution.py
@@ -45,19 +45,17 @@
     return x
 
 
-def field_kernel(
-    columns, dest_ref, tile_ref, tests_ref, src_ref, cur_ref, blocks_hbm, out_ref,
-    source_rows, near_rows, start, padded, tests_wide, blocks_ref, blocks_sem
+def prepare_kernel(
+    axes, dest_ref, tile_ref, src_ref, cur_ref, blocks_hbm, source_rows, start, near_rows, padded, blocks_ref, blocks_sem
 ):
-    devices, _, row_dev = tests_ref.shape
+    rows, columns = axes
     width = src_ref.shape[1]
-    items = blocks_ref.shape[0]
+    items, _, row_dev, _ = blocks_ref.shape
     per_row = LANES // row_dev
     tiles = width // LANES
-    gain = TURNS / math.sqrt(width * devices)
+    gain = TURNS / math.sqrt(width * rows * columns)
     lane = lax.broadcasted_iota(jnp.int32, (SUB, LANES), 1)
     sub = lax.broadcasted_iota(jnp.int32, (SUB, LANES), 0)
-
     blocks_copy = pltpu.make_async_copy(blocks_hbm, blocks_ref, blocks_sem)
     blocks_copy.start()
 
@@ -75,7 +73,7 @@
 
     blocks_copy.wait()
     start[...] = jnp.zeros_like(start)
-    row_base = lax.axis_index("row") * columns
+    mine = lax.axis_index("col")
     for group in range(items // per_row):
         owner = jnp.zeros((SUB, LANES), jnp.int32)
         for k in range(per_row):
@@ -87,20 +85,32 @@
             bi = blocks_ref[block, 1]
             near_rows[0, pl.ds(k * row_dev, row_dev), :] = br * cr - bi * ci
             near_rows[1, pl.ds(k * row_dev, row_dev), :] = br * ci + bi * cr
-            owner = jnp.where(lane // row_dev == k, dest_ref[block], owner)
+            away = lax.rem(mine - dest_ref[block] + columns, columns) * rows
+            owner = jnp.where(lane // row_dev == k, away, owner)
         ones = jnp.ones((SUB, LANES), jnp.float32)
         for part in range(2):
             term = lax.dot_general(
                 ones, near_rows[part], (((1,), (1,)), ((), ())),
                 precision=lax.Precision.HIGHEST, preferred_element_type=jnp.float32,
             )
-            for block in range(columns // SUB):
-                place = pl.ds(pl.multiple_of(row_base + block * SUB, SUB), SUB)
+            for block in range(rows * columns // SUB):
+                place = pl.ds(block * SUB, SUB)
                 start[part, place, :] += jnp.where(owner == sub + block * SUB, term, 0.0)
 
+
+def far_kernel(axes, *refs):
+    rows, columns = axes
+    devices = rows * columns
+    tests_refs, (source_rows, start, out_ref, tests_wide) = refs[:columns], refs[columns:]
+    row_dev = out_ref.shape[2]
+    lane = lax.broadcasted_iota(jnp.int32, (SUB, LANES), 1)
+
+    per_group = SUB // rows
     for group in range(devices // SUB):
         for c in range(3):
-            points = tests_ref[pl.ds(group * SUB, SUB), c, :] * TURNS
+            points = jnp.concatenate(
+                [tests_refs[group * per_group + k][:, c, :] for k in range(per_group)], axis=0
+            ) * TURNS
             points = jnp.concatenate([points, jnp.zeros((SUB, LANES - row_dev), jnp.float32)], axis=1)
             tests_wide[c, pl.ds(group * SUB, SUB), :] = lane_repeat(points, row_dev)
 
@@ -132,7 +142,7 @@
             return tuple(new)
 
         sums = tuple((start[0, place, :], start[1, place, :]) for place in places)
-        sums = lax.fori_loop(0, width // per_row, step, sums, unroll=2)
+        sums = lax.fori_loop(0, source_rows.shape[0], step, sums, unroll=2)
         for place, (re, im) in zip(places, sums):
             shift = LANES // 2
             while shift >= row_dev:
@@ -146,33 +156,56 @@
     lax.fori_loop(0, devices // (SUB * chunk), far, 0)
 
 
-def local(test_points, src_points, currents, near_blocks, near_dest, near_tile):
+def forward(x, axis, size, steps):
+    return lax.ppermute(x, axis, [(i, (i + steps) % size) for i in range(size)])
+
+
+def local(rows, columns, test_points, src_points, currents, near_blocks, near_dest, near_tile):
     row_dev = test_points.shape[1]
     width = src_points.shape[1]
-    columns = lax.axis_size("col")
-    devices = lax.axis_size("row") * columns
-    copies = jnp.broadcast_to(test_points[None], (devices, 3, row_dev))
-    tests = lax.all_to_all(copies, ("row", "col"), split_axis=0, concat_axis=0, tiled=True)
+    devices = rows * columns
     vmem = pl.BlockSpec(memory_space=pltpu.VMEM)
     smem = pl.BlockSpec(memory_space=pltpu.SMEM)
-    partial = pl.pallas_call(
-        functools.partial(field_kernel, columns),
-        out_shape=jax.ShapeDtypeStruct((devices, 2, row_dev), jnp.float32),
-        in_specs=[smem, smem, vmem, vmem, vmem, pl.BlockSpec(memory_space=pl.ANY)],
-        out_specs=vmem,
+
+    nearby = [test_points] + [forward(test_points, "row", rows, k) for k in range(1, rows)]
+    nearby = jnp.stack(nearby)
+    tests = [nearby] + [forward(nearby, "col", columns, k) for k in range(1, columns)]
+
+    source_rows, start = pl.pallas_call(
+        functools.partial(prepare_kernel, (rows, columns)),
+        out_shape=(
+            jax.ShapeDtypeStruct((width * row_dev // LANES, SUB, LANES), jnp.float32),
+            jax.ShapeDtypeStruct((2, devices, LANES), jnp.float32),
+        ),
+        in_specs=[smem, smem, vmem, vmem, pl.BlockSpec(memory_space=pl.ANY)],
+        out_specs=(vmem, vmem),
         scratch_shapes=[
-            pltpu.VMEM((width * row_dev // LANES, SUB, LANES), jnp.float32),
             pltpu.VMEM((2, LANES, LANES), jnp.float32),
-            pltpu.VMEM((2, devices, LANES), jnp.float32),
             pltpu.VMEM((SUB, width), jnp.float32),
-            pltpu.VMEM((3, devices, LANES), jnp.float32),
             pltpu.VMEM(near_blocks.shape, jnp.float32),
             pltpu.SemaphoreType.DMA,
         ],
         compiler_params=pltpu.CompilerParams(vmem_limit_bytes=24 << 20),
-    )(near_dest.reshape(-1), near_tile.reshape(-1), tests, src_points, currents, near_blocks)
-    parts = lax.all_to_all(partial, ("row", "col"), split_axis=0, concat_axis=0, tiled=True)
-    return parts.sum(axis=0)
+        cost_estimate=pl.CostEstimate(flops=4 << 20, bytes_accessed=1 << 20, transcendentals=0),
+    )(near_dest.reshape(-1), near_tile.reshape(-1), src_points, currents, near_blocks)
+
+    partial = pl.pallas_call(
+        functools.partial(far_kernel, (rows, columns)),
+        out_shape=jax.ShapeDtypeStruct((devices, 2, row_dev), jnp.float32),
+        in_specs=[vmem] * (columns + 2),
+        out_specs=vmem,
+        scratch_shapes=[pltpu.VMEM((3, devices, LANES), jnp.float32)],
+        compiler_params=pltpu.CompilerParams(vmem_limit_bytes=24 << 20),
+    )(*tests, source_rows, start)
+
+    partial = partial.reshape(columns, rows, 2, row_dev)
+    line = partial[0]
+    for k in range(1, columns):
+        line = line + forward(partial[k], "col", columns, columns - k)
+    total = line[0]
+    for k in range(1, rows):
+        total = total + forward(line[k], "row", rows, rows - k)
+    return total
 
 
 def solution(mesh):
@@ -185,4 +218,5 @@
         P(("row", "col"), None),
     )
     out_specs = P(None, ("row", "col"))
-    return jax.shard_map(local, mesh=mesh, in_specs=in_specs, out_specs=out_specs, check_vma=False)
+    body = functools.partial(local, mesh.shape["row"], mesh.shape["col"])
+    return jax.shard_map(body, mesh=mesh, in_specs=in_specs, out_specs=out_specs, check_vma=False)

time: 30.7 us -> 44.9 us (1.46)
  starting transfers between devices: 0 us -> 28.5 us
  blocking collectives: 23.3 us -> 0 us
  waiting for transfers between devices: 0 us -> 7.56 us
  other arithmetic: 0.6 us -> 1.28 us
    ppermute x0 -> x20, starting transfers between devices: none -> 28.5 us  [forward(): return lax.ppermute(x, axis, [(i, (i + steps) % size) for i in range(size)])]
    all_to_all x2 -> x0, blocking collectives: 23.3 us -> none  [the longest x1 14.4 us: local(): lax.all_to_all(copies, ('row', 'col'), split_axis=0, concat_axis=0, tiled...]
    ppermute x0 -> x20, waiting for transfers between devices: none -> 7.56 us  [forward(): return lax.ppermute(x, axis, [(i, (i + steps) % size) for i in range(size)])]
    unnamed x10, local copies, waits for them, and re-layouts: 0.67 us -> 1.57 us
    broadcast_in_dim x1 -> x0, local copies, waits for them, and re-layouts: 0.73 us -> none  [local(): copies = jnp.broadcast_to(test_points[None], (devices, 3, row_dev))]
    another operation x0 -> x1, other arithmetic: none -> 0.7 us  [local(): nearby = jnp.stack(nearby)]
    reduce_sum x1 -> x0, other arithmetic: 0.6 us -> none  [local(): return parts.sum(axis=0)]
    add x0 -> x2, other arithmetic: none -> 0.58 us  [the longest x1 0.57 us: local(): total = total + forward(line[k], 'row', rows, rows - k)]
  transfers between devices with their start and end apart: 0 -> 20, of which waited for: 0 -> 8; matrix products, arithmetic and copies ran while one was open for 0% -> 0% of each run, Pallas kernels for 0% -> 3%
where the time goes in v1:
time: 44.9 us; the launch traced here: 44.4 us
  starting transfers between devices  28.5 us (63%)
  waiting for transfers between devices  7.56 us (17%)
  Pallas kernels  5.36 us (12%)
  local copies, waits for them, and re-layouts  1.58 us (4%)
  other arithmetic  1.28 us (3%)
    ppermute x20, starting transfers between devices, forward(): return lax.ppermute(x, axis, [(i, (i + steps) % size) for i in range(size)])  28.5 us
    ppermute x20, waiting for transfers between devices, forward(): return lax.ppermute(x, axis, [(i, (i + steps) % size) for i in range(size)])  7.56 us
    pallas_call x1, Pallas kernels, local(): pl.pallas_call(functools.partial(far_kernel, (rows, columns)), out_shape=...  3.85 us
    unnamed x10, local copies, waits for them, and re-layouts  1.57 us
    pallas_call x1, Pallas kernels, local(): pl.pallas_call(functools.partial(prepare_kernel, (rows, columns)), out_sh...  1.51 us
  transfers between devices with their start and end apart: 20, of which 8 were waited for; matrix products, arithmetic and copies ran while one was open for 0% of the time, Pallas kernels for 3%

profile of v1, /device:TPU:0, one launch (start us, length us, event | category | flops | bytes accessed | tf_op | source)
XLA Modules:
  0.0 44.4 jit_solution(14276400386113354863)
XLA Ops:
  0.5 2.0 %collective-permute-start.2 = (f32[3,16]{1,0:T(4,128)}, f32[3,16]{1,0:T(4,128)S(1)}, u32[]{:S(2)}, u32[]{:S(2)}) collective-permute-start(f32[3,16]{1,0:T(4,128)} %param.6), channel_id=1, source_target_pairs={{0,24},{8,0},{16,8},{24,16},{1,25},{9,1},{17,9},{25,17},{2,26},{10... | collective-permute-start | bytes 584 | tf_op jit(solution)/shard_map/ppermute | solution.py:160
  2.4 2.3 %collective-permute-start.1 = (f32[3,16]{1,0:T(4,128)}, f32[3,16]{1,0:T(4,128)S(1)}, u32[]{:S(2)}, u32[]{:S(2)}) collective-permute-start(f32[3,16]{1,0:T(4,128)} %param.6), channel_id=1, source_target_pairs={{0,16},{8,24},{16,0},{24,8},{1,17},{9,25},{17,1},{25,9},{2,18},{10... | collective-permute-start | bytes 584 | tf_op jit(solution)/shard_map/ppermute | solution.py:160
  4.7 1.8 %collective-permute-done.1 = f32[3,16]{1,0:T(4,128)S(1)} collective-permute-done((f32[3,16]{1,0:T(4,128)}, f32[3,16]{1,0:T(4,128)S(1)}, u32[]{:S(2)}, u32[]{:S(2)}) %collective-permute-start.1) | collective-permute-done | bytes 224 | tf_op jit(solution)/shard_map/ppermute | solution.py:160
  6.5 0.7 %pad_maximum_fusion.refs_0_ = f32[4,3,16]{2,1,0:T(4,128)S(1)} fusion(f32[1,3,16]{2,1,0:T(4,128)S(1)} %bitcast.24, f32[1,3,16]{2,1,0:T(4,128)S(1)} %bitcast.25, f32[1,3,16]{2,1,0:T(4,128)S(1)} %bitcast.23, f32[1,3,16]{2,1,0:T(4,128)} %bitcast.22), kind=kLoop, calls=%fused_computation | loop fusion | flops 576 | bytes 1536 | tf_op jit(solution)/shard_map/stack | solution.py:171
  7.2 5.1 %collective-permute-start.9 = (f32[4,3,16]{2,1,0:T(4,128)S(1)}, f32[4,3,16]{2,1,0:T(4,128)S(1)}, u32[]{:S(2)}, u32[]{:S(2)}) collective-permute-start(f32[4,3,16]{2,1,0:T(4,128)S(1)} %pad_maximum_fusion.refs_0_), channel_id=1, source_target_pairs={{0,7},{1,0},{2,1},{3,2},{4,3},{5,4},{6,5},{7,6},{8,15},{9,8},{10,9... | collective-permute-start | bytes 2312 | tf_op jit(solution)/shard_map/ppermute | solution.py:160
  12.7 3.0 %collective-permute-start.6 = (f32[4,3,16]{2,1,0:T(4,128)S(1)}, f32[4,3,16]{2,1,0:T(4,128)S(1)}, u32[]{:S(2)}, u32[]{:S(2)}) collective-permute-start(f32[4,3,16]{2,1,0:T(4,128)S(1)} %pad_maximum_fusion.refs_0_), channel_id=1, source_target_pairs={{0,4},{1,5},{2,6},{3,7},{4,0},{5,1},{6,2},{7,3},{8,12},{9,13},{10,... | collective-permute-start | bytes 2312 | tf_op jit(solution)/shard_map/ppermute | solution.py:160
  15.7 1.9 %collective-permute-start.4 = (f32[4,3,16]{2,1,0:T(4,128)S(1)}, f32[4,3,16]{2,1,0:T(4,128)S(1)}, u32[]{:S(2)}, u32[]{:S(2)}) collective-permute-start(f32[4,3,16]{2,1,0:T(4,128)S(1)} %pad_maximum_fusion.refs_0_), channel_id=1, source_target_pairs={{0,2},{1,3},{2,4},{3,5},{4,6},{5,7},{6,0},{7,1},{8,10},{9,11},{10,... | collective-permute-start | bytes 2312 | tf_op jit(solution)/shard_map/ppermute | solution.py:160
  17.5 1.1 %collective-permute-start.3 = (f32[4,3,16]{2,1,0:T(4,128)S(1)}, f32[4,3,16]{2,1,0:T(4,128)S(1)}, u32[]{:S(2)}, u32[]{:S(2)}) collective-permute-start(f32[4,3,16]{2,1,0:T(4,128)S(1)} %pad_maximum_fusion.refs_0_), channel_id=1, source_target_pairs={{0,1},{1,2},{2,3},{3,4},{4,5},{5,6},{6,7},{7,0},{8,9},{9,10},{10,1... | collective-permute-start | bytes 2312 | tf_op jit(solution)/shard_map/ppermute | solution.py:160
  18.7 0.6 %copy-done.3 = s32[8,1]{0,1:T(1,128)S(1)} copy-done((s32[8,1]{0,1:T(1,128)S(1)}, s32[8,1]{0,1:T(1,128)}, u32[]{:S(2)}) %copy-start.3) | copy-done | bytes 56
  19.4 0.9 %copy-done = f32[8,2,16,128]{3,2,1,0:T(8,128)S(1)} copy-done((f32[8,2,16,128]{3,2,1,0:T(8,128)S(1)}, f32[8,2,16,128]{3,2,1,0:T(8,128)}, u32[]{:S(2)}) %copy-start) | copy-done | bytes 131096
  20.3 1.5 %shard_map.64 = (f32[128,8,128]{2,1,0:T(8,128)S(1)}, f32[2,32,128]{2,1,0:T(8,128)S(1)}) custom-call(s32[8]{0:T(128)S(1)} %bitcast.20, s32[8]{0:T(128)S(1)} %bitcast.21, f32[3,1024]{1,0:T(4,128)S(1)} %copy-done.1, f32[2,1024]{1,0:T(2,128)S(1)} %copy-done.2, f32[8,2,16,128]{3,2,1,0:T(8,128)S(1)} %copy-done), custom_call_target="tpu_custom_call" | custom-call | flops 4194304 | bytes 1048576 | tf_op jit(solution)/shard_map/pallas_call | solution.py:174
  22.2 1.7 %collective-permute-done.3.refs_1_ = f32[4,3,16]{2,1,0:T(4,128)S(1)} collective-permute-done((f32[4,3,16]{2,1,0:T(4,128)S(1)}, f32[4,3,16]{2,1,0:T(4,128)S(1)}, u32[]{:S(2)}, u32[]{:S(2)}) %collective-permute-start.3) | collective-permute-done | bytes 800 | tf_op jit(solution)/shard_map/ppermute | solution.py:160
  23.9 3.9 %shard_map.65 = f32[32,2,16]{2,1,0:T(2,128)S(1)} custom-call(f32[4,3,16]{2,1,0:T(4,128)S(1)} %pad_maximum_fusion.refs_0_, f32[4,3,16]{2,1,0:T(4,128)S(1)} %collective-permute-done.3.refs_1_, f32[4,3,16]{2,1,0:T(4,128)S(1)} %collective-permute-done.4.refs_2_, f32[4,3,16]{2,1,0:T(4,128)S(1)} %collective-permute-done.5.refs_3_, ...), custom_call_target="tpu_custom_call" | custom-call | tf_op jit(solution)/shard_map/pallas_call | solution.py:192
  27.8 1.6 %collective-permute-start.10 = (f32[4,2,16]{2,1,0:T(2,128)S(1)}, f32[4,2,16]{2,1,0:T(2,128)S(1)}, u32[]{:S(2)}, u32[]{:S(2)}) collective-permute-start(f32[4,2,16]{2,1,0:T(2,128)S(1)} %get-tuple-element.9), channel_id=1, source_target_pairs={{0,7},{1,0},{2,1},{3,2},{4,3},{5,4},{6,5},{7,6},{8,15},{9,8},{10,9... | collective-permute-start | bytes 1544 | tf_op jit(solution)/shard_map/ppermute | solution.py:160
  30.2 2.4 %collective-permute-start.14 = (f32[4,2,16]{2,1,0:T(2,128)S(1)}, f32[4,2,16]{2,1,0:T(2,128)S(1)}, u32[]{:S(2)}, u32[]{:S(2)}) collective-permute-start(f32[4,2,16]{2,1,0:T(2,128)S(1)} %get-tuple-element.12), channel_id=1, source_target_pairs={{0,3},{1,4},{2,5},{3,6},{4,7},{5,0},{6,1},{7,2},{8,11},{9,12},{10,... | collective-permute-start | bytes 1544 | tf_op jit(solution)/shard_map/ppermute | solution.py:160
  32.6 2.1 %collective-permute-start.13 = (f32[4,2,16]{2,1,0:T(2,128)S(1)}, f32[4,2,16]{2,1,0:T(2,128)S(1)}, u32[]{:S(2)}, u32[]{:S(2)}) collective-permute-start(f32[4,2,16]{2,1,0:T(2,128)S(1)} %get-tuple-element.13), channel_id=1, source_target_pairs={{0,4},{1,5},{2,6},{3,7},{4,0},{5,1},{6,2},{7,3},{8,12},{9,13},{10,... | collective-permute-start | bytes 1544 | tf_op jit(solution)/shard_map/ppermute | solution.py:160
  34.6 0.8 %collective-permute-start.12 = (f32[4,2,16]{2,1,0:T(2,128)S(1)}, f32[4,2,16]{2,1,0:T(2,128)S(1)}, u32[]{:S(2)}, u32[]{:S(2)}) collective-permute-start(f32[4,2,16]{2,1,0:T(2,128)S(1)} %get-tuple-element.14), channel_id=1, source_target_pairs={{0,5},{1,6},{2,7},{3,0},{4,1},{5,2},{6,3},{7,4},{8,13},{9,14},{10,... | collective-permute-start | bytes 1544 | tf_op jit(solution)/shard_map/ppermute | solution.py:160
  35.7 2.6 %collective-permute-start.11 = (f32[4,2,16]{2,1,0:T(2,128)S(1)}, f32[4,2,16]{2,1,0:T(2,128)S(1)}, u32[]{:S(2)}, u32[]{:S(2)}) collective-permute-start(f32[4,2,16]{2,1,0:T(2,128)S(1)} %get-tuple-element.15), channel_id=1, source_target_pairs={{0,6},{1,7},{2,0},{3,1},{4,2},{5,3},{6,4},{7,5},{8,14},{9,15},{10,... | collective-permute-start | bytes 1544 | tf_op jit(solution)/shard_map/ppermute | solution.py:160
  38.3 0.8 %collective-permute-done.12 = f32[4,2,16]{2,1,0:T(2,128)S(1)} collective-permute-done((f32[4,2,16]{2,1,0:T(2,128)S(1)}, f32[4,2,16]{2,1,0:T(2,128)S(1)}, u32[]{:S(2)}, u32[]{:S(2)}) %collective-permute-start.12) | collective-permute-done | bytes 544 | tf_op jit(solution)/shard_map/ppermute | solution.py:160
  39.1 0.5 %collective-permute-done.11 = f32[4,2,16]{2,1,0:T(2,128)S(1)} collective-permute-done((f32[4,2,16]{2,1,0:T(2,128)S(1)}, f32[4,2,16]{2,1,0:T(2,128)S(1)}, u32[]{:S(2)}, u32[]{:S(2)}) %collective-permute-start.11) | collective-permute-done | bytes 544 | tf_op jit(solution)/shard_map/ppermute | solution.py:160
  40.2 1.5 %collective-permute-start.18 = (f32[2,16]{1,0:T(2,128)S(1)}, f32[2,16]{1,0:T(2,128)S(1)}, u32[]{:S(2)}, u32[]{:S(2)}) collective-permute-start(f32[2,16]{1,0:T(2,128)S(1)} %get-tuple-element.18), channel_id=1, source_target_pairs={{0,16},{8,24},{16,0},{24,8},{1,17},{9,25},{17,1},{25,9},{2,18},{10... | collective-permute-start | bytes 392 | tf_op jit(solution)/shard_map/ppermute | solution.py:160
  41.7 1.1 %collective-permute-done.19 = f32[2,16]{1,0:T(2,128)S(1)} collective-permute-done((f32[2,16]{1,0:T(2,128)S(1)}, f32[2,16]{1,0:T(2,128)S(1)}, u32[]{:S(2)}, u32[]{:S(2)}) %collective-permute-start.19) | collective-permute-done | bytes 160 | tf_op jit(solution)/shard_map/ppermute | solution.py:160
  42.8 1.0 %collective-permute-done.18 = f32[2,16]{1,0:T(2,128)S(1)} collective-permute-done((f32[2,16]{1,0:T(2,128)S(1)}, f32[2,16]{1,0:T(2,128)S(1)}, u32[]{:S(2)}, u32[]{:S(2)}) %collective-permute-start.18) | collective-permute-done | bytes 160 | tf_op jit(solution)/shard_map/ppermute | solution.py:160
  43.8 0.6 %fusion.8 = f32[2,16]{1,0:T(2,128)} fusion(f32[2,16]{1,0:T(2,128)S(1)} %collective-permute-done.19, f32[2,16]{1,0:T(2,128)S(1)} %collective-permute-done.18, f32[2,16]{1,0:T(2,128)S(1)} %collective-permute-done.17, f32[4,2,16]{2,1,0:T(2,128)S(1)} %fusion.5), kind=kLoop, calls=%fused_computation.14 | loop fusion | flops 96 | bytes 640 | tf_op jit(solution)/shard_map/add | solution.py:207
  (33 shorter events, 3.0 us)
Async XLA Ops:
  0.0 18.7 %copy-start.1 = (f32[3,1024]{1,0:T(4,128)S(1)}, f32[3,1024]{1,0:T(4,128)}, u32[]{:S(2)}) copy-start(f32[3,1024]{1,0:T(4,128)} %src_ref.1) | copy-start | bytes 36868
  0.0 4.7 %collective-permute-start = (f32[3,16]{1,0:T(4,128)}, f32[3,16]{1,0:T(4,128)S(1)}, u32[]{:S(2)}, u32[]{:S(2)}) collective-permute-start(f32[3,16]{1,0:T(4,128)} %param.6), channel_id=1, source_target_pairs={{0,8},{8,16},{16,24},{24,0},{1,9},{9,17},{17,25},{25,1},{2,10},{10... | collective-permute-start | bytes 584 | tf_op jit(solution)/shard_map/ppermute | solution.py:160
  0.5 4.2 %collective-permute-start.2 = (f32[3,16]{1,0:T(4,128)}, f32[3,16]{1,0:T(4,128)S(1)}, u32[]{:S(2)}, u32[]{:S(2)}) collective-permute-start(f32[3,16]{1,0:T(4,128)} %param.6), channel_id=1, source_target_pairs={{0,24},{8,0},{16,8},{24,16},{1,25},{9,1},{17,9},{25,17},{2,26},{10... | collective-permute-start | bytes 584 | tf_op jit(solution)/shard_map/ppermute | solution.py:160
  2.4 4.1 %collective-permute-start.1 = (f32[3,16]{1,0:T(4,128)}, f32[3,16]{1,0:T(4,128)S(1)}, u32[]{:S(2)}, u32[]{:S(2)}) collective-permute-start(f32[3,16]{1,0:T(4,128)} %param.6), channel_id=1, source_target_pairs={{0,16},{8,24},{16,0},{24,8},{1,17},{9,25},{17,1},{25,9},{2,18},{10... | collective-permute-start | bytes 584 | tf_op jit(solution)/shard_map/ppermute | solution.py:160
  6.5 12.2 %copy-start.2 = (f32[2,1024]{1,0:T(2,128)S(1)}, f32[2,1024]{1,0:T(2,128)}, u32[]{:S(2)}) copy-start(f32[2,1024]{1,0:T(2,128)} %cur_ref.1) | copy-start | bytes 24580
  7.2 8.5 %collective-permute-start.9 = (f32[4,3,16]{2,1,0:T(4,128)S(1)}, f32[4,3,16]{2,1,0:T(4,128)S(1)}, u32[]{:S(2)}, u32[]{:S(2)}) collective-permute-start(f32[4,3,16]{2,1,0:T(4,128)S(1)} %pad_maximum_fusion.refs_0_), channel_id=1, source_target_pairs={{0,7},{1,0},{2,1},{3,2},{4,3},{5,4},{6,5},{7,6},{8,15},{9,8},{10,9... | collective-permute-start | bytes 2312 | tf_op jit(solution)/shard_map/ppermute | solution.py:160
  12.3 5.3 %collective-permute-start.8 = (f32[4,3,16]{2,1,0:T(4,128)S(1)}, f32[4,3,16]{2,1,0:T(4,128)S(1)}, u32[]{:S(2)}, u32[]{:S(2)}) collective-permute-start(f32[4,3,16]{2,1,0:T(4,128)S(1)} %pad_maximum_fusion.refs_0_), channel_id=1, source_target_pairs={{0,6},{1,7},{2,0},{3,1},{4,2},{5,3},{6,4},{7,5},{8,14},{9,15},{10,... | collective-permute-start | bytes 2312 | tf_op jit(solution)/shard_map/ppermute | solution.py:160
  12.7 9.1 %collective-permute-start.7 = (f32[4,3,16]{2,1,0:T(4,128)S(1)}, f32[4,3,16]{2,1,0:T(4,128)S(1)}, u32[]{:S(2)}, u32[]{:S(2)}) collective-permute-start(f32[4,3,16]{2,1,0:T(4,128)S(1)} %pad_maximum_fusion.refs_0_), channel_id=1, source_target_pairs={{0,5},{1,6},{2,7},{3,0},{4,1},{5,2},{6,3},{7,4},{8,13},{9,14},{10,... | collective-permute-start | bytes 2312 | tf_op jit(solution)/shard_map/ppermute | solution.py:160
  12.7 9.1 %collective-permute-start.6 = (f32[4,3,16]{2,1,0:T(4,128)S(1)}, f32[4,3,16]{2,1,0:T(4,128)S(1)}, u32[]{:S(2)}, u32[]{:S(2)}) collective-permute-start(f32[4,3,16]{2,1,0:T(4,128)S(1)} %pad_maximum_fusion.refs_0_), channel_id=1, source_target_pairs={{0,4},{1,5},{2,6},{3,7},{4,0},{5,1},{6,2},{7,3},{8,12},{9,13},{10,... | collective-permute-start | bytes 2312 | tf_op jit(solution)/shard_map/ppermute | solution.py:160
  15.7 6.1 %collective-permute-start.5 = (f32[4,3,16]{2,1,0:T(4,128)S(1)}, f32[4,3,16]{2,1,0:T(4,128)S(1)}, u32[]{:S(2)}, u32[]{:S(2)}) collective-permute-start(f32[4,3,16]{2,1,0:T(4,128)S(1)} %pad_maximum_fusion.refs_0_), channel_id=1, source_target_pairs={{0,3},{1,4},{2,5},{3,6},{4,7},{5,0},{6,1},{7,2},{8,11},{9,12},{10,... | collective-permute-start | bytes 2312 | tf_op jit(solution)/shard_map/ppermute | solution.py:160
  15.7 6.5 %collective-permute-start.4 = (f32[4,3,16]{2,1,0:T(4,128)S(1)}, f32[4,3,16]{2,1,0:T(4,128)S(1)}, u32[]{:S(2)}, u32[]{:S(2)}) collective-permute-start(f32[4,3,16]{2,1,0:T(4,128)S(1)} %pad_maximum_fusion.refs_0_), channel_id=1, source_target_pairs={{0,2},{1,3},{2,4},{3,5},{4,6},{5,7},{6,0},{7,1},{8,10},{9,11},{10,... | collective-permute-start | bytes 2312 | tf_op jit(solution)/shard_map/ppermute | solution.py:160
  17.5 6.3 %collective-permute-start.3 = (f32[4,3,16]{2,1,0:T(4,128)S(1)}, f32[4,3,16]{2,1,0:T(4,128)S(1)}, u32[]{:S(2)}, u32[]{:S(2)}) collective-permute-start(f32[4,3,16]{2,1,0:T(4,128)S(1)} %pad_maximum_fusion.refs_0_), channel_id=1, source_target_pairs={{0,1},{1,2},{2,3},{3,4},{4,5},{5,6},{6,7},{7,0},{8,9},{9,10},{10,1... | collective-permute-start | bytes 2312 | tf_op jit(solution)/shard_map/ppermute | solution.py:160
  18.7 0.7 %copy-start.4 = (s32[8,1]{0,1:T(1,128)S(1)}, s32[8,1]{0,1:T(1,128)}, u32[]{:S(2)}) copy-start(s32[8,1]{0,1:T(1,128)} %param.11) | copy-start | bytes 100
  19.4 0.9 %copy-start = (f32[8,2,16,128]{3,2,1,0:T(8,128)S(1)}, f32[8,2,16,128]{3,2,1,0:T(8,128)}, u32[]{:S(2)}) copy-start(f32[8,2,16,128]{3,2,1,0:T(8,128)} %blocks_hbm.1) | copy-start | bytes 393220
  27.8 6.9 %collective-permute-start.10 = (f32[4,2,16]{2,1,0:T(2,128)S(1)}, f32[4,2,16]{2,1,0:T(2,128)S(1)}, u32[]{:S(2)}, u32[]{:S(2)}) collective-permute-start(f32[4,2,16]{2,1,0:T(2,128)S(1)} %get-tuple-element.9), channel_id=1, source_target_pairs={{0,7},{1,0},{2,1},{3,2},{4,3},{5,4},{6,5},{7,6},{8,15},{9,8},{10,9... | collective-permute-start | bytes 1544 | tf_op jit(solution)/shard_map/ppermute | solution.py:160
  29.3 6.3 %collective-permute-start.16 = (f32[4,2,16]{2,1,0:T(2,128)S(1)}, f32[4,2,16]{2,1,0:T(2,128)S(1)}, u32[]{:S(2)}, u32[]{:S(2)}) collective-permute-start(f32[4,2,16]{2,1,0:T(2,128)S(1)} %get-tuple-element.10), channel_id=1, source_target_pairs={{0,1},{1,2},{2,3},{3,4},{4,5},{5,6},{6,7},{7,0},{8,9},{9,10},{10,1... | collective-permute-start | bytes 1544 | tf_op jit(solution)/shard_map/ppermute | solution.py:160
  29.8 8.5 %collective-permute-start.15 = (f32[4,2,16]{2,1,0:T(2,128)S(1)}, f32[4,2,16]{2,1,0:T(2,128)S(1)}, u32[]{:S(2)}, u32[]{:S(2)}) collective-permute-start(f32[4,2,16]{2,1,0:T(2,128)S(1)} %get-tuple-element.11), channel_id=1, source_target_pairs={{0,2},{1,3},{2,4},{3,5},{4,6},{5,7},{6,0},{7,1},{8,10},{9,11},{10,... | collective-permute-start | bytes 1544 | tf_op jit(solution)/shard_map/ppermute | solution.py:160
  30.2 8.1 %collective-permute-start.14 = (f32[4,2,16]{2,1,0:T(2,128)S(1)}, f32[4,2,16]{2,1,0:T(2,128)S(1)}, u32[]{:S(2)}, u32[]{:S(2)}) collective-permute-start(f32[4,2,16]{2,1,0:T(2,128)S(1)} %get-tuple-element.12), channel_id=1, source_target_pairs={{0,3},{1,4},{2,5},{3,6},{4,7},{5,0},{6,1},{7,2},{8,11},{9,12},{10,... | collective-permute-start | bytes 1544 | tf_op jit(solution)/shard_map/ppermute | solution.py:160
  32.6 5.7 %collective-permute-start.13 = (f32[4,2,16]{2,1,0:T(2,128)S(1)}, f32[4,2,16]{2,1,0:T(2,128)S(1)}, u32[]{:S(2)}, u32[]{:S(2)}) collective-permute-start(f32[4,2,16]{2,1,0:T(2,128)S(1)} %get-tuple-element.13), channel_id=1, source_target_pairs={{0,4},{1,5},{2,6},{3,7},{4,0},{5,1},{6,2},{7,3},{8,12},{9,13},{10,... | collective-permute-start | bytes 1544 | tf_op jit(solution)/shard_map/ppermute | solution.py:160
  34.6 4.5 %collective-permute-start.12 = (f32[4,2,16]{2,1,0:T(2,128)S(1)}, f32[4,2,16]{2,1,0:T(2,128)S(1)}, u32[]{:S(2)}, u32[]{:S(2)}) collective-permute-start(f32[4,2,16]{2,1,0:T(2,128)S(1)} %get-tuple-element.14), channel_id=1, source_target_pairs={{0,5},{1,6},{2,7},{3,0},{4,1},{5,2},{6,3},{7,4},{8,13},{9,14},{10,... | collective-permute-start | bytes 1544 | tf_op jit(solution)/shard_map/ppermute | solution.py:160
  35.7 4.0 %collective-permute-start.11 = (f32[4,2,16]{2,1,0:T(2,128)S(1)}, f32[4,2,16]{2,1,0:T(2,128)S(1)}, u32[]{:S(2)}, u32[]{:S(2)}) collective-permute-start(f32[4,2,16]{2,1,0:T(2,128)S(1)} %get-tuple-element.15), channel_id=1, source_target_pairs={{0,6},{1,7},{2,0},{3,1},{4,2},{5,3},{6,4},{7,5},{8,14},{9,15},{10,... | collective-permute-start | bytes 1544 | tf_op jit(solution)/shard_map/ppermute | solution.py:160
  39.7 2.1 %collective-permute-start.17 = (f32[2,16]{1,0:T(2,128)S(1)}, f32[2,16]{1,0:T(2,128)S(1)}, u32[]{:S(2)}, u32[]{:S(2)}) collective-permute-start(f32[2,16]{1,0:T(2,128)S(1)} %get-tuple-element.16), channel_id=1, source_target_pairs={{0,24},{8,0},{16,8},{24,16},{1,25},{9,1},{17,9},{25,17},{2,26},{10... | collective-permute-start | bytes 392 | tf_op jit(solution)/shard_map/ppermute | solution.py:160
  39.7 3.0 %collective-permute-start.19 = (f32[2,16]{1,0:T(2,128)S(1)}, f32[2,16]{1,0:T(2,128)S(1)}, u32[]{:S(2)}, u32[]{:S(2)}) collective-permute-start(f32[2,16]{1,0:T(2,128)S(1)} %get-tuple-element.17), channel_id=1, source_target_pairs={{0,8},{8,16},{16,24},{24,0},{1,9},{9,17},{17,25},{25,1},{2,10},{10... | collective-permute-start | bytes 392 | tf_op jit(solution)/shard_map/ppermute | solution.py:160
  40.2 3.6 %collective-permute-start.18 = (f32[2,16]{1,0:T(2,128)S(1)}, f32[2,16]{1,0:T(2,128)S(1)}, u32[]{:S(2)}, u32[]{:S(2)}) collective-permute-start(f32[2,16]{1,0:T(2,128)S(1)} %get-tuple-element.18), channel_id=1, source_target_pairs={{0,16},{8,24},{16,0},{24,8},{1,17},{9,25},{17,1},{25,9},{2,18},{10... | collective-permute-start | bytes 392 | tf_op jit(solution)/shard_map/ppermute | solution.py:160
  (1 other events, 0.7 us)

commit v2 on v0

v2 whole, which is shorter than its diff:
```python
import functools
import math

import jax
import jax.numpy as jnp
import numpy as np
from jax import lax
from jax.experimental import pallas as pl
from jax.experimental.pallas import tpu as pltpu
from jax.sharding import PartitionSpec as P

WAVENUMBER = 40.0
SOFTENING = 0.01
TURNS = WAVENUMBER / (2.0 * math.pi)
LANES = 128
SUB = 8


def even_fit(function, terms, reach):
    nodes = np.cos((np.arange(400) + 0.5) * np.pi / 400)
    squares = (nodes + 1) * 0.5 * reach * reach
    fit = np.polynomial.chebyshev.Chebyshev.fit(squares, function(np.sqrt(squares)), terms - 1)
    return [float(value) for value in fit.convert(kind=np.polynomial.Polynomial).coef]


ROOT2 = math.sqrt(2.0)
SINE = even_fit(lambda u: ROOT2 * math.pi * np.sinc(u), 5, 0.5)
COSINE = even_fit(lambda u: -ROOT2 * np.cos(np.pi * u), 5, 0.5)
ROUNDER = 1.5 * 2.0**23


def horner(coefficients, x):
    total = coefficients[-1] * x + coefficients[-2]
    for value in coefficients[-3::-1]:
        total = total * x + value
    return total


def pack_kernel(
    half_columns, gain, dest_hbm, tile_hbm, src_hbm, cur_hbm, blocks_hbm, copies_ref,
    dest_ref, tile_ref, src_ref, cur_ref, blocks_ref, message, near_rows, near_all, sems
):
    moves = [
        pltpu.make_async_copy(source, target, sems.at[k])
        for k, (source, target) in enumerate((
            (src_hbm, src_ref), (cur_hbm, cur_ref), (blocks_hbm, blocks_ref), (dest_hbm, dest_ref), (tile_hbm, tile_ref)
        ))
    ]
    for move in moves:
        move.start()
    members = copies_ref.shape[0]
    tiles = src_ref.shape[1] // LANES
    items, _, row_dev, _ = blocks_ref.shape
    per_row = LANES // row_dev
    columns = 2 * half_columns
    lane = lax.broadcasted_iota(jnp.int32, (SUB, LANES), 1)
    sub = lax.broadcasted_iota(jnp.int32, (SUB, LANES), 0)

    message[5 * tiles :, :] = jnp.zeros((message.shape[0] - 5 * tiles, LANES), jnp.float32)
    near_all[...] = jnp.zeros_like(near_all)
    moves[0].wait()
    moves[1].wait()
    for tile in range(tiles):
        part = pl.ds(tile * LANES, LANES)
        for c in range(3):
            message[c * tiles + tile : c * tiles + tile + 1, :] = src_ref[c : c + 1, part] * TURNS
        for c in range(2):
            message[(3 + c) * tiles + tile : (3 + c) * tiles + tile + 1, :] = cur_ref[c : c + 1, part]
    cr = message[3 * tiles : 4 * tiles, :]
    ci = message[4 * tiles : 5 * tiles, :]
    message[3 * tiles : 4 * tiles, :] = jnp.sqrt(cr * cr + ci * ci) * gain
    message[4 * tiles : 5 * tiles, :] = jnp.arctan2(ci, cr) * (0.5 / math.pi)

    def copy(member, _):
        copies_ref[member] = message[...]
        return 0

    lax.fori_loop(0, members, copy, 0, unroll=4)

    for move in moves[2:]:
        move.wait()
    for group in range(items // per_row):
        owner = jnp.zeros((SUB, LANES), jnp.int32)
        for k in range(per_row):
            block = group * per_row + k
            tile = pl.multiple_of(tile_ref[block] * LANES, LANES)
            cr = cur_ref[0:1, pl.ds(tile, LANES)]
            ci = cur_ref[1:2, pl.ds(tile, LANES)]
            br = blocks_ref[block, 0]
            bi = blocks_ref[block, 1]
            near_rows[pl.ds(k * row_dev, row_dev), :] = br * cr - bi * ci
            near_rows[pl.ds(LANES + k * row_dev, row_dev), :] = br * ci + bi * cr
            owner = jnp.where(lane // row_dev == k, dest_ref[block], owner)
        terms = lax.dot_general(
            jnp.ones((SUB, LANES), jnp.float32), near_rows[...], (((1,), (1,)), ((), ())),
            precision=lax.Precision.HIGHEST, preferred_element_type=jnp.float32,
        )
        for block in range(columns // SUB):
            place = pl.ds(block * SUB, SUB)
            mine = owner == sub + block * SUB
            near_all[0, place, :] += jnp.where(mine, terms[:, :LANES], 0.0)
            near_all[1, place, :] += jnp.where(mine, terms[:, LANES:], 0.0)
    for block in range(columns // SUB):
        place = pl.ds(block * SUB, SUB)
        re = near_all[0, place, :]
        im = near_all[1, place, :]
        shift = LANES // 2
        while shift >= row_dev:
            re = re + pltpu.roll(re, shift, 1)
            im = im + pltpu.roll(im, shift, 1)
            shift //= 2
        near_all[0, place, :] = jnp.where(lane < row_dev, re, jnp.where(lane < 2 * row_dev, im, 0.0))
    base = lax.axis_index("row") * half_columns
    for k in range(half_columns):
        for half in range(2):
            spot = 5 * tiles + half
            copies_ref[base + k, spot : spot + 1, :] = near_all[0, half * half_columns + k : half * half_columns + k + 1, :]


def far_kernel(half_columns, other, tests_ref, messages_ref, out_ref):
    members = messages_ref.shape[0]
    tiles = (messages_ref.shape[1] - SUB) // 5
    row_dev = tests_ref.shape[1]
    groups = row_dev // SUB
    lane = lax.broadcasted_iota(jnp.int32, (row_dev, LANES), 1)
    sub = lax.broadcasted_iota(jnp.int32, (row_dev, LANES), 0)
    soft = (SOFTENING * TURNS) ** 2

    points = jnp.concatenate([tests_ref[...], jnp.zeros((3, LANES - row_dev), jnp.float32)], axis=1) * TURNS
    tests = []
    for c in range(3):
        column = jnp.sum(jnp.where(lane == sub, points[c : c + 1, :], 0.0), axis=1, keepdims=True)
        wide = jnp.broadcast_to(column, (row_dev, LANES))
        tests.append([wide[g * SUB : (g + 1) * SUB] for g in range(groups)])

    def step(member, sums):
        for tile in range(tiles):
            sx, sy, sz, size, turn = [
                jnp.broadcast_to(messages_ref[member, c * tiles + tile : c * tiles + tile + 1, :], (SUB, LANES))
                for c in range(5)
            ]
            new = []
            for g, (re, im) in enumerate(sums):
                dx = tests[0][g] - sx
                dy = tests[1][g] - sy
                dz = tests[2][g] - sz
                square = dx * dx + dy * dy + (dz * dz + soft)
                inverse = lax.rsqrt(square)
                t = square * inverse - turn
                u = t - ((t + ROUNDER) - ROUNDER)
                u2 = u * u
                s = u * horner(SINE, u2)
                c = horner(COSINE, u2)
                a = inverse * size
                new.append((re + a * (1.0 - s * s), im + a * (s * c)))
            sums = tuple(new)
        return sums

    zero = jnp.zeros((SUB, LANES), jnp.float32)
    sums = lax.fori_loop(0, members, step, tuple((zero, zero) for _ in range(groups)))
    re, im = [
        jnp.concatenate([jnp.sum(pair[part], axis=1, keepdims=True) for pair in sums], axis=0) for part in range(2)
    ]
    both = jnp.where(lane == sub, re, jnp.where(lane == sub + row_dev, im, 0.0))
    both = jnp.sum(both, axis=0, keepdims=True)
    half = lax.axis_index("half")
    spot = 5 * tiles + (1 - half if other else half)
    base = lax.axis_index("row") * half_columns
    for k in range(half_columns):
        both = both + messages_ref[base + k, pl.ds(spot, 1), :]
    out_ref[0:1, :] = both[:, :row_dev]
    out_ref[1:2, :] = both[:, row_dev : 2 * row_dev]


def swap(x):
    return lax.ppermute(x, "half", [(0, 1), (1, 0)])


def local(rows, half_columns, test_points, src_points, currents, near_blocks, near_dest, near_tile):
    row_dev = test_points.shape[1]
    width = src_points.shape[1]
    items = near_blocks.shape[0]
    members = rows * half_columns
    gain = TURNS / math.sqrt(width * members * 2)
    message = (5 * width // LANES + SUB, LANES)
    vmem = pl.BlockSpec(memory_space=pltpu.VMEM)
    hbm = pl.BlockSpec(memory_space=pltpu.HBM)
    params = pltpu.CompilerParams(vmem_limit_bytes=24 << 20)

    partner_points = swap(test_points)
    copies = pl.pallas_call(
        functools.partial(pack_kernel, half_columns, gain),
        out_shape=jax.ShapeDtypeStruct((members,) + message, jnp.float32),
        in_specs=[hbm] * 5,
        out_specs=vmem,
        scratch_shapes=[
            pltpu.SMEM((items,), jnp.int32),
            pltpu.SMEM((items,), jnp.int32),
            pltpu.VMEM((3, width), jnp.float32),
            pltpu.VMEM((2, width), jnp.float32),
            pltpu.VMEM(near_blocks.shape, jnp.float32),
            pltpu.VMEM(message, jnp.float32),
            pltpu.VMEM((2 * LANES, LANES), jnp.float32),
            pltpu.VMEM((2, 2 * half_columns, LANES), jnp.float32),
            pltpu.SemaphoreType.DMA((5,)),
        ],
        compiler_params=params,
        cost_estimate=pl.CostEstimate(flops=1 << 20, bytes_accessed=1 << 20, transcendentals=0),
    )(near_dest.reshape(-1), near_tile.reshape(-1), src_points, currents, near_blocks)
    messages = lax.all_to_all(copies, ("row", "column"), split_axis=0, concat_axis=0, tiled=True)

    def far(points, other):
        evaluations = width * members * row_dev
        return pl.pallas_call(
            functools.partial(far_kernel, half_columns, other),
            out_shape=jax.ShapeDtypeStruct((2, row_dev), jnp.float32),
            in_specs=[vmem, vmem],
            out_specs=vmem,
            compiler_params=params,
            cost_estimate=pl.CostEstimate(flops=40 * evaluations, bytes_accessed=4 << 20, transcendentals=evaluations),
        )(points, messages)

    from_partner = swap(far(partner_points, True))
    return far(test_points, False) + from_partner


def solution(mesh):
    rows, columns = mesh.shape["row"], mesh.shape["col"]
    finer = jax.sharding.Mesh(mesh.devices.reshape(rows, 2, columns // 2), ("row", "half", "column"))
    every = ("row", "half", "column")
    in_specs = (
        P(None, every),
        P(None, every),
        P(None, every),
        P(every, None, None, None),
        P(every, None),
        P(every, None),
    )
    body = functools.partial(local, rows, columns // 2)
    return jax.shard_map(body, mesh=finer, in_specs=in_specs, out_specs=P(None, every), check_vma=False)
```

time: 30.7 us -> 27.1 us (0.88)
  blocking collectives: 23.3 us -> 0 us
  starting transfers between devices: 0 us -> 11.6 us
  waiting for transfers between devices: 0 us -> 5.93 us
  local copies, waits for them, and re-layouts: 1.39 us -> 2.99 us
  Pallas kernels: 5.17 us -> 5.65 us
    all_to_all x2 -> x0, blocking collectives: 23.3 us -> none  [the longest x1 14.4 us: local(): lax.all_to_all(copies, ('row', 'col'), split_axis=0, concat_axis=0, tiled...]
    all_to_all x0 -> x1, starting transfers between devices: none -> 6.3 us  [local(): lax.all_to_all(copies, ('row', 'column'), split_axis=0, concat_axis=0, ti...]
    ppermute x0 -> x2, starting transfers between devices: none -> 5.26 us  [swap(): return lax.ppermute(x, 'half', [(0, 1), (1, 0)])]
    all_to_all x0 -> x1, waiting for transfers between devices: none -> 3.29 us  [local(): lax.all_to_all(copies, ('row', 'column'), split_axis=0, concat_axis=0, ti...]
    ppermute x0 -> x2, waiting for transfers between devices: none -> 2.65 us  [swap(): return lax.ppermute(x, 'half', [(0, 1), (1, 0)])]
    unnamed x10 -> x12, local copies, waits for them, and re-layouts: 0.67 us -> 2.99 us
    broadcast_in_dim x1 -> x0, local copies, waits for them, and re-layouts: 0.73 us -> none  [local(): copies = jnp.broadcast_to(test_points[None], (devices, 3, row_dev))]
    reduce_sum x1 -> x0, other arithmetic: 0.6 us -> none  [local(): return parts.sum(axis=0)]
  transfers between devices with their start and end apart: 0 -> 3, of which waited for: 0 -> 2; matrix products, arithmetic and copies ran while one was open for 0% -> 0% of each run, Pallas kernels for 0% -> 7%
where the time goes in v2:
time: 27.1 us; the launch traced here: 26.7 us
  starting transfers between devices  11.6 us (43%)
  waiting for transfers between devices  5.93 us (22%)
  Pallas kernels  5.65 us (21%)
  local copies, waits for them, and re-layouts  2.99 us (11%)
  other arithmetic  0.56 us (2%)
    all_to_all x1, starting transfers between devices, local(): lax.all_to_all(copies, ('row', 'column'), split_axis=0, concat_axis=0, ti...  6.3 us
    ppermute x2, starting transfers between devices, swap(): return lax.ppermute(x, 'half', [(0, 1), (1, 0)])  5.26 us
    pallas_call x2, Pallas kernels, far(): pl.pallas_call(functools.partial(far_kernel, half_columns, other), out_sh...  3.7 us
    all_to_all x1, waiting for transfers between devices, local(): lax.all_to_all(copies, ('row', 'column'), split_axis=0, concat_axis=0, ti...  3.29 us
    unnamed x12, local copies, waits for them, and re-layouts  2.99 us
    ppermute x2, waiting for transfers between devices, swap(): return lax.ppermute(x, 'half', [(0, 1), (1, 0)])  2.65 us
    pallas_call x1, Pallas kernels, local(): pl.pallas_call(functools.partial(pack_kernel, half_columns, gain), out_sh...  1.94 us
    add x1, other arithmetic, local(): return far(test_points, False) + from_partner  0.56 us
  transfers between devices with their start and end apart: 3, of which 2 were waited for; matrix products, arithmetic and copies ran while one was open for 0% of the time, Pallas kernels for 7%

profile of v2, /device:TPU:0, one launch (start us, length us, event | category | flops | bytes accessed | tf_op | source)
XLA Modules:
  0.0 26.7 jit_solution(17818664741109347175)
XLA Ops:
  0.0 0.0 copy-start.3
  0.0 0.0 copy-start.4
  0.0 0.7 %copy-done.3 = s32[8,1]{0,1:T(1,128)S(1)} copy-done((s32[8,1]{0,1:T(1,128)S(1)}, s32[8,1]{0,1:T(1,128)}, u32[]{:S(2)}) %copy-start.3) | copy-done | bytes 56
  0.7 0.0 copy-done.4
  0.7 0.0 copy-start
  0.7 0.9 %copy-done = f32[8,2,16,128]{3,2,1,0:T(8,128)S(1)} copy-done((f32[8,2,16,128]{3,2,1,0:T(8,128)S(1)}, f32[8,2,16,128]{3,2,1,0:T(8,128)}, u32[]{:S(2)}) %copy-start) | copy-done | bytes 131096
  1.6 0.0 copy-start.1
  1.6 0.7 %copy-done.1 = f32[3,1024]{1,0:T(4,128)S(1)} copy-done((f32[3,1024]{1,0:T(4,128)S(1)}, f32[3,1024]{1,0:T(4,128)}, u32[]{:S(2)}) %copy-start.1) | copy-done | bytes 12312
  2.3 0.0 copy-start.2
  2.3 0.7 %copy-done.2 = f32[2,1024]{1,0:T(2,128)S(1)} copy-done((f32[2,1024]{1,0:T(2,128)S(1)}, f32[2,1024]{1,0:T(2,128)}, u32[]{:S(2)}) %copy-start.2) | copy-done | bytes 8216
  3.0 1.9 %shard_map.64 = f32[16,48,128]{2,1,0:T(8,128)} custom-call(s32[8]{0:T(128)S(1)} %bitcast.2, s32[8]{0:T(128)S(1)} %bitcast.3, f32[3,1024]{1,0:T(4,128)S(1)} %copy-done.1, f32[2,1024]{1,0:T(2,128)S(1)} %copy-done.2, f32[8,2,16,128]{3,2,1,0:T(8,128)S(1)} %copy-done), custom_call_target="tpu_custom_call" | custom-call | flops 1048576 | bytes 1048576 | tf_op jit(solution)/shard_map/pallas_call | solution.py:191
  4.9 0.0 copy-start.5
  5.0 6.3 %all-to-all-start = ((f32[16,48,128]{2,1,0:T(8,128)}), f32[16,48,128]{2,1,0:T(8,128)S(1)}, u32[]{:S(2)}, u32[]{:S(2)}) async-start(f32[16,48,128]{2,1,0:T(8,128)} %shard_map.64), calls=%async_computation | async-start | bytes 786432 | tf_op jit(solution)/shard_map/all_to_all | solution.py:210
  11.3 0.0 copy-done.5
  11.3 2.7 %collective-permute-start = (f32[3,16]{1,0:T(4,128)S(1)}, f32[3,16]{1,0:T(4,128)S(1)}, u32[]{:S(2)}, u32[]{:S(2)}) collective-permute-start(f32[3,16]{1,0:T(4,128)S(1)} %copy-done.5), channel_id=1, source_target_pairs={{0,4},{4,0},{1,5},{5,1},{2,6},{6,2},{3,7},{7,3},{8,12},{12,8},{9,1... | collective-permute-start | bytes 584 | tf_op jit(solution)/shard_map/ppermute | solution.py:176
  13.9 2.6 %collective-permute-done.tests_ref = f32[3,16]{1,0:T(4,128)S(1)} collective-permute-done((f32[3,16]{1,0:T(4,128)S(1)}, f32[3,16]{1,0:T(4,128)S(1)}, u32[]{:S(2)}, u32[]{:S(2)}) %collective-permute-start) | collective-permute-done | bytes 224 | tf_op jit(solution)/shard_map/ppermute | solution.py:176
  16.5 3.3 %all-to-all-done.messages_ref = f32[16,48,128]{2,1,0:T(8,128)S(1)} async-done(((f32[16,48,128]{2,1,0:T(8,128)}), f32[16,48,128]{2,1,0:T(8,128)S(1)}, u32[]{:S(2)}, u32[]{:S(2)}) %all-to-all-start) | async-done | bytes 393248 | tf_op jit(solution)/shard_map/all_to_all | solution.py:210
  19.8 1.9 %shard_map.66 = f32[2,16]{1,0:T(2,128)S(1)} custom-call(f32[3,16]{1,0:T(4,128)S(1)} %collective-permute-done.tests_ref, f32[16,48,128]{2,1,0:T(8,128)S(1)} %all-to-all-done.messages_ref), custom_call_target="tpu_custom_call" | custom-call | flops 10485760 | bytes 4194304 | tf_op jit(solution)/shard_map/pallas_call | solution.py:214
  21.7 2.6 %collective-permute-start.1 = (f32[2,16]{1,0:T(2,128)S(1)}, f32[2,16]{1,0:T(2,128)S(1)}, u32[]{:S(2)}, u32[]{:S(2)}) collective-permute-start(f32[2,16]{1,0:T(2,128)S(1)} %shard_map.66), channel_id=1, source_target_pairs={{0,4},{4,0},{1,5},{5,1},{2,6},{6,2},{3,7},{7,3},{8,12},{12,8},{9,1... | collective-permute-start | bytes 392 | tf_op jit(solution)/shard_map/ppermute | solution.py:176
  24.3 1.9 %shard_map.65 = f32[2,16]{1,0:T(2,128)S(1)} custom-call(f32[3,16]{1,0:T(4,128)S(1)} %copy-done.5, f32[16,48,128]{2,1,0:T(8,128)S(1)} %all-to-all-done.messages_ref), custom_call_target="tpu_custom_call" | custom-call | flops 10485760 | bytes 4194304 | tf_op jit(solution)/shard_map/pallas_call | solution.py:214
  26.1 0.0 collective-permute-done.1
  26.2 0.6 %add.3 = f32[2,16]{1,0:T(2,128)} add(f32[2,16]{1,0:T(2,128)S(1)} %shard_map.65, f32[2,16]{1,0:T(2,128)S(1)} %collective-permute-done.1) | non-fusion elementwise | flops 32 | bytes 384 | tf_op jit(solution)/shard_map/add | solution.py:224
Async XLA Ops:
  0.0 0.7 %copy-start.3 = (s32[8,1]{0,1:T(1,128)S(1)}, s32[8,1]{0,1:T(1,128)}, u32[]{:S(2)}) copy-start(s32[8,1]{0,1:T(1,128)} %param.10) | copy-start | bytes 100
  0.0 0.7 %copy-start.4 = (s32[8,1]{0,1:T(1,128)S(1)}, s32[8,1]{0,1:T(1,128)}, u32[]{:S(2)}) copy-start(s32[8,1]{0,1:T(1,128)} %param.11) | copy-start | bytes 100
  0.7 0.9 %copy-start = (f32[8,2,16,128]{3,2,1,0:T(8,128)S(1)}, f32[8,2,16,128]{3,2,1,0:T(8,128)}, u32[]{:S(2)}) copy-start(f32[8,2,16,128]{3,2,1,0:T(8,128)} %blocks_hbm.1) | copy-start | bytes 393220
  1.6 0.7 %copy-start.1 = (f32[3,1024]{1,0:T(4,128)S(1)}, f32[3,1024]{1,0:T(4,128)}, u32[]{:S(2)}) copy-start(f32[3,1024]{1,0:T(4,128)} %src_hbm.1) | copy-start | bytes 36868
  2.3 0.7 %copy-start.2 = (f32[2,1024]{1,0:T(2,128)S(1)}, f32[2,1024]{1,0:T(2,128)}, u32[]{:S(2)}) copy-start(f32[2,1024]{1,0:T(2,128)} %cur_hbm.1) | copy-start | bytes 24580
  4.9 6.3 %copy-start.5 = (f32[3,16]{1,0:T(4,128)S(1)}, f32[3,16]{1,0:T(4,128)}, u32[]{:S(2)}) copy-start(f32[3,16]{1,0:T(4,128)} %tests_ref.1) | copy-start | bytes 580
  5.0 14.9 %all-to-all-start = ((f32[16,48,128]{2,1,0:T(8,128)}), f32[16,48,128]{2,1,0:T(8,128)S(1)}, u32[]{:S(2)}, u32[]{:S(2)}) async-start(f32[16,48,128]{2,1,0:T(8,128)} %shard_map.64), calls=%async_computation | async-start | bytes 786432 | tf_op jit(solution)/shard_map/all_to_all | solution.py:210
  11.3 5.3 %collective-permute-start = (f32[3,16]{1,0:T(4,128)S(1)}, f32[3,16]{1,0:T(4,128)S(1)}, u32[]{:S(2)}, u32[]{:S(2)}) collective-permute-start(f32[3,16]{1,0:T(4,128)S(1)} %copy-done.5), channel_id=1, source_target_pairs={{0,4},{4,0},{1,5},{5,1},{2,6},{6,2},{3,7},{7,3},{8,12},{12,8},{9,1... | collective-permute-start | bytes 584 | tf_op jit(solution)/shard_map/ppermute | solution.py:176
  21.7 4.5 %collective-permute-start.1 = (f32[2,16]{1,0:T(2,128)S(1)}, f32[2,16]{1,0:T(2,128)S(1)}, u32[]{:S(2)}, u32[]{:S(2)}) collective-permute-start(f32[2,16]{1,0:T(2,128)S(1)} %shard_map.66), channel_id=1, source_target_pairs={{0,4},{4,0},{1,5},{5,1},{2,6},{6,2},{3,7},{7,3},{8,12},{12,8},{9,1... | collective-permute-start | bytes 392 | tf_op jit(solution)/shard_map/ppermute | solution.py:176

commit v3 on v2

--- a/solution.py
+++ b/solution.py
@@ -24,7 +24,7 @@
 
 
 ROOT2 = math.sqrt(2.0)
-SINE = even_fit(lambda u: ROOT2 * math.pi * np.sinc(u), 5, 0.5)
+SINE = even_fit(lambda u: ROOT2 * math.pi * np.sinc(u), 4, 0.5)
 COSINE = even_fit(lambda u: -ROOT2 * np.cos(np.pi * u), 5, 0.5)
 ROUNDER = 1.5 * 2.0**23
 
@@ -38,7 +38,7 @@
 
 def pack_kernel(
     half_columns, gain, dest_hbm, tile_hbm, src_hbm, cur_hbm, blocks_hbm, copies_ref,
-    dest_ref, tile_ref, src_ref, cur_ref, blocks_ref, message, near_rows, near_all, sems
+    dest_ref, tile_ref, src_ref, cur_ref, blocks_ref, message, near_all, sems
 ):
     moves = [
         pltpu.make_async_copy(source, target, sems.at[k])
@@ -81,6 +81,7 @@
         move.wait()
     for group in range(items // per_row):
         owner = jnp.zeros((SUB, LANES), jnp.int32)
+        sums = [jnp.zeros((SUB, LANES), jnp.float32)] * 2
         for k in range(per_row):
             block = group * per_row + k
             tile = pl.multiple_of(tile_ref[block] * LANES, LANES)
@@ -88,18 +89,18 @@
             ci = cur_ref[1:2, pl.ds(tile, LANES)]
             br = blocks_ref[block, 0]
             bi = blocks_ref[block, 1]
-            near_rows[pl.ds(k * row_dev, row_dev), :] = br * cr - bi * ci
-            near_rows[pl.ds(LANES + k * row_dev, row_dev), :] = br * ci + bi * cr
+            for part, product in enumerate((br * cr - bi * ci, br * ci + bi * cr)):
+                total = jnp.sum(product, axis=1, keepdims=True)
+                for piece in range(row_dev // SUB):
+                    spot = lane == sub + (k * row_dev + piece * SUB)
+                    sums[part] = jnp.where(spot, total[piece * SUB : (piece + 1) * SUB], sums[part])
             owner = jnp.where(lane // row_dev == k, dest_ref[block], owner)
-        terms = lax.dot_general(
-            jnp.ones((SUB, LANES), jnp.float32), near_rows[...], (((1,), (1,)), ((), ())),
-            precision=lax.Precision.HIGHEST, preferred_element_type=jnp.float32,
-        )
+        terms = [jnp.sum(x, axis=0, keepdims=True) for x in sums]
         for block in range(columns // SUB):
             place = pl.ds(block * SUB, SUB)
             mine = owner == sub + block * SUB
-            near_all[0, place, :] += jnp.where(mine, terms[:, :LANES], 0.0)
-            near_all[1, place, :] += jnp.where(mine, terms[:, LANES:], 0.0)
+            for part in range(2):
+                near_all[part, place, :] += jnp.where(mine, terms[part], 0.0)
     for block in range(columns // SUB):
         place = pl.ds(block * SUB, SUB)
         re = near_all[0, place, :]
@@ -152,12 +153,13 @@
                 s = u * horner(SINE, u2)
                 c = horner(COSINE, u2)
                 a = inverse * size
-                new.append((re + a * (1.0 - s * s), im + a * (s * c)))
+                p = a * s
+                new.append(((re + a) - p * s, im + p * c))
             sums = tuple(new)
         return sums
 
     zero = jnp.zeros((SUB, LANES), jnp.float32)
-    sums = lax.fori_loop(0, members, step, tuple((zero, zero) for _ in range(groups)))
+    sums = lax.fori_loop(0, members, step, tuple((zero, zero) for _ in range(groups)), unroll=2)
     re, im = [
         jnp.concatenate([jnp.sum(pair[part], axis=1, keepdims=True) for pair in sums], axis=0) for part in range(2)
     ]
@@ -200,11 +202,9 @@
             pltpu.VMEM((2, width), jnp.float32),
             pltpu.VMEM(near_blocks.shape, jnp.float32),
             pltpu.VMEM(message, jnp.float32),
-            pltpu.VMEM((2 * LANES, LANES), jnp.float32),
             pltpu.VMEM((2, 2 * half_columns, LANES), jnp.float32),
             pltpu.SemaphoreType.DMA((5,)),
         ],
-        compiler_params=params,
         cost_estimate=pl.CostEstimate(flops=1 << 20, bytes_accessed=1 << 20, transcendentals=0),
     )(near_dest.reshape(-1), near_tile.reshape(-1), src_points, currents, near_blocks)
     messages = lax.all_to_all(copies, ("row", "column"), split_axis=0, concat_axis=0, tiled=True)

time: 27.1 us -> 24 us (0.89)
  local copies, waits for them, and re-layouts: 2.99 us -> 0.01 us
    unnamed x12 -> x2, local copies, waits for them, and re-layouts: 2.99 us -> 0.01 us
    pallas_call x2, Pallas kernels: 3.7 us -> 3.35 us  [far(): pl.pallas_call(functools.partial(far_kernel, half_columns, other), out_sh...]
  transfers between devices with their start and end apart: 3 -> 3, of which waited for: 2 -> 3; matrix products, arithmetic and copies ran while one was open for 0% -> 0% of each run, Pallas kernels for 7% -> 7%
where the time goes in v3:
time: 24 us; the launch traced here: 23.7 us
  starting transfers between devices  11.5 us (48%)
  waiting for transfers between devices  6.11 us (25%)
  Pallas kernels  5.43 us (23%)
  other arithmetic  0.56 us (2%)
    all_to_all x1, starting transfers between devices, local(): lax.all_to_all(copies, ('row', 'column'), split_axis=0, concat_axis=0, ti...  6.3 us
    ppermute x2, starting transfers between devices, swap(): return lax.ppermute(x, 'half', [(0, 1), (1, 0)])  5.24 us
    pallas_call x2, Pallas kernels, far(): pl.pallas_call(functools.partial(far_kernel, half_columns, other), out_sh...  3.35 us
    all_to_all x1, waiting for transfers between devices, local(): lax.all_to_all(copies, ('row', 'column'), split_axis=0, concat_axis=0, ti...  3.29 us
    ppermute x2, waiting for transfers between devices, swap(): return lax.ppermute(x, 'half', [(0, 1), (1, 0)])  2.82 us
    pallas_call x1, Pallas kernels, local(): pl.pallas_call(functools.partial(pack_kernel, half_columns, gain), out_sh...  2.08 us
    add x1, other arithmetic, local(): return far(test_points, False) + from_partner  0.56 us
  transfers between devices with their start and end apart: 3, of which 3 were waited for; matrix products, arithmetic and copies ran while one was open for 0% of the time, Pallas kernels for 7%

profile of v3, /device:TPU:0, one launch (start us, length us, event | category | flops | bytes accessed | tf_op | source)
XLA Modules:
  0.0 23.7 jit_solution(2237265023623654481)
XLA Ops:
  0.0 2.1 %shard_map.64 = f32[16,48,128]{2,1,0:T(8,128)} custom-call(s32[8]{0:T(128)} %bitcast.2, s32[8]{0:T(128)} %bitcast.3, f32[3,1024]{1,0:T(4,128)} %src_hbm.1, f32[2,1024]{1,0:T(2,128)} %cur_hbm.1, f32[8,2,16,128]{3,2,1,0:T(8,128)} %blocks_hbm.1), custom_call_target="tpu_custom_call" | custom-call | flops 1048576 | bytes 1048576 | tf_op jit(solution)/shard_map/pallas_call | solution.py:193
  2.1 0.0 copy-start
  2.1 6.3 %all-to-all-start = ((f32[16,48,128]{2,1,0:T(8,128)}), f32[16,48,128]{2,1,0:T(8,128)S(1)}, u32[]{:S(2)}, u32[]{:S(2)}) async-start(f32[16,48,128]{2,1,0:T(8,128)} %shard_map.64), calls=%async_computation | async-start | bytes 786432 | tf_op jit(solution)/shard_map/all_to_all | solution.py:210
  8.4 0.0 copy-done
  8.4 2.7 %collective-permute-start = (f32[3,16]{1,0:T(4,128)S(1)}, f32[3,16]{1,0:T(4,128)S(1)}, u32[]{:S(2)}, u32[]{:S(2)}) collective-permute-start(f32[3,16]{1,0:T(4,128)S(1)} %copy-done), channel_id=1, source_target_pairs={{0,4},{4,0},{1,5},{5,1},{2,6},{6,2},{3,7},{7,3},{8,12},{12,8},{9,1... | collective-permute-start | bytes 584 | tf_op jit(solution)/shard_map/ppermute | solution.py:178
  11.1 2.6 %collective-permute-done.tests_ref = f32[3,16]{1,0:T(4,128)S(1)} collective-permute-done((f32[3,16]{1,0:T(4,128)S(1)}, f32[3,16]{1,0:T(4,128)S(1)}, u32[]{:S(2)}, u32[]{:S(2)}) %collective-permute-start) | collective-permute-done | bytes 224 | tf_op jit(solution)/shard_map/ppermute | solution.py:178
  13.7 3.3 %all-to-all-done.messages_ref = f32[16,48,128]{2,1,0:T(8,128)S(1)} async-done(((f32[16,48,128]{2,1,0:T(8,128)}), f32[16,48,128]{2,1,0:T(8,128)S(1)}, u32[]{:S(2)}, u32[]{:S(2)}) %all-to-all-start) | async-done | bytes 393248 | tf_op jit(solution)/shard_map/all_to_all | solution.py:210
  17.0 1.7 %shard_map.66 = f32[2,16]{1,0:T(2,128)S(1)} custom-call(f32[3,16]{1,0:T(4,128)S(1)} %collective-permute-done.tests_ref, f32[16,48,128]{2,1,0:T(8,128)S(1)} %all-to-all-done.messages_ref), custom_call_target="tpu_custom_call" | custom-call | flops 10485760 | bytes 4194304 | tf_op jit(solution)/shard_map/pallas_call | solution.py:214
  18.6 2.6 %collective-permute-start.1 = (f32[2,16]{1,0:T(2,128)S(1)}, f32[2,16]{1,0:T(2,128)S(1)}, u32[]{:S(2)}, u32[]{:S(2)}) collective-permute-start(f32[2,16]{1,0:T(2,128)S(1)} %shard_map.66), channel_id=1, source_target_pairs={{0,4},{4,0},{1,5},{5,1},{2,6},{6,2},{3,7},{7,3},{8,12},{12,8},{9,1... | collective-permute-start | bytes 392 | tf_op jit(solution)/shard_map/ppermute | solution.py:178
  21.2 1.7 %shard_map.65 = f32[2,16]{1,0:T(2,128)S(1)} custom-call(f32[3,16]{1,0:T(4,128)S(1)} %copy-done, f32[16,48,128]{2,1,0:T(8,128)S(1)} %all-to-all-done.messages_ref), custom_call_target="tpu_custom_call" | custom-call | flops 10485760 | bytes 4194304 | tf_op jit(solution)/shard_map/pallas_call | solution.py:214
  22.9 0.2 collective-permute-done.1
  23.1 0.6 %add.3 = f32[2,16]{1,0:T(2,128)} add(f32[2,16]{1,0:T(2,128)S(1)} %shard_map.65, f32[2,16]{1,0:T(2,128)S(1)} %collective-permute-done.1) | non-fusion elementwise | flops 32 | bytes 384 | tf_op jit(solution)/shard_map/add | solution.py:224
Async XLA Ops:
  2.1 6.3 %copy-start = (f32[3,16]{1,0:T(4,128)S(1)}, f32[3,16]{1,0:T(4,128)}, u32[]{:S(2)}) copy-start(f32[3,16]{1,0:T(4,128)} %tests_ref.1) | copy-start | bytes 580
  2.1 14.9 %all-to-all-start = ((f32[16,48,128]{2,1,0:T(8,128)}), f32[16,48,128]{2,1,0:T(8,128)S(1)}, u32[]{:S(2)}, u32[]{:S(2)}) async-start(f32[16,48,128]{2,1,0:T(8,128)} %shard_map.64), calls=%async_computation | async-start | bytes 786432 | tf_op jit(solution)/shard_map/all_to_all | solution.py:210
  8.4 5.3 %collective-permute-start = (f32[3,16]{1,0:T(4,128)S(1)}, f32[3,16]{1,0:T(4,128)S(1)}, u32[]{:S(2)}, u32[]{:S(2)}) collective-permute-start(f32[3,16]{1,0:T(4,128)S(1)} %copy-done), channel_id=1, source_target_pairs={{0,4},{4,0},{1,5},{5,1},{2,6},{6,2},{3,7},{7,3},{8,12},{12,8},{9,1... | collective-permute-start | bytes 584 | tf_op jit(solution)/shard_map/ppermute | solution.py:178
  18.6 4.5 %collective-permute-start.1 = (f32[2,16]{1,0:T(2,128)S(1)}, f32[2,16]{1,0:T(2,128)S(1)}, u32[]{:S(2)}, u32[]{:S(2)}) collective-permute-start(f32[2,16]{1,0:T(2,128)S(1)} %shard_map.66), channel_id=1, source_target_pairs={{0,4},{4,0},{1,5},{5,1},{2,6},{6,2},{3,7},{7,3},{8,12},{12,8},{9,1... | collective-permute-start | bytes 392 | tf_op jit(solution)/shard_map/ppermute | solution.py:178

commit v4 on v3

--- a/solution.py
+++ b/solution.py
@@ -58,27 +58,9 @@
 
     message[5 * tiles :, :] = jnp.zeros((message.shape[0] - 5 * tiles, LANES), jnp.float32)
     near_all[...] = jnp.zeros_like(near_all)
-    moves[0].wait()
-    moves[1].wait()
-    for tile in range(tiles):
-        part = pl.ds(tile * LANES, LANES)
-        for c in range(3):
-            message[c * tiles + tile : c * tiles + tile + 1, :] = src_ref[c : c + 1, part] * TURNS
-        for c in range(2):
-            message[(3 + c) * tiles + tile : (3 + c) * tiles + tile + 1, :] = cur_ref[c : c + 1, part]
-    cr = message[3 * tiles : 4 * tiles, :]
-    ci = message[4 * tiles : 5 * tiles, :]
-    message[3 * tiles : 4 * tiles, :] = jnp.sqrt(cr * cr + ci * ci) * gain
-    message[4 * tiles : 5 * tiles, :] = jnp.arctan2(ci, cr) * (0.5 / math.pi)
-
-    def copy(member, _):
-        copies_ref[member] = message[...]
-        return 0
-
-    lax.fori_loop(0, members, copy, 0, unroll=4)
-
-    for move in moves[2:]:
+    for move in moves:
         move.wait()
+
     for group in range(items // per_row):
         owner = jnp.zeros((SUB, LANES), jnp.int32)
         sums = [jnp.zeros((SUB, LANES), jnp.float32)] * 2
@@ -111,6 +93,24 @@
             im = im + pltpu.roll(im, shift, 1)
             shift //= 2
         near_all[0, place, :] = jnp.where(lane < row_dev, re, jnp.where(lane < 2 * row_dev, im, 0.0))
+
+    for tile in range(tiles):
+        part = pl.ds(tile * LANES, LANES)
+        for c in range(3):
+            message[c * tiles + tile : c * tiles + tile + 1, :] = src_ref[c : c + 1, part] * TURNS
+        for c in range(2):
+            message[(3 + c) * tiles + tile : (3 + c) * tiles + tile + 1, :] = cur_ref[c : c + 1, part]
+    cr = message[3 * tiles : 4 * tiles, :]
+    ci = message[4 * tiles : 5 * tiles, :]
+    message[3 * tiles : 4 * tiles, :] = jnp.sqrt(cr * cr + ci * ci) * gain
+    message[4 * tiles : 5 * tiles, :] = jnp.arctan2(ci, cr) * (0.5 / math.pi)
+
+    def copy(member, _):
+        copies_ref[member] = message[...]
+        return 0
+
+    lax.fori_loop(0, members, copy, 0, unroll=16)
+
     base = lax.axis_index("row") * half_columns
     for k in range(half_columns):
         for half in range(2):
@@ -118,7 +118,7 @@
             copies_ref[base + k, spot : spot + 1, :] = near_all[0, half * half_columns + k : half * half_columns + k + 1, :]
 
 
-def far_kernel(half_columns, other, tests_ref, messages_ref, out_ref):
+def far_sums(half_columns, other, tests_ref, messages_ref, out_ref):
     members = messages_ref.shape[0]
     tiles = (messages_ref.shape[1] - SUB) // 5
     row_dev = tests_ref.shape[1]
@@ -174,8 +174,30 @@
     out_ref[1:2, :] = both[:, row_dev : 2 * row_dev]
 
 
-def swap(x):
-    return lax.ppermute(x, "half", [(0, 1), (1, 0)])
+def partner_kernel(half_columns, tests_ref, messages_ref, out_ref):
+    far_sums(half_columns, True, tests_ref, messages_ref, out_ref)
+
+
+def early_kernel(half_columns, tests_ref, messages_ref, sent_ref, out_ref, send_ref):
+    send_ref[...] = sent_ref[...]
+
+    @pl.when(lax.axis_index("half") == 0)
+    def _():
+        far_sums(half_columns, False, tests_ref, messages_ref, out_ref)
+
+    @pl.when(lax.axis_index("half") != 0)
+    def _():
+        out_ref[...] = jnp.zeros_like(out_ref)
+
+
+def late_kernel(half_columns, tests_ref, messages_ref, early_ref, out_ref):
+    @pl.when(lax.axis_index("half") == 0)
+    def _():
+        out_ref[...] = early_ref[...]
+
+    @pl.when(lax.axis_index("half") != 0)
+    def _():
+        far_sums(half_columns, False, tests_ref, messages_ref, out_ref)
 
 
 def local(rows, half_columns, test_points, src_points, currents, near_blocks, near_dest, near_tile):
@@ -189,7 +211,7 @@
     hbm = pl.BlockSpec(memory_space=pltpu.HBM)
     params = pltpu.CompilerParams(vmem_limit_bytes=24 << 20)
 
-    partner_points = swap(test_points)
+    partner_points = lax.ppermute(test_points, "half", [(0, 1), (1, 0)])
     copies = pl.pallas_call(
         functools.partial(pack_kernel, half_columns, gain),
         out_shape=jax.ShapeDtypeStruct((members,) + message, jnp.float32),
@@ -209,19 +231,25 @@
     )(near_dest.reshape(-1), near_tile.reshape(-1), src_points, currents, near_blocks)
     messages = lax.all_to_all(copies, ("row", "column"), split_axis=0, concat_axis=0, tiled=True)
 
-    def far(points, other):
-        evaluations = width * members * row_dev
+    evaluations = width * members * row_dev
+    sums = jax.ShapeDtypeStruct((2, row_dev), jnp.float32)
+
+    def far(body, outs, *operands):
         return pl.pallas_call(
-            functools.partial(far_kernel, half_columns, other),
-            out_shape=jax.ShapeDtypeStruct((2, row_dev), jnp.float32),
-            in_specs=[vmem, vmem],
-            out_specs=vmem,
+            functools.partial(body, half_columns),
+            out_shape=[sums] * outs,
+            in_specs=[vmem] * len(operands),
+            out_specs=[vmem] * outs,
             compiler_params=params,
             cost_estimate=pl.CostEstimate(flops=40 * evaluations, bytes_accessed=4 << 20, transcendentals=evaluations),
-        )(points, messages)
-
-    from_partner = swap(far(partner_points, True))
-    return far(test_points, False) + from_partner
+        )(*operands)
+
+    (sent,) = far(partner_kernel, 1, partner_points, messages)
+    to_first = lax.ppermute(sent, "half", [(1, 0)])
+    early, send = far(early_kernel, 2, test_points, messages, sent)
+    to_second = lax.ppermute(send, "half", [(0, 1)])
+    (own,) = far(late_kernel, 1, test_points, messages, early)
+    return own + to_first + to_second
 
 
 def solution(mesh):

time: 24 us -> 27.6 us (1.15)
  starting transfers between devices: 11.5 us -> 14 us
  waiting for transfers between devices: 6.11 us -> 7.14 us
    ppermute x2 -> x3, starting transfers between devices: 5.24 us -> 7.73 us  [the longest x1 3.78 us: local(): to_second = lax.ppermute(send, 'half', [(0, 1)])]
    ppermute x2 -> x3, waiting for transfers between devices: 2.82 us -> 3.86 us  [the longest x1 2.6 us: local(): partner_points = lax.ppermute(test_points, 'half', [(0, 1), (1, 0)])]
    pallas_call x2 -> x3, Pallas kernels: 3.35 us -> 3.38 us  [far(): pl.pallas_call(functools.partial(body, half_columns), out_shape=[sums] *...]
  transfers between devices with their start and end apart: 3 -> 4, of which waited for: 3 -> 3; matrix products, arithmetic and copies ran while one was open for 0% -> 0% of each run, Pallas kernels for 7% -> 6%
where the time goes in v4:
time: 27.6 us; the launch traced here: 27.3 us
  starting transfers between devices  14 us (51%)
  waiting for transfers between devices  7.14 us (26%)
  Pallas kernels  5.48 us (20%)
  other arithmetic  0.57 us (2%)
    all_to_all x1, starting transfers between devices, local(): lax.all_to_all(copies, ('row', 'column'), split_axis=0, concat_axis=0, ti...  6.3 us
    ppermute x1, starting transfers between devices, local(): to_second = lax.ppermute(send, 'half', [(0, 1)])  3.78 us
    pallas_call x3, Pallas kernels, far(): pl.pallas_call(functools.partial(body, half_columns), out_shape=[sums] *...  3.38 us
    all_to_all x1, waiting for transfers between devices, local(): lax.all_to_all(copies, ('row', 'column'), split_axis=0, concat_axis=0, ti...  3.29 us
    ppermute x1, starting transfers between devices, local(): partner_points = lax.ppermute(test_points, 'half', [(0, 1), (1, 0)])  2.65 us
    ppermute x1, waiting for transfers between devices, local(): partner_points = lax.ppermute(test_points, 'half', [(0, 1), (1, 0)])  2.6 us
    pallas_call x1, Pallas kernels, local(): pl.pallas_call(functools.partial(pack_kernel, half_columns, gain), out_sh...  2.09 us
    ppermute x1, starting transfers between devices, local(): to_first = lax.ppermute(sent, 'half', [(1, 0)])  1.3 us
  transfers between devices with their start and end apart: 4, of which 3 were waited for; matrix products, arithmetic and copies ran while one was open for 0% of the time, Pallas kernels for 6%

profile of v4, /device:TPU:0, one launch (start us, length us, event | category | flops | bytes accessed | tf_op | source)
XLA Modules:
  0.0 27.3 jit_solution(10327792622897619049)
XLA Ops:
  0.0 2.1 %shard_map.64 = f32[16,48,128]{2,1,0:T(8,128)} custom-call(s32[8]{0:T(128)} %bitcast.2, s32[8]{0:T(128)} %bitcast.3, f32[3,1024]{1,0:T(4,128)} %src_hbm.1, f32[2,1024]{1,0:T(2,128)} %cur_hbm.1, f32[8,2,16,128]{3,2,1,0:T(8,128)} %blocks_hbm.1), custom_call_target="tpu_custom_call" | custom-call | flops 1048576 | bytes 1048576 | tf_op jit(solution)/shard_map/pallas_call | solution.py:215
  2.1 0.0 copy-start
  2.1 6.3 %all-to-all-start = ((f32[16,48,128]{2,1,0:T(8,128)}), f32[16,48,128]{2,1,0:T(8,128)S(1)}, u32[]{:S(2)}, u32[]{:S(2)}) async-start(f32[16,48,128]{2,1,0:T(8,128)} %shard_map.64), calls=%async_computation | async-start | bytes 786432 | tf_op jit(solution)/shard_map/all_to_all | solution.py:232
  8.4 0.0 copy-done
  8.4 2.7 %collective-permute-start = (f32[3,16]{1,0:T(4,128)S(1)}, f32[3,16]{1,0:T(4,128)S(1)}, u32[]{:S(2)}, u32[]{:S(2)}) collective-permute-start(f32[3,16]{1,0:T(4,128)S(1)} %copy-done), channel_id=1, source_target_pairs={{0,4},{4,0},{1,5},{5,1},{2,6},{6,2},{3,7},{7,3},{8,12},{12,8},{9,1... | collective-permute-start | bytes 584 | tf_op jit(solution)/shard_map/ppermute | solution.py:214
  11.1 2.6 %collective-permute-done.tests_ref = f32[3,16]{1,0:T(4,128)S(1)} collective-permute-done((f32[3,16]{1,0:T(4,128)S(1)}, f32[3,16]{1,0:T(4,128)S(1)}, u32[]{:S(2)}, u32[]{:S(2)}) %collective-permute-start) | collective-permute-done | bytes 224 | tf_op jit(solution)/shard_map/ppermute | solution.py:214
  13.7 3.3 %all-to-all-done.messages_ref = f32[16,48,128]{2,1,0:T(8,128)S(1)} async-done(((f32[16,48,128]{2,1,0:T(8,128)}), f32[16,48,128]{2,1,0:T(8,128)S(1)}, u32[]{:S(2)}, u32[]{:S(2)}) %all-to-all-start) | async-done | bytes 393248 | tf_op jit(solution)/shard_map/all_to_all | solution.py:232
  17.0 1.7 %shard_map.65.sent_ref = f32[2,16]{1,0:T(2,128)S(1)} custom-call(f32[3,16]{1,0:T(4,128)S(1)} %collective-permute-done.tests_ref, f32[16,48,128]{2,1,0:T(8,128)S(1)} %all-to-all-done.messages_ref), custom_call_target="tpu_custom_call" | custom-call | flops 10485760 | bytes 4194304 | tf_op jit(solution)/shard_map/pallas_call | solution.py:238
  18.7 1.3 %collective-permute-start.1 = (f32[2,16]{1,0:T(2,128)S(1)}, f32[2,16]{1,0:T(2,128)S(1)}, u32[]{:S(2)}, u32[]{:S(2)}) collective-permute-start(f32[2,16]{1,0:T(2,128)S(1)} %shard_map.65.sent_ref), channel_id=1, source_target_pairs={{4,0},{5,1},{6,2},{7,3},{12,8},{13,9},{14,10},{15,11},{20,16},{21,... | collective-permute-start | bytes 392 | tf_op jit(solution)/shard_map/ppermute | solution.py:248
  20.0 1.7 %shard_map.66 = (f32[2,16]{1,0:T(2,128)S(1)}, f32[2,16]{1,0:T(2,128)S(1)}) custom-call(f32[3,16]{1,0:T(4,128)S(1)} %copy-done, f32[16,48,128]{2,1,0:T(8,128)S(1)} %all-to-all-done.messages_ref, f32[2,16]{1,0:T(2,128)S(1)} %shard_map.65.sent_ref), custom_call_target="tpu_custom_call" | custom-call | flops 10485760 | bytes 4194304 | tf_op jit(solution)/shard_map/pallas_call | solution.py:238
  21.6 3.8 %collective-permute-start.2 = (f32[2,16]{1,0:T(2,128)S(1)}, f32[2,16]{1,0:T(2,128)S(1)}, u32[]{:S(2)}, u32[]{:S(2)}) collective-permute-start(f32[2,16]{1,0:T(2,128)S(1)} %get-tuple-element.8), channel_id=1, source_target_pairs={{0,4},{1,5},{2,6},{3,7},{8,12},{9,13},{10,14},{11,15},{16,20},{17,... | collective-permute-start | bytes 392 | tf_op jit(solution)/shard_map/ppermute | solution.py:250
  25.5 1.3 %collective-permute-done.2 = f32[2,16]{1,0:T(2,128)S(1)} collective-permute-done((f32[2,16]{1,0:T(2,128)S(1)}, f32[2,16]{1,0:T(2,128)S(1)}, u32[]{:S(2)}, u32[]{:S(2)}) %collective-permute-start.2) | collective-permute-done | bytes 160 | tf_op jit(solution)/shard_map/ppermute | solution.py:250
  26.7 0.0 collective-permute-done.1
  26.7 0.6 %add_add_fusion = f32[2,16]{1,0:T(2,128)} fusion(f32[2,16]{1,0:T(2,128)S(1)} %collective-permute-done.2, f32[2,16]{1,0:T(2,128)S(1)} %shard_map.67, f32[2,16]{1,0:T(2,128)S(1)} %collective-permute-done.1), kind=kLoop, calls=%fused_computation | loop fusion | flops 64 | bytes 512 | tf_op jit(solution)/shard_map/add | solution.py:252
  (1 shorter events, 0.0 us)
Async XLA Ops:
  2.1 6.3 %copy-start = (f32[3,16]{1,0:T(4,128)S(1)}, f32[3,16]{1,0:T(4,128)}, u32[]{:S(2)}) copy-start(f32[3,16]{1,0:T(4,128)} %tests_ref.3) | copy-start | bytes 580
  2.1 14.9 %all-to-all-start = ((f32[16,48,128]{2,1,0:T(8,128)}), f32[16,48,128]{2,1,0:T(8,128)S(1)}, u32[]{:S(2)}, u32[]{:S(2)}) async-start(f32[16,48,128]{2,1,0:T(8,128)} %shard_map.64), calls=%async_computation | async-start | bytes 786432 | tf_op jit(solution)/shard_map/all_to_all | solution.py:232
  8.4 5.3 %collective-permute-start = (f32[3,16]{1,0:T(4,128)S(1)}, f32[3,16]{1,0:T(4,128)S(1)}, u32[]{:S(2)}, u32[]{:S(2)}) collective-permute-start(f32[3,16]{1,0:T(4,128)S(1)} %copy-done), channel_id=1, source_target_pairs={{0,4},{4,0},{1,5},{5,1},{2,6},{6,2},{3,7},{7,3},{8,12},{12,8},{9,1... | collective-permute-start | bytes 584 | tf_op jit(solution)/shard_map/ppermute | solution.py:214
  18.7 8.1 %collective-permute-start.1 = (f32[2,16]{1,0:T(2,128)S(1)}, f32[2,16]{1,0:T(2,128)S(1)}, u32[]{:S(2)}, u32[]{:S(2)}) collective-permute-start(f32[2,16]{1,0:T(2,128)S(1)} %shard_map.65.sent_ref), channel_id=1, source_target_pairs={{4,0},{5,1},{6,2},{7,3},{12,8},{13,9},{14,10},{15,11},{20,16},{21,... | collective-permute-start | bytes 392 | tf_op jit(solution)/shard_map/ppermute | solution.py:248
  21.6 5.1 %collective-permute-start.2 = (f32[2,16]{1,0:T(2,128)S(1)}, f32[2,16]{1,0:T(2,128)S(1)}, u32[]{:S(2)}, u32[]{:S(2)}) collective-permute-start(f32[2,16]{1,0:T(2,128)S(1)} %get-tuple-element.8), channel_id=1, source_target_pairs={{0,4},{1,5},{2,6},{3,7},{8,12},{9,13},{10,14},{11,15},{16,20},{17,... | collective-permute-start | bytes 392 | tf_op jit(solution)/shard_map/ppermute | solution.py:250

commit v5 on v4

--- a/solution.py
+++ b/solution.py
@@ -76,7 +76,7 @@
                 for piece in range(row_dev // SUB):
                     spot = lane == sub + (k * row_dev + piece * SUB)
                     sums[part] = jnp.where(spot, total[piece * SUB : (piece + 1) * SUB], sums[part])
-            owner = jnp.where(lane // row_dev == k, dest_ref[block], owner)
+            owner = jnp.where(lane >= k * row_dev, dest_ref[block], owner)
         terms = [jnp.sum(x, axis=0, keepdims=True) for x in sums]
         for block in range(columns // SUB):
             place = pl.ds(block * SUB, SUB)
@@ -111,28 +111,29 @@
 
     lax.fori_loop(0, members, copy, 0, unroll=16)
 
-    base = lax.axis_index("row") * half_columns
+    base = lax.axis_index("x") * half_columns
     for k in range(half_columns):
         for half in range(2):
             spot = 5 * tiles + half
             copies_ref[base + k, spot : spot + 1, :] = near_all[0, half * half_columns + k : half * half_columns + k + 1, :]
 
 
-def far_sums(half_columns, other, tests_ref, messages_ref, out_ref):
+def wide_points(tests_ref):
+    row_dev = tests_ref.shape[1]
+    lane = lax.broadcasted_iota(jnp.int32, (row_dev, LANES), 1)
+    sub = lax.broadcasted_iota(jnp.int32, (row_dev, LANES), 0)
+    points = jnp.concatenate([tests_ref[...], jnp.zeros((3, LANES - row_dev), jnp.float32)], axis=1) * TURNS
+    columns = []
+    for c in range(3):
+        column = jnp.sum(jnp.where(lane == sub, points[c : c + 1, :], 0.0), axis=1, keepdims=True)
+        columns.append(jnp.broadcast_to(column, (row_dev, LANES)))
+    return [[column[g * SUB : (g + 1) * SUB] for column in columns] for g in range(row_dev // SUB)]
+
+
+def far_loop(tests, sums, messages_ref):
     members = messages_ref.shape[0]
     tiles = (messages_ref.shape[1] - SUB) // 5
-    row_dev = tests_ref.shape[1]
-    groups = row_dev // SUB
-    lane = lax.broadcasted_iota(jnp.int32, (row_dev, LANES), 1)
-    sub = lax.broadcasted_iota(jnp.int32, (row_dev, LANES), 0)
     soft = (SOFTENING * TURNS) ** 2
-
-    points = jnp.concatenate([tests_ref[...], jnp.zeros((3, LANES - row_dev), jnp.float32)], axis=1) * TURNS
-    tests = []
-    for c in range(3):
-        column = jnp.sum(jnp.where(lane == sub, points[c : c + 1, :], 0.0), axis=1, keepdims=True)
-        wide = jnp.broadcast_to(column, (row_dev, LANES))
-        tests.append([wide[g * SUB : (g + 1) * SUB] for g in range(groups)])
 
     def step(member, sums):
         for tile in range(tiles):
@@ -141,10 +142,10 @@
                 for c in range(5)
             ]
             new = []
-            for g, (re, im) in enumerate(sums):
-                dx = tests[0][g] - sx
-                dy = tests[1][g] - sy
-                dz = tests[2][g] - sz
+            for (tx, ty, tz), (re, im) in zip(tests, sums):
+                dx = tx - sx
+                dy = ty - sy
+                dz = tz - sz
                 square = dx * dx + dy * dy + (dz * dz + soft)
                 inverse = lax.rsqrt(square)
                 t = square * inverse - turn
@@ -158,8 +159,29 @@
             sums = tuple(new)
         return sums
 
+    return lax.fori_loop(0, members, step, tuple(sums), unroll=4 // len(tests))
+
+
+def first_kernel(partner_ref, tests_ref, messages_ref, sums_ref):
+    groups = tests_ref.shape[1] // SUB
+    tests = wide_points(partner_ref) + wide_points(tests_ref)
     zero = jnp.zeros((SUB, LANES), jnp.float32)
-    sums = lax.fori_loop(0, members, step, tuple((zero, zero) for _ in range(groups)), unroll=2)
+    for k, pair in enumerate(far_loop(tests, [(zero, zero)] * len(tests), messages_ref)):
+        for part in range(2):
+            sums_ref[k // groups, part, pl.ds(k % groups * SUB, SUB), :] = pair[part]
+
+
+def second_kernel(half_columns, other, tests_ref, sums_ref, messages_ref, sibling_ref, out_ref):
+    row_dev = tests_ref.shape[1]
+    tiles = (messages_ref.shape[1] - SUB) // 5
+    lane = lax.broadcasted_iota(jnp.int32, (row_dev, LANES), 1)
+    sub = lax.broadcasted_iota(jnp.int32, (row_dev, LANES), 0)
+    tests = wide_points(tests_ref)
+    which = 0 if other else 1
+    sums = [
+        (sums_ref[which, 0, pl.ds(g * SUB, SUB), :], sums_ref[which, 1, pl.ds(g * SUB, SUB), :]) for g in range(len(tests))
+    ]
+    sums = far_loop(tests, sums, sibling_ref)
     re, im = [
         jnp.concatenate([jnp.sum(pair[part], axis=1, keepdims=True) for pair in sums], axis=0) for part in range(2)
     ]
@@ -167,51 +189,29 @@
     both = jnp.sum(both, axis=0, keepdims=True)
     half = lax.axis_index("half")
     spot = 5 * tiles + (1 - half if other else half)
-    base = lax.axis_index("row") * half_columns
+    base = lax.axis_index("x") * half_columns
     for k in range(half_columns):
         both = both + messages_ref[base + k, pl.ds(spot, 1), :]
     out_ref[0:1, :] = both[:, :row_dev]
     out_ref[1:2, :] = both[:, row_dev : 2 * row_dev]
 
 
-def partner_kernel(half_columns, tests_ref, messages_ref, out_ref):
-    far_sums(half_columns, True, tests_ref, messages_ref, out_ref)
-
-
-def early_kernel(half_columns, tests_ref, messages_ref, sent_ref, out_ref, send_ref):
-    send_ref[...] = sent_ref[...]
-
-    @pl.when(lax.axis_index("half") == 0)
-    def _():
-        far_sums(half_columns, False, tests_ref, messages_ref, out_ref)
-
-    @pl.when(lax.axis_index("half") != 0)
-    def _():
-        out_ref[...] = jnp.zeros_like(out_ref)
-
-
-def late_kernel(half_columns, tests_ref, messages_ref, early_ref, out_ref):
-    @pl.when(lax.axis_index("half") == 0)
-    def _():
-        out_ref[...] = early_ref[...]
-
-    @pl.when(lax.axis_index("half") != 0)
-    def _():
-        far_sums(half_columns, False, tests_ref, messages_ref, out_ref)
+def swap(x, axis):
+    return lax.ppermute(x, axis, [(0, 1), (1, 0)])
 
 
 def local(rows, half_columns, test_points, src_points, currents, near_blocks, near_dest, near_tile):
     row_dev = test_points.shape[1]
     width = src_points.shape[1]
     items = near_blocks.shape[0]
-    members = rows * half_columns
-    gain = TURNS / math.sqrt(width * members * 2)
+    members = rows // 2 * half_columns
+    gain = TURNS / math.sqrt(width * members * 4)
     message = (5 * width // LANES + SUB, LANES)
     vmem = pl.BlockSpec(memory_space=pltpu.VMEM)
     hbm = pl.BlockSpec(memory_space=pltpu.HBM)
     params = pltpu.CompilerParams(vmem_limit_bytes=24 << 20)
 
-    partner_points = lax.ppermute(test_points, "half", [(0, 1), (1, 0)])
+    partner_points = swap(test_points, "half")
     copies = pl.pallas_call(
         functools.partial(pack_kernel, half_columns, gain),
         out_shape=jax.ShapeDtypeStruct((members,) + message, jnp.float32),
@@ -229,33 +229,45 @@
         ],
         cost_estimate=pl.CostEstimate(flops=1 << 20, bytes_accessed=1 << 20, transcendentals=0),
     )(near_dest.reshape(-1), near_tile.reshape(-1), src_points, currents, near_blocks)
-    messages = lax.all_to_all(copies, ("row", "column"), split_axis=0, concat_axis=0, tiled=True)
+    messages = lax.all_to_all(copies, ("x", "column"), split_axis=0, concat_axis=0, tiled=True)
+
+    sibling = swap(messages, "core")
 
     evaluations = width * members * row_dev
-    sums = jax.ShapeDtypeStruct((2, row_dev), jnp.float32)
-
-    def far(body, outs, *operands):
+
+    def cost(times):
+        return dict(
+            compiler_params=params,
+            cost_estimate=pl.CostEstimate(
+                flops=40 * evaluations * times, bytes_accessed=2 << 20, transcendentals=evaluations * times
+            ),
+        )
+
+    sums = pl.pallas_call(
+        first_kernel,
+        out_shape=jax.ShapeDtypeStruct((2, 2, row_dev, LANES), jnp.float32),
+        in_specs=[vmem] * 3,
+        out_specs=vmem,
+        **cost(2),
+    )(partner_points, test_points, messages)
+
+    def second(points, other):
         return pl.pallas_call(
-            functools.partial(body, half_columns),
-            out_shape=[sums] * outs,
-            in_specs=[vmem] * len(operands),
-            out_specs=[vmem] * outs,
-            compiler_params=params,
-            cost_estimate=pl.CostEstimate(flops=40 * evaluations, bytes_accessed=4 << 20, transcendentals=evaluations),
-        )(*operands)
-
-    (sent,) = far(partner_kernel, 1, partner_points, messages)
-    to_first = lax.ppermute(sent, "half", [(1, 0)])
-    early, send = far(early_kernel, 2, test_points, messages, sent)
-    to_second = lax.ppermute(send, "half", [(0, 1)])
-    (own,) = far(late_kernel, 1, test_points, messages, early)
-    return own + to_first + to_second
+            functools.partial(second_kernel, half_columns, other),
+            out_shape=jax.ShapeDtypeStruct((2, row_dev), jnp.float32),
+            in_specs=[vmem] * 4,
+            out_specs=vmem,
+            **cost(1),
+        )(points, sums, messages, sibling)
+
+    from_partner = swap(second(partner_points, True), "half")
+    return second(test_points, False) + from_partner
 
 
 def solution(mesh):
     rows, columns = mesh.shape["row"], mesh.shape["col"]
-    finer = jax.sharding.Mesh(mesh.devices.reshape(rows, 2, columns // 2), ("row", "half", "column"))
-    every = ("row", "half", "column")
+    finer = jax.sharding.Mesh(mesh.devices.reshape(rows // 2, 2, 2, columns // 2), ("x", "core", "half", "column"))
+    every = ("x", "core", "half", "column")
     in_specs = (
         P(None, every),
         P(None, every),

time: 27.6 us -> 27.1 us (0.982)
  blocking collectives: 0 us -> 12.8 us
  starting transfers between devices: 14 us -> 5.2 us
  waiting for transfers between devices: 7.14 us -> 2.78 us
    all_to_all x0 -> x1, blocking collectives: none -> 12.8 us  [local(): lax.all_to_all(copies, ('x', 'column'), split_axis=0, concat_axis=0, tile...]
    all_to_all x1 -> x0, starting transfers between devices: 6.3 us -> none  [local(): lax.all_to_all(copies, ('row', 'column'), split_axis=0, concat_axis=0, ti...]
    all_to_all x1 -> x0, waiting for transfers between devices: 3.29 us -> none  [local(): lax.all_to_all(copies, ('row', 'column'), split_axis=0, concat_axis=0, ti...]
    ppermute x3, starting transfers between devices: 7.73 us -> 5.2 us  [swap(): return lax.ppermute(x, axis, [(0, 1), (1, 0)])]
    ppermute x3, waiting for transfers between devices: 3.86 us -> 2.78 us  [swap(): return lax.ppermute(x, axis, [(0, 1), (1, 0)])]
  transfers between devices with their start and end apart: 4 -> 3, of which waited for: 3 -> 2; matrix products, arithmetic and copies ran while one was open for 0% -> 0% of each run, Pallas kernels for 6% -> 9%
where the time goes in v5:
time: 27.1 us; the launch traced here: 26.9 us
  blocking collectives  12.8 us (47%)
  Pallas kernels  5.47 us (20%)
  starting transfers between devices  5.2 us (19%)
  waiting for transfers between devices  2.78 us (10%)
  other arithmetic  0.56 us (2%)
    all_to_all x1, blocking collectives, local(): lax.all_to_all(copies, ('x', 'column'), split_axis=0, concat_axis=0, tile...  12.8 us
    ppermute x3, starting transfers between devices, swap(): return lax.ppermute(x, axis, [(0, 1), (1, 0)])  5.2 us
    ppermute x3, waiting for transfers between devices, swap(): return lax.ppermute(x, axis, [(0, 1), (1, 0)])  2.78 us
    pallas_call x1, Pallas kernels, local(): pl.pallas_call(functools.partial(pack_kernel, half_columns, gain), out_sh...  2.05 us
    pallas_call x2, Pallas kernels, second(): pl.pallas_call(functools.partial(second_kernel, half_columns, other), out...  1.99 us
    pallas_call x1, Pallas kernels, local(): pl.pallas_call(first_kernel, out_shape=jax.ShapeDtypeStruct((2, 2, row_de...  1.44 us
    add x1, other arithmetic, local(): return second(test_points, False) + from_partner  0.56 us
  transfers between devices with their start and end apart: 3, of which 2 were waited for; matrix products, arithmetic and copies ran while one was open for 0% of the time, Pallas kernels for 9%

profile of v5, /device:TPU:0, one launch (start us, length us, event | category | flops | bytes accessed | tf_op | source)
XLA Modules:
  0.0 26.9 jit_solution(1457189703286573676)
XLA Ops:
  0.0 2.0 %shard_map.64 = f32[8,48,128]{2,1,0:T(8,128)} custom-call(s32[8]{0:T(128)} %bitcast.2, s32[8]{0:T(128)} %bitcast.3, f32[3,1024]{1,0:T(4,128)} %src_hbm.1, f32[2,1024]{1,0:T(2,128)} %cur_hbm.1, f32[8,2,16,128]{3,2,1,0:T(8,128)} %blocks_hbm.1), custom_call_target="tpu_custom_call" | custom-call | flops 1048576 | bytes 1048576 | tf_op jit(solution)/shard_map/pallas_call | solution.py:215
  2.1 0.0 copy-start
  2.1 12.8 %all_to_all.5.messages_ref = f32[8,48,128]{2,1,0:T(8,128)S(1)} all-to-all(f32[8,48,128]{2,1,0:T(8,128)} %shard_map.64), channel_id=1, replica_groups=mesh['x'=2,'core'=2,'half'=2,'column'=4] {'x','column'}, dimensions={0} | all-to-all | bytes 393216 | tf_op jit(solution)/shard_map/all_to_all | solution.py:232
  14.9 0.0 collective-permute-start.1
  14.9 0.0 copy-done
  14.9 2.6 %collective-permute-start = (f32[3,16]{1,0:T(4,128)S(1)}, f32[3,16]{1,0:T(4,128)S(1)}, u32[]{:S(2)}, u32[]{:S(2)}) collective-permute-start(f32[3,16]{1,0:T(4,128)S(1)} %copy-done), channel_id=1, source_target_pairs={{0,4},{4,0},{1,5},{5,1},{2,6},{6,2},{3,7},{7,3},{8,12},{12,8},{9,1... | collective-permute-start | bytes 584 | tf_op jit(solution)/shard_map/ppermute | solution.py:200
  17.5 1.9 %collective-permute-done.partner_ref.tests_ref = f32[3,16]{1,0:T(4,128)S(1)} collective-permute-done((f32[3,16]{1,0:T(4,128)S(1)}, f32[3,16]{1,0:T(4,128)S(1)}, u32[]{:S(2)}, u32[]{:S(2)}) %collective-permute-start) | collective-permute-done | bytes 224 | tf_op jit(solution)/shard_map/ppermute | solution.py:200
  19.4 1.4 %shard_map.65.sums_ref = f32[2,2,16,128]{3,2,1,0:T(8,128)S(1)} custom-call(f32[3,16]{1,0:T(4,128)S(1)} %collective-permute-done.partner_ref.tests_ref, f32[3,16]{1,0:T(4,128)S(1)} %copy-done, f32[8,48,128]{2,1,0:T(8,128)S(1)} %all_to_all.5.messages_ref), custom_call_target="tpu_custom_call" | custom-call | flops 10485760 | bytes 2097152 | tf_op jit(solution)/shard_map/pallas_call | solution.py:246
  20.8 0.0 collective-permute-done.1.sibling_ref
  20.8 1.0 %shard_map.67 = f32[2,16]{1,0:T(2,128)S(1)} custom-call(f32[3,16]{1,0:T(4,128)S(1)} %collective-permute-done.partner_ref.tests_ref, f32[2,2,16,128]{3,2,1,0:T(8,128)S(1)} %shard_map.65.sums_ref, f32[8,48,128]{2,1,0:T(8,128)S(1)} %all_to_all.5.messages_ref, f32[8,48,128]{2,1,0:T(8,128)S(1)} %collective-permute-done.1.sibling_ref), custom_call_target="tpu_custom_call" | custom-call | flops 5242880 | bytes 2097152 | tf_op jit(solution)/shard_map/pallas_call | solution.py:255
  21.8 2.6 %collective-permute-start.2 = (f32[2,16]{1,0:T(2,128)S(1)}, f32[2,16]{1,0:T(2,128)S(1)}, u32[]{:S(2)}, u32[]{:S(2)}) collective-permute-start(f32[2,16]{1,0:T(2,128)S(1)} %shard_map.67), channel_id=1, source_target_pairs={{0,4},{4,0},{1,5},{5,1},{2,6},{6,2},{3,7},{7,3},{8,12},{12,8},{9,1... | collective-permute-start | bytes 392 | tf_op jit(solution)/shard_map/ppermute | solution.py:200
  24.4 1.0 %shard_map.66 = f32[2,16]{1,0:T(2,128)S(1)} custom-call(f32[3,16]{1,0:T(4,128)S(1)} %copy-done, f32[2,2,16,128]{3,2,1,0:T(8,128)S(1)} %shard_map.65.sums_ref, f32[8,48,128]{2,1,0:T(8,128)S(1)} %all_to_all.5.messages_ref, f32[8,48,128]{2,1,0:T(8,128)S(1)} %collective-permute-done.1.sibling_ref), custom_call_target="tpu_custom_call" | custom-call | flops 5242880 | bytes 2097152 | tf_op jit(solution)/shard_map/pallas_call | solution.py:255
  25.4 0.9 %collective-permute-done.2 = f32[2,16]{1,0:T(2,128)S(1)} collective-permute-done((f32[2,16]{1,0:T(2,128)S(1)}, f32[2,16]{1,0:T(2,128)S(1)}, u32[]{:S(2)}, u32[]{:S(2)}) %collective-permute-start.2) | collective-permute-done | bytes 160 | tf_op jit(solution)/shard_map/ppermute | solution.py:200
  26.3 0.6 %add.3 = f32[2,16]{1,0:T(2,128)} add(f32[2,16]{1,0:T(2,128)S(1)} %shard_map.66, f32[2,16]{1,0:T(2,128)S(1)} %collective-permute-done.2) | non-fusion elementwise | flops 32 | bytes 384 | tf_op jit(solution)/shard_map/add | solution.py:264
Async XLA Ops:
  2.1 12.8 %copy-start = (f32[3,16]{1,0:T(4,128)S(1)}, f32[3,16]{1,0:T(4,128)}, u32[]{:S(2)}) copy-start(f32[3,16]{1,0:T(4,128)} %tests_ref.3) | copy-start | bytes 580
  14.9 5.9 %collective-permute-start.1 = (f32[8,48,128]{2,1,0:T(8,128)S(1)}, f32[8,48,128]{2,1,0:T(8,128)S(1)}, u32[]{:S(2)}, u32[]{:S(2)}) collective-permute-start(f32[8,48,128]{2,1,0:T(8,128)S(1)} %all_to_all.5.messages_ref), channel_id=1, source_target_pairs={{0,8},{8,0},{1,9},{9,1},{2,10},{10,2},{3,11},{11,3},{4,12},{12,4},... | collective-permute-start | bytes 589832 | tf_op jit(solution)/shard_map/ppermute | solution.py:200
  14.9 4.5 %collective-permute-start = (f32[3,16]{1,0:T(4,128)S(1)}, f32[3,16]{1,0:T(4,128)S(1)}, u32[]{:S(2)}, u32[]{:S(2)}) collective-permute-start(f32[3,16]{1,0:T(4,128)S(1)} %copy-done), channel_id=1, source_target_pairs={{0,4},{4,0},{1,5},{5,1},{2,6},{6,2},{3,7},{7,3},{8,12},{12,8},{9,1... | collective-permute-start | bytes 584 | tf_op jit(solution)/shard_map/ppermute | solution.py:200
  21.8 4.5 %collective-permute-start.2 = (f32[2,16]{1,0:T(2,128)S(1)}, f32[2,16]{1,0:T(2,128)S(1)}, u32[]{:S(2)}, u32[]{:S(2)}) collective-permute-start(f32[2,16]{1,0:T(2,128)S(1)} %shard_map.67), channel_id=1, source_target_pairs={{0,4},{4,0},{1,5},{5,1},{2,6},{6,2},{3,7},{7,3},{8,12},{12,8},{9,1... | collective-permute-start | bytes 392 | tf_op jit(solution)/shard_map/ppermute | solution.py:200

commit v6 on v5

--- a/solution.py
+++ b/solution.py
@@ -118,16 +118,19 @@
             copies_ref[base + k, spot : spot + 1, :] = near_all[0, half * half_columns + k : half * half_columns + k + 1, :]
 
 
-def wide_points(tests_ref):
+def points_kernel(partner_ref, tests_ref, wide_ref):
     row_dev = tests_ref.shape[1]
     lane = lax.broadcasted_iota(jnp.int32, (row_dev, LANES), 1)
     sub = lax.broadcasted_iota(jnp.int32, (row_dev, LANES), 0)
-    points = jnp.concatenate([tests_ref[...], jnp.zeros((3, LANES - row_dev), jnp.float32)], axis=1) * TURNS
-    columns = []
-    for c in range(3):
-        column = jnp.sum(jnp.where(lane == sub, points[c : c + 1, :], 0.0), axis=1, keepdims=True)
-        columns.append(jnp.broadcast_to(column, (row_dev, LANES)))
-    return [[column[g * SUB : (g + 1) * SUB] for column in columns] for g in range(row_dev // SUB)]
+    for which, ref in enumerate((partner_ref, tests_ref)):
+        points = jnp.concatenate([ref[...], jnp.zeros((3, LANES - row_dev), jnp.float32)], axis=1) * TURNS
+        for c in range(3):
+            column = jnp.sum(jnp.where(lane == sub, points[c : c + 1, :], 0.0), axis=1, keepdims=True)
+            wide_ref[which, c] = jnp.broadcast_to(column, (row_dev, LANES))
+
+
+def groups_of(wide_ref, which):
+    return [[wide_ref[which, c, pl.ds(g * SUB, SUB), :] for c in range(3)] for g in range(wide_ref.shape[2] // SUB)]
 
 
 def far_loop(tests, sums, messages_ref):
@@ -162,22 +165,22 @@
     return lax.fori_loop(0, members, step, tuple(sums), unroll=4 // len(tests))
 
 
-def first_kernel(partner_ref, tests_ref, messages_ref, sums_ref):
-    groups = tests_ref.shape[1] // SUB
-    tests = wide_points(partner_ref) + wide_points(tests_ref)
+def first_kernel(wide_ref, messages_ref, sums_ref):
+    groups = wide_ref.shape[2] // SUB
+    tests = groups_of(wide_ref, 0) + groups_of(wide_ref, 1)
     zero = jnp.zeros((SUB, LANES), jnp.float32)
     for k, pair in enumerate(far_loop(tests, [(zero, zero)] * len(tests), messages_ref)):
         for part in range(2):
             sums_ref[k // groups, part, pl.ds(k % groups * SUB, SUB), :] = pair[part]
 
 
-def second_kernel(half_columns, other, tests_ref, sums_ref, messages_ref, sibling_ref, out_ref):
-    row_dev = tests_ref.shape[1]
+def second_kernel(half_columns, other, wide_ref, sums_ref, messages_ref, sibling_ref, out_ref):
+    row_dev = wide_ref.shape[2]
     tiles = (messages_ref.shape[1] - SUB) // 5
     lane = lax.broadcasted_iota(jnp.int32, (row_dev, LANES), 1)
     sub = lax.broadcasted_iota(jnp.int32, (row_dev, LANES), 0)
-    tests = wide_points(tests_ref)
     which = 0 if other else 1
+    tests = groups_of(wide_ref, which)
     sums = [
         (sums_ref[which, 0, pl.ds(g * SUB, SUB), :], sums_ref[which, 1, pl.ds(g * SUB, SUB), :]) for g in range(len(tests))
     ]
@@ -243,25 +246,33 @@
             ),
         )
 
+    wide = pl.pallas_call(
+        points_kernel,
+        out_shape=jax.ShapeDtypeStruct((2, 3, row_dev, LANES), jnp.float32),
+        in_specs=[vmem] * 2,
+        out_specs=vmem,
+        **cost(1),
+    )(partner_points, test_points)
+
     sums = pl.pallas_call(
         first_kernel,
         out_shape=jax.ShapeDtypeStruct((2, 2, row_dev, LANES), jnp.float32),
-        in_specs=[vmem] * 3,
+        in_specs=[vmem] * 2,
         out_specs=vmem,
         **cost(2),
-    )(partner_points, test_points, messages)
-
-    def second(points, other):
+    )(wide, messages)
+
+    def second(other):
         return pl.pallas_call(
             functools.partial(second_kernel, half_columns, other),
             out_shape=jax.ShapeDtypeStruct((2, row_dev), jnp.float32),
             in_specs=[vmem] * 4,
             out_specs=vmem,
             **cost(1),
-        )(points, sums, messages, sibling)
-
-    from_partner = swap(second(partner_points, True), "half")
-    return second(test_points, False) + from_partner
+        )(wide, sums, messages, sibling)
+
+    from_partner = swap(second(True), "half")
+    return second(False) + from_partner
 
 
 def solution(mesh):

time: 27.1 us -> 27.1 us (level)
  no operation moved by 1% of the time
where the time goes in v6:
time: 27.1 us; the launch traced here: 26.8 us
  blocking collectives  12.8 us (47%)
  Pallas kernels  5.32 us (20%)
  starting transfers between devices  5.2 us (19%)
  waiting for transfers between devices  2.86 us (11%)
  other arithmetic  0.56 us (2%)
    all_to_all x1, blocking collectives, local(): lax.all_to_all(copies, ('x', 'column'), split_axis=0, concat_axis=0, tile...  12.8 us
    ppermute x3, starting transfers between devices, swap(): return lax.ppermute(x, axis, [(0, 1), (1, 0)])  5.2 us
    ppermute x3, waiting for transfers between devices, swap(): return lax.ppermute(x, axis, [(0, 1), (1, 0)])  2.86 us
    pallas_call x1, Pallas kernels, local(): pl.pallas_call(functools.partial(pack_kernel, half_columns, gain), out_sh...  2.05 us
    pallas_call x2, Pallas kernels, second(): pl.pallas_call(functools.partial(second_kernel, half_columns, other), out...  1.83 us
    pallas_call x1, Pallas kernels, local(): pl.pallas_call(first_kernel, out_shape=jax.ShapeDtypeStruct((2, 2, row_de...  1.36 us
    add x1, other arithmetic, local(): return second(False) + from_partner  0.56 us
  transfers between devices with their start and end apart: 3, of which 2 were waited for; matrix products, arithmetic and copies ran while one was open for 0% of the time, Pallas kernels for 9%

profile of v6, /device:TPU:0, one launch (start us, length us, event | category | flops | bytes accessed | tf_op | source)
XLA Modules:
  0.0 26.8 jit_solution(11677368020649514171)
XLA Ops:
  0.0 2.0 %shard_map.65 = f32[8,48,128]{2,1,0:T(8,128)} custom-call(s32[8]{0:T(128)} %bitcast.2, s32[8]{0:T(128)} %bitcast.3, f32[3,1024]{1,0:T(4,128)} %src_hbm.1, f32[2,1024]{1,0:T(2,128)} %cur_hbm.1, f32[8,2,16,128]{3,2,1,0:T(8,128)} %blocks_hbm.1), custom_call_target="tpu_custom_call" | custom-call | flops 1048576 | bytes 1048576 | tf_op jit(solution)/shard_map/pallas_call | solution.py:218
  2.1 0.0 copy-start
  2.1 12.8 %all_to_all.5.messages_ref = f32[8,48,128]{2,1,0:T(8,128)S(1)} all-to-all(f32[8,48,128]{2,1,0:T(8,128)} %shard_map.65), channel_id=1, replica_groups=mesh['x'=2,'core'=2,'half'=2,'column'=4] {'x','column'}, dimensions={0} | all-to-all | bytes 393216 | tf_op jit(solution)/shard_map/all_to_all | solution.py:235
  14.9 0.0 collective-permute-start.1
  14.9 0.0 copy-done
  14.9 2.6 %collective-permute-start = (f32[3,16]{1,0:T(4,128)S(1)}, f32[3,16]{1,0:T(4,128)S(1)}, u32[]{:S(2)}, u32[]{:S(2)}) collective-permute-start(f32[3,16]{1,0:T(4,128)S(1)} %copy-done), channel_id=1, source_target_pairs={{0,4},{4,0},{1,5},{5,1},{2,6},{6,2},{3,7},{7,3},{8,12},{12,8},{9,1... | collective-permute-start | bytes 584 | tf_op jit(solution)/shard_map/ppermute | solution.py:203
  17.5 1.9 %collective-permute-done.partner_ref = f32[3,16]{1,0:T(4,128)S(1)} collective-permute-done((f32[3,16]{1,0:T(4,128)S(1)}, f32[3,16]{1,0:T(4,128)S(1)}, u32[]{:S(2)}, u32[]{:S(2)}) %collective-permute-start) | collective-permute-done | bytes 224 | tf_op jit(solution)/shard_map/ppermute | solution.py:203
  19.4 0.1 shard_map.64.wide_ref
  19.5 1.4 %shard_map.66.sums_ref = f32[2,2,16,128]{3,2,1,0:T(8,128)S(1)} custom-call(f32[2,3,16,128]{3,2,1,0:T(8,128)S(1)} %shard_map.64.wide_ref, f32[8,48,128]{2,1,0:T(8,128)S(1)} %all_to_all.5.messages_ref), custom_call_target="tpu_custom_call" | custom-call | flops 10485760 | bytes 2097152 | tf_op jit(solution)/shard_map/pallas_call | solution.py:257
  20.8 0.0 collective-permute-done.1.sibling_ref
  20.8 0.9 %shard_map.68 = f32[2,16]{1,0:T(2,128)S(1)} custom-call(f32[2,3,16,128]{3,2,1,0:T(8,128)S(1)} %shard_map.64.wide_ref, f32[2,2,16,128]{3,2,1,0:T(8,128)S(1)} %shard_map.66.sums_ref, f32[8,48,128]{2,1,0:T(8,128)S(1)} %all_to_all.5.messages_ref, f32[8,48,128]{2,1,0:T(8,128)S(1)} %collective-permute-done.1.sibling_ref), custom_call_target="tpu_custom_call" | custom-call | flops 5242880 | bytes 2097152 | tf_op jit(solution)/shard_map/pallas_call | solution.py:266
  21.8 2.6 %collective-permute-start.2 = (f32[2,16]{1,0:T(2,128)S(1)}, f32[2,16]{1,0:T(2,128)S(1)}, u32[]{:S(2)}, u32[]{:S(2)}) collective-permute-start(f32[2,16]{1,0:T(2,128)S(1)} %shard_map.68), channel_id=1, source_target_pairs={{0,4},{4,0},{1,5},{5,1},{2,6},{6,2},{3,7},{7,3},{8,12},{12,8},{9,1... | collective-permute-start | bytes 392 | tf_op jit(solution)/shard_map/ppermute | solution.py:203
  24.4 0.9 %shard_map.67 = f32[2,16]{1,0:T(2,128)S(1)} custom-call(f32[2,3,16,128]{3,2,1,0:T(8,128)S(1)} %shard_map.64.wide_ref, f32[2,2,16,128]{3,2,1,0:T(8,128)S(1)} %shard_map.66.sums_ref, f32[8,48,128]{2,1,0:T(8,128)S(1)} %all_to_all.5.messages_ref, f32[8,48,128]{2,1,0:T(8,128)S(1)} %collective-permute-done.1.sibling_ref), custom_call_target="tpu_custom_call" | custom-call | flops 5242880 | bytes 2097152 | tf_op jit(solution)/shard_map/pallas_call | solution.py:266
  25.3 1.0 %collective-permute-done.2 = f32[2,16]{1,0:T(2,128)S(1)} collective-permute-done((f32[2,16]{1,0:T(2,128)S(1)}, f32[2,16]{1,0:T(2,128)S(1)}, u32[]{:S(2)}, u32[]{:S(2)}) %collective-permute-start.2) | collective-permute-done | bytes 160 | tf_op jit(solution)/shard_map/ppermute | solution.py:203
  26.2 0.6 %add.3 = f32[2,16]{1,0:T(2,128)} add(f32[2,16]{1,0:T(2,128)S(1)} %shard_map.67, f32[2,16]{1,0:T(2,128)S(1)} %collective-permute-done.2) | non-fusion elementwise | flops 32 | bytes 384 | tf_op jit(solution)/shard_map/add | solution.py:275
Async XLA Ops:
  2.1 12.8 %copy-start = (f32[3,16]{1,0:T(4,128)S(1)}, f32[3,16]{1,0:T(4,128)}, u32[]{:S(2)}) copy-start(f32[3,16]{1,0:T(4,128)} %tests_ref.1) | copy-start | bytes 580
  14.9 5.9 %collective-permute-start.1 = (f32[8,48,128]{2,1,0:T(8,128)S(1)}, f32[8,48,128]{2,1,0:T(8,128)S(1)}, u32[]{:S(2)}, u32[]{:S(2)}) collective-permute-start(f32[8,48,128]{2,1,0:T(8,128)S(1)} %all_to_all.5.messages_ref), channel_id=1, source_target_pairs={{0,8},{8,0},{1,9},{9,1},{2,10},{10,2},{3,11},{11,3},{4,12},{12,4},... | collective-permute-start | bytes 589832 | tf_op jit(solution)/shard_map/ppermute | solution.py:203
  14.9 4.5 %collective-permute-start = (f32[3,16]{1,0:T(4,128)S(1)}, f32[3,16]{1,0:T(4,128)S(1)}, u32[]{:S(2)}, u32[]{:S(2)}) collective-permute-start(f32[3,16]{1,0:T(4,128)S(1)} %copy-done), channel_id=1, source_target_pairs={{0,4},{4,0},{1,5},{5,1},{2,6},{6,2},{3,7},{7,3},{8,12},{12,8},{9,1... | collective-permute-start | bytes 584 | tf_op jit(solution)/shard_map/ppermute | solution.py:203
  21.8 4.5 %collective-permute-start.2 = (f32[2,16]{1,0:T(2,128)S(1)}, f32[2,16]{1,0:T(2,128)S(1)}, u32[]{:S(2)}, u32[]{:S(2)}) collective-permute-start(f32[2,16]{1,0:T(2,128)S(1)} %shard_map.68), channel_id=1, source_target_pairs={{0,4},{4,0},{1,5},{5,1},{2,6},{6,2},{3,7},{7,3},{8,12},{12,8},{9,1... | collective-permute-start | bytes 392 | tf_op jit(solution)/shard_map/ppermute | solution.py:203

commit v7 on v6

--- a/solution.py
+++ b/solution.py
@@ -234,7 +234,6 @@
     )(near_dest.reshape(-1), near_tile.reshape(-1), src_points, currents, near_blocks)
     messages = lax.all_to_all(copies, ("x", "column"), split_axis=0, concat_axis=0, tiled=True)
 
-    sibling = swap(messages, "core")
 
     evaluations = width * members * row_dev
 
@@ -254,6 +253,8 @@
         **cost(1),
     )(partner_points, test_points)
 
+    messages, wide = lax.optimization_barrier((messages, wide))
+    sibling = swap(messages, "core")
     sums = pl.pallas_call(
         first_kernel,
         out_shape=jax.ShapeDtypeStruct((2, 2, row_dev, LANES), jnp.float32),

time: 27.1 us -> 22.6 us (0.83)
  blocking collectives: 12.8 us -> 0 us
  starting transfers between devices: 5.2 us -> 11.5 us
  waiting for transfers between devices: 2.86 us -> 4.92 us
    all_to_all x1 -> x0, blocking collectives: 12.8 us -> none  [local(): lax.all_to_all(copies, ('x', 'column'), split_axis=0, concat_axis=0, tile...]
    all_to_all x0 -> x1, starting transfers between devices: none -> 6.2 us  [local(): lax.all_to_all(copies, ('x', 'column'), split_axis=0, concat_axis=0, tile...]
    all_to_all x0 -> x1, waiting for transfers between devices: none -> 1.88 us  [local(): lax.all_to_all(copies, ('x', 'column'), split_axis=0, concat_axis=0, tile...]
  transfers between devices with their start and end apart: 3 -> 4, of which waited for: 2 -> 4; matrix products, arithmetic and copies ran while one was open for 0% -> 0% of each run, Pallas kernels for 9% -> 11%
where the time goes in v7:
time: 22.6 us; the launch traced here: 22.3 us
  starting transfers between devices  11.5 us (51%)
  Pallas kernels  5.31 us (23%)
  waiting for transfers between devices  4.92 us (22%)
  other arithmetic  0.56 us (2%)
    all_to_all x1, starting transfers between devices, local(): lax.all_to_all(copies, ('x', 'column'), split_axis=0, concat_axis=0, tile...  6.2 us
    ppermute x3, starting transfers between devices, swap(): return lax.ppermute(x, axis, [(0, 1), (1, 0)])  5.26 us
    ppermute x3, waiting for transfers between devices, swap(): return lax.ppermute(x, axis, [(0, 1), (1, 0)])  3.04 us
    pallas_call x1, Pallas kernels, local(): pl.pallas_call(functools.partial(pack_kernel, half_columns, gain), out_sh...  2.04 us
    all_to_all x1, waiting for transfers between devices, local(): lax.all_to_all(copies, ('x', 'column'), split_axis=0, concat_axis=0, tile...  1.88 us
    pallas_call x2, Pallas kernels, second(): pl.pallas_call(functools.partial(second_kernel, half_columns, other), out...  1.82 us
    pallas_call x1, Pallas kernels, local(): pl.pallas_call(first_kernel, out_shape=jax.ShapeDtypeStruct((2, 2, row_de...  1.36 us
    add x1, other arithmetic, local(): return second(False) + from_partner  0.56 us
  transfers between devices with their start and end apart: 4, of which 4 were waited for; matrix products, arithmetic and copies ran while one was open for 0% of the time, Pallas kernels for 11%

profile of v7, /device:TPU:0, one launch (start us, length us, event | category | flops | bytes accessed | tf_op | source)
XLA Modules:
  0.0 22.3 jit_solution(6497695202333161622)
XLA Ops:
  0.0 2.0 %shard_map.64 = f32[8,48,128]{2,1,0:T(8,128)} custom-call(s32[8]{0:T(128)} %bitcast.2, s32[8]{0:T(128)} %bitcast.3, f32[3,1024]{1,0:T(4,128)} %src_hbm.1, f32[2,1024]{1,0:T(2,128)} %cur_hbm.1, f32[8,2,16,128]{3,2,1,0:T(8,128)} %blocks_hbm.1), custom_call_target="tpu_custom_call" | custom-call | flops 1048576 | bytes 1048576 | tf_op jit(solution)/shard_map/pallas_call | solution.py:218
  2.1 0.0 copy-start
  2.1 6.2 %all-to-all-start = ((f32[8,48,128]{2,1,0:T(8,128)}), f32[8,48,128]{2,1,0:T(8,128)S(1)}, u32[]{:S(2)}, u32[]{:S(2)}) async-start(f32[8,48,128]{2,1,0:T(8,128)} %shard_map.64), calls=%async_computation | async-start | bytes 393216 | tf_op jit(solution)/shard_map/all_to_all | solution.py:235
  8.3 0.0 copy-done
  8.3 2.7 %collective-permute-start = (f32[3,16]{1,0:T(4,128)S(1)}, f32[3,16]{1,0:T(4,128)S(1)}, u32[]{:S(2)}, u32[]{:S(2)}) collective-permute-start(f32[3,16]{1,0:T(4,128)S(1)} %copy-done), channel_id=1, source_target_pairs={{0,4},{4,0},{1,5},{5,1},{2,6},{6,2},{3,7},{7,3},{8,12},{12,8},{9,1... | collective-permute-start | bytes 584 | tf_op jit(solution)/shard_map/ppermute | solution.py:203
  10.9 2.0 %collective-permute-done.partner_ref = f32[3,16]{1,0:T(4,128)S(1)} collective-permute-done((f32[3,16]{1,0:T(4,128)S(1)}, f32[3,16]{1,0:T(4,128)S(1)}, u32[]{:S(2)}, u32[]{:S(2)}) %collective-permute-start) | collective-permute-done | bytes 224 | tf_op jit(solution)/shard_map/ppermute | solution.py:203
  12.9 0.1 shard_map.65.wide_ref
  13.0 1.9 %all-to-all-done.messages_ref = f32[8,48,128]{2,1,0:T(8,128)S(1)} async-done(((f32[8,48,128]{2,1,0:T(8,128)}), f32[8,48,128]{2,1,0:T(8,128)S(1)}, u32[]{:S(2)}, u32[]{:S(2)}) %all-to-all-start) | async-done | bytes 196640 | tf_op jit(solution)/shard_map/all_to_all | solution.py:235
  14.9 0.0 collective-permute-start.1
  14.9 1.4 %shard_map.66.sums_ref = f32[2,2,16,128]{3,2,1,0:T(8,128)S(1)} custom-call(f32[2,3,16,128]{3,2,1,0:T(8,128)S(1)} %shard_map.65.wide_ref, f32[8,48,128]{2,1,0:T(8,128)S(1)} %all-to-all-done.messages_ref), custom_call_target="tpu_custom_call" | custom-call | flops 10485760 | bytes 2097152 | tf_op jit(solution)/shard_map/pallas_call | solution.py:258
  16.2 0.1 collective-permute-done.1.sibling_ref
  16.3 0.9 %shard_map.68 = f32[2,16]{1,0:T(2,128)S(1)} custom-call(f32[2,3,16,128]{3,2,1,0:T(8,128)S(1)} %shard_map.65.wide_ref, f32[2,2,16,128]{3,2,1,0:T(8,128)S(1)} %shard_map.66.sums_ref, f32[8,48,128]{2,1,0:T(8,128)S(1)} %all-to-all-done.messages_ref, f32[8,48,128]{2,1,0:T(8,128)S(1)} %collective-permute-done.1.sibling_ref), custom_call_target="tpu_custom_call" | custom-call | flops 5242880 | bytes 2097152 | tf_op jit(solution)/shard_map/pallas_call | solution.py:267
  17.2 2.6 %collective-permute-start.2 = (f32[2,16]{1,0:T(2,128)S(1)}, f32[2,16]{1,0:T(2,128)S(1)}, u32[]{:S(2)}, u32[]{:S(2)}) collective-permute-start(f32[2,16]{1,0:T(2,128)S(1)} %shard_map.68), channel_id=1, source_target_pairs={{0,4},{4,0},{1,5},{5,1},{2,6},{6,2},{3,7},{7,3},{8,12},{12,8},{9,1... | collective-permute-start | bytes 392 | tf_op jit(solution)/shard_map/ppermute | solution.py:203
  19.8 0.9 %shard_map.67 = f32[2,16]{1,0:T(2,128)S(1)} custom-call(f32[2,3,16,128]{3,2,1,0:T(8,128)S(1)} %shard_map.65.wide_ref, f32[2,2,16,128]{3,2,1,0:T(8,128)S(1)} %shard_map.66.sums_ref, f32[8,48,128]{2,1,0:T(8,128)S(1)} %all-to-all-done.messages_ref, f32[8,48,128]{2,1,0:T(8,128)S(1)} %collective-permute-done.1.sibling_ref), custom_call_target="tpu_custom_call" | custom-call | flops 5242880 | bytes 2097152 | tf_op jit(solution)/shard_map/pallas_call | solution.py:267
  20.8 1.0 %collective-permute-done.2 = f32[2,16]{1,0:T(2,128)S(1)} collective-permute-done((f32[2,16]{1,0:T(2,128)S(1)}, f32[2,16]{1,0:T(2,128)S(1)}, u32[]{:S(2)}, u32[]{:S(2)}) %collective-permute-start.2) | collective-permute-done | bytes 160 | tf_op jit(solution)/shard_map/ppermute | solution.py:203
  21.7 0.6 %add.3 = f32[2,16]{1,0:T(2,128)} add(f32[2,16]{1,0:T(2,128)S(1)} %shard_map.67, f32[2,16]{1,0:T(2,128)S(1)} %collective-permute-done.2) | non-fusion elementwise | flops 32 | bytes 384 | tf_op jit(solution)/shard_map/add | solution.py:276
Async XLA Ops:
  2.1 6.2 %copy-start = (f32[3,16]{1,0:T(4,128)S(1)}, f32[3,16]{1,0:T(4,128)}, u32[]{:S(2)}) copy-start(f32[3,16]{1,0:T(4,128)} %tests_ref.1) | copy-start | bytes 580
  2.1 12.8 %all-to-all-start = ((f32[8,48,128]{2,1,0:T(8,128)}), f32[8,48,128]{2,1,0:T(8,128)S(1)}, u32[]{:S(2)}, u32[]{:S(2)}) async-start(f32[8,48,128]{2,1,0:T(8,128)} %shard_map.64), calls=%async_computation | async-start | bytes 393216 | tf_op jit(solution)/shard_map/all_to_all | solution.py:235
  8.3 4.6 %collective-permute-start = (f32[3,16]{1,0:T(4,128)S(1)}, f32[3,16]{1,0:T(4,128)S(1)}, u32[]{:S(2)}, u32[]{:S(2)}) collective-permute-start(f32[3,16]{1,0:T(4,128)S(1)} %copy-done), channel_id=1, source_target_pairs={{0,4},{4,0},{1,5},{5,1},{2,6},{6,2},{3,7},{7,3},{8,12},{12,8},{9,1... | collective-permute-start | bytes 584 | tf_op jit(solution)/shard_map/ppermute | solution.py:203
  14.9 1.4 %collective-permute-start.1 = (f32[8,48,128]{2,1,0:T(8,128)S(1)}, f32[8,48,128]{2,1,0:T(8,128)S(1)}, u32[]{:S(2)}, u32[]{:S(2)}) collective-permute-start(f32[8,48,128]{2,1,0:T(8,128)S(1)} %all-to-all-done.messages_ref), channel_id=1, source_target_pairs={{0,8},{8,0},{1,9},{9,1},{2,10},{10,2},{3,11},{11,3},{4,12},{12,4},... | collective-permute-start | bytes 589832 | tf_op jit(solution)/shard_map/ppermute | solution.py:203
  17.2 4.5 %collective-permute-start.2 = (f32[2,16]{1,0:T(2,128)S(1)}, f32[2,16]{1,0:T(2,128)S(1)}, u32[]{:S(2)}, u32[]{:S(2)}) collective-permute-start(f32[2,16]{1,0:T(2,128)S(1)} %shard_map.68), channel_id=1, source_target_pairs={{0,4},{4,0},{1,5},{5,1},{2,6},{6,2},{3,7},{7,3},{8,12},{12,8},{9,1... | collective-permute-start | bytes 392 | tf_op jit(solution)/shard_map/ppermute | solution.py:203

commit v8 on v7

v8 whole, which is shorter than its diff:
```python
import functools
import math

import jax
import jax.numpy as jnp
import numpy as np
from jax import lax
from jax.experimental import pallas as pl
from jax.experimental.pallas import tpu as pltpu
from jax.sharding import PartitionSpec as P

WAVENUMBER = 40.0
SOFTENING = 0.01
TURNS = WAVENUMBER / (2.0 * math.pi)
LANES = 128
SUB = 8


def even_fit(function, terms, reach):
    nodes = np.cos((np.arange(400) + 0.5) * np.pi / 400)
    squares = (nodes + 1) * 0.5 * reach * reach
    fit = np.polynomial.chebyshev.Chebyshev.fit(squares, function(np.sqrt(squares)), terms - 1)
    return [float(value) for value in fit.convert(kind=np.polynomial.Polynomial).coef]


ROOT2 = math.sqrt(2.0)
SINE = even_fit(lambda u: ROOT2 * math.pi * np.sinc(u), 4, 0.5)
COSINE = even_fit(lambda u: -ROOT2 * np.cos(np.pi * u), 5, 0.5)
ANGLE = even_fit(lambda r: np.arctan(r) / (2 * np.pi * r), 9, 1.0)
ROUNDER = 1.5 * 2.0**23


def horner(coefficients, x):
    total = coefficients[-1] * x + coefficients[-2]
    for value in coefficients[-3::-1]:
        total = total * x + value
    return total


def phase_of(re, im):
    wide = jnp.abs(re)
    high = jnp.abs(im)
    larger = jnp.maximum(wide, high)
    ratio = jnp.minimum(wide, high) / jnp.where(larger == 0.0, 1.0, larger)
    turn = ratio * horner(ANGLE, ratio * ratio)
    turn = jnp.where(high > wide, 0.25 - turn, turn)
    turn = jnp.where(re < 0.0, 0.5 - turn, turn)
    return jnp.where(im < 0.0, -turn, turn)


def pack_kernel(
    half_columns, gain, dest_hbm, tile_hbm, src_hbm, cur_hbm, blocks_hbm, copies_ref,
    dest_ref, tile_ref, src_ref, cur_ref, blocks_ref, message, near_all, sems
):
    moves = [
        pltpu.make_async_copy(source, target, sems.at[k])
        for k, (source, target) in enumerate((
            (src_hbm, src_ref), (cur_hbm, cur_ref), (blocks_hbm, blocks_ref), (dest_hbm, dest_ref), (tile_hbm, tile_ref)
        ))
    ]
    for move in moves:
        move.start()
    members = copies_ref.shape[0]
    tiles = src_ref.shape[1] // LANES
    items, _, row_dev, _ = blocks_ref.shape
    columns = 2 * half_columns
    lane = lax.broadcasted_iota(jnp.int32, (SUB, LANES), 1)
    sub = lax.broadcasted_iota(jnp.int32, (SUB, LANES), 0)
    for move in moves:
        move.wait()

    for tile in range(tiles):
        part = pl.ds(tile * LANES, LANES)
        message[pl.ds(3 * tiles + tile, 2, stride=tiles), :] = cur_ref[:, part]
        message[pl.ds(tile, 3, stride=tiles), :] = src_ref[:, part]
    cr = message[3 * tiles : 4 * tiles, :]
    ci = message[4 * tiles : 5 * tiles, :]
    places = message[: 3 * tiles, :] * TURNS
    size = jnp.sqrt(cr * cr + ci * ci) * gain
    turn = phase_of(cr, ci)

    near = [jnp.zeros((SUB, LANES), jnp.float32)] * (columns // SUB)
    for block in range(items):
        tile = pl.multiple_of(tile_ref[block] * LANES, LANES)
        cr = cur_ref[0:1, pl.ds(tile, LANES)]
        ci = cur_ref[1:2, pl.ds(tile, LANES)]
        br = blocks_ref[block, 0]
        bi = blocks_ref[block, 1]
        row = jnp.zeros((SUB, LANES), jnp.float32)
        for part, product in enumerate((br * cr - bi * ci, br * ci + bi * cr)):
            total = jnp.sum(product, axis=1, keepdims=True)
            for piece in range(row_dev // SUB):
                spot = lane == sub + (part * row_dev + piece * SUB)
                row = jnp.where(spot, total[piece * SUB : (piece + 1) * SUB], row)
        row = jnp.sum(row, axis=0, keepdims=True)
        for group in range(columns // SUB):
            near[group] = near[group] + jnp.where(sub + group * SUB == dest_ref[block], row, 0.0)
    for group in range(columns // SUB):
        near_all[pl.ds(group * SUB, SUB), :] = near[group]

    def copy(member, _):
        copies_ref[member, : 3 * tiles, :] = places
        copies_ref[member, 3 * tiles : 4 * tiles, :] = size
        copies_ref[member, 4 * tiles : 5 * tiles, :] = turn
        copies_ref[member, 5 * tiles :, :] = jnp.zeros((SUB, LANES), jnp.float32)
        return 0

    lax.fori_loop(0, members, copy, 0, unroll=8)
    base = lax.axis_index("x") * half_columns
    for k in range(half_columns):
        for half in range(2):
            spot = 5 * tiles + half
            copies_ref[base + k, spot : spot + 1, :] = near_all[half * half_columns + k : half * half_columns + k + 1, :]


def points_kernel(partner_ref, across_ref, tests_ref, wide_ref):
    row_dev = tests_ref.shape[1]
    lane = lax.broadcasted_iota(jnp.int32, (row_dev, LANES), 1)
    sub = lax.broadcasted_iota(jnp.int32, (row_dev, LANES), 0)
    for which, ref in enumerate((partner_ref, across_ref, tests_ref)):
        points = jnp.concatenate([ref[...], jnp.zeros((3, LANES - row_dev), jnp.float32)], axis=1) * TURNS
        for c in range(3):
            column = jnp.sum(jnp.where(lane == sub, points[c : c + 1, :], 0.0), axis=1, keepdims=True)
            wide_ref[which, c] = jnp.broadcast_to(column, (row_dev, LANES))


def groups_of(wide_ref, which):
    return [[wide_ref[which, c, pl.ds(g * SUB, SUB), :] for c in range(3)] for g in range(wide_ref.shape[2] // SUB)]


def far_loop(tests, sums, messages_ref):
    members = messages_ref.shape[0]
    tiles = (messages_ref.shape[1] - SUB) // 5
    soft = (SOFTENING * TURNS) ** 2

    def step(member, sums):
        for tile in range(tiles):
            sx, sy, sz, size, turn = [
                jnp.broadcast_to(messages_ref[member, c * tiles + tile : c * tiles + tile + 1, :], (SUB, LANES))
                for c in range(5)
            ]
            new = []
            for (tx, ty, tz), (re, im) in zip(tests, sums):
                dx = tx - sx
                dy = ty - sy
                dz = tz - sz
                square = dx * dx + dy * dy + (dz * dz + soft)
                inverse = lax.rsqrt(square)
                t = square * inverse - turn
                u = t - ((t + ROUNDER) - ROUNDER)
                u2 = u * u
                s = u * horner(SINE, u2)
                c = horner(COSINE, u2)
                a = inverse * size
                p = a * s
                new.append(((re + a) - p * s, im + p * c))
            sums = tuple(new)
        return sums

    return lax.fori_loop(0, members, step, tuple(sums), unroll=4 // len(tests))


def rows_of(sums):
    row_dev = len(sums) * SUB
    diagonal = lax.broadcasted_iota(jnp.int32, (row_dev, LANES), 1) == lax.broadcasted_iota(jnp.int32, (row_dev, LANES), 0)
    rows = []
    for part in range(2):
        column = jnp.concatenate([jnp.sum(pair[part], axis=1, keepdims=True) for pair in sums], axis=0)
        rows.append(jnp.sum(jnp.where(diagonal, column, 0.0), axis=0, keepdims=True))
    return rows


def near_of(half_columns, other, messages_ref):
    half = lax.axis_index("half")
    spot = messages_ref.shape[1] - SUB + (1 - half if other else half)
    base = lax.axis_index("x") * half_columns
    total = messages_ref[base, pl.ds(spot, 1), :]
    for k in range(1, half_columns):
        total = total + messages_ref[base + k, pl.ds(spot, 1), :]
    return total


def first_kernel(half_columns, wide_ref, messages_ref, partner_out, across_out):
    row_dev = wide_ref.shape[2]
    groups = row_dev // SUB
    near = near_of(half_columns, True, messages_ref)
    zero = jnp.zeros((SUB, LANES), jnp.float32)
    sums = far_loop(groups_of(wide_ref, 0) + groups_of(wide_ref, 1), [(zero, zero)] * (2 * groups), messages_ref)
    re, im = rows_of(sums[:groups])
    partner_out[0:1, :] = re[:, :row_dev] + near[:, :row_dev]
    partner_out[1:2, :] = im[:, :row_dev] + near[:, row_dev : 2 * row_dev]
    re, im = rows_of(sums[groups:])
    across_out[0:1, :] = re[:, :row_dev]
    across_out[1:2, :] = im[:, :row_dev]


def second_kernel(half_columns, wide_ref, messages_ref, sibling_ref, out_ref):
    row_dev = wide_ref.shape[2]
    near = near_of(half_columns, False, messages_ref)
    tests = groups_of(wide_ref, 2)
    zero = jnp.zeros((SUB, LANES), jnp.float32)
    sums = far_loop(tests, [(zero, zero)] * len(tests), messages_ref)
    re, im = rows_of(far_loop(tests, sums, sibling_ref))
    out_ref[0:1, :] = re[:, :row_dev] + near[:, :row_dev]
    out_ref[1:2, :] = im[:, :row_dev] + near[:, row_dev : 2 * row_dev]


def swap(x, axis):
    return lax.ppermute(x, axis, [(0, 1), (1, 0)])


def across(x):
    return lax.ppermute(x, ("core", "half"), [(i, 3 - i) for i in range(4)])


def local(rows, half_columns, test_points, src_points, currents, near_blocks, near_dest, near_tile):
    row_dev = test_points.shape[1]
    width = src_points.shape[1]
    items = near_blocks.shape[0]
    members = rows // 2 * half_columns
    gain = TURNS / math.sqrt(width * members * 4)
    message = (5 * width // LANES + SUB, LANES)
    vmem = pl.BlockSpec(memory_space=pltpu.VMEM)
    hbm = pl.BlockSpec(memory_space=pltpu.HBM)
    params = pltpu.CompilerParams(vmem_limit_bytes=24 << 20)

    partner_points = swap(test_points, "half")
    across_points = across(test_points)
    copies = pl.pallas_call(
        functools.partial(pack_kernel, half_columns, gain),
        out_shape=jax.ShapeDtypeStruct((members,) + message, jnp.float32),
        in_specs=[hbm] * 5,
        out_specs=vmem,
        scratch_shapes=[
            pltpu.SMEM((items,), jnp.int32),
            pltpu.SMEM((items,), jnp.int32),
            pltpu.VMEM((3, width), jnp.float32),
            pltpu.VMEM((2, width), jnp.float32),
            pltpu.VMEM(near_blocks.shape, jnp.float32),
            pltpu.VMEM(message, jnp.float32),
            pltpu.VMEM((2 * half_columns, LANES), jnp.float32),
            pltpu.SemaphoreType.DMA((5,)),
        ],
        cost_estimate=pl.CostEstimate(flops=1 << 20, bytes_accessed=1 << 20, transcendentals=0),
    )(near_dest.reshape(-1), near_tile.reshape(-1), src_points, currents, near_blocks)
    messages = lax.all_to_all(copies, ("x", "column"), split_axis=0, concat_axis=0, tiled=True)


    evaluations = width * members * row_dev

    def cost(times):
        return dict(
            compiler_params=params,
            cost_estimate=pl.CostEstimate(
                flops=40 * evaluations * times, bytes_accessed=2 << 20, transcendentals=evaluations * times
            ),
        )

    wide = pl.pallas_call(
        points_kernel,
        out_shape=jax.ShapeDtypeStruct((3, 3, row_dev, LANES), jnp.float32),
        in_specs=[vmem] * 3,
        out_specs=vmem,
        **cost(1),
    )(partner_points, across_points, test_points)

    messages, wide = lax.optimization_barrier((messages, wide))
    sibling = swap(messages, "core")
    sums = jax.ShapeDtypeStruct((2, row_dev), jnp.float32)
    to_partner, to_across = pl.pallas_call(
        functools.partial(first_kernel, half_columns),
        out_shape=(sums, sums),
        in_specs=[vmem] * 2,
        out_specs=(vmem, vmem),
        **cost(2),
    )(wide, messages)
    from_partner = swap(to_partner, "half")
    from_across = across(to_across)
    own = pl.pallas_call(
        functools.partial(second_kernel, half_columns),
        out_shape=sums,
        in_specs=[vmem] * 3,
        out_specs=vmem,
        **cost(2),
    )(wide, messages, sibling)
    return own + from_partner + from_across


def solution(mesh):
    rows, columns = mesh.shape["row"], mesh.shape["col"]
    finer = jax.sharding.Mesh(mesh.devices.reshape(rows // 2, 2, 2, columns // 2), ("x", "core", "half", "column"))
    every = ("x", "core", "half", "column")
    in_specs = (
        P(None, every),
        P(None, every),
        P(None, every),
        P(every, None, None, None),
        P(every, None),
        P(every, None),
    )
    body = functools.partial(local, rows, columns // 2)
    return jax.shard_map(body, mesh=finer, in_specs=in_specs, out_specs=P(None, every), check_vma=False)
```

time: 22.6 us -> 23.6 us (1.044)
  waiting for transfers between devices: 4.92 us -> 5.99 us
  Pallas kernels: 5.31 us -> 4.95 us
    ppermute x0 -> x2, waiting for transfers between devices: none -> 3.8 us  [across(): return lax.ppermute(x, ('core', 'half'), [(i, 3 - i) for i in range(4)])]
    all_to_all x1, waiting for transfers between devices: 1.88 us -> 0.01 us  [local(): lax.all_to_all(copies, ('x', 'column'), split_axis=0, concat_axis=0, tile...]
    ppermute x3, waiting for transfers between devices: 3.04 us -> 2.19 us  [swap(): return lax.ppermute(x, axis, [(0, 1), (1, 0)])]
    ppermute x0 -> x2, starting transfers between devices: none -> 0.27 us  [across(): return lax.ppermute(x, ('core', 'half'), [(i, 3 - i) for i in range(4)])]
    pallas_call x1, Pallas kernels: 2.04 us -> 1.8 us  [local(): pl.pallas_call(functools.partial(pack_kernel, half_columns, gain), out_sh...]
    pallas_call x4 -> x3, Pallas kernels: 3.26 us -> 3.15 us  [the longest x1 1.54 us: local(): pl.pallas_call(functools.partial(first_kernel, half_columns), out_shape=(...]
  transfers between devices with their start and end apart: 4 -> 6, of which waited for: 4 -> 4; matrix products, arithmetic and copies ran while one was open for 0% -> 0% of each run, Pallas kernels for 11% -> 14%
where the time goes in v8:
time: 23.6 us; the launch traced here: 23.3 us
  starting transfers between devices  11.7 us (50%)
  waiting for transfers between devices  5.99 us (25%)
  Pallas kernels  4.95 us (21%)
  other arithmetic  0.57 us (2%)
    all_to_all x1, starting transfers between devices, local(): lax.all_to_all(copies, ('x', 'column'), split_axis=0, concat_axis=0, tile...  6.2 us
    ppermute x3, starting transfers between devices, swap(): return lax.ppermute(x, axis, [(0, 1), (1, 0)])  5.25 us
    ppermute x2, waiting for transfers between devices, across(): return lax.ppermute(x, ('core', 'half'), [(i, 3 - i) for i in range(4)])  3.8 us
    ppermute x3, waiting for transfers between devices, swap(): return lax.ppermute(x, axis, [(0, 1), (1, 0)])  2.19 us
    pallas_call x1, Pallas kernels, local(): pl.pallas_call(functools.partial(pack_kernel, half_columns, gain), out_sh...  1.8 us
    pallas_call x1, Pallas kernels, local(): pl.pallas_call(functools.partial(first_kernel, half_columns), out_shape=(...  1.54 us
    pallas_call x1, Pallas kernels, local(): pl.pallas_call(functools.partial(second_kernel, half_columns), out_shape=...  1.53 us
    add x1, other arithmetic, local(): return own + from_partner + from_across  0.57 us
  transfers between devices with their start and end apart: 6, of which 4 were waited for; matrix products, arithmetic and copies ran while one was open for 0% of the time, Pallas kernels for 14%

profile of v8, /device:TPU:0, one launch (start us, length us, event | category | flops | bytes accessed | tf_op | source)
XLA Modules:
  0.0 23.3 jit_solution(8423754782366850238)
XLA Ops:
  0.0 1.8 %shard_map.64 = f32[8,48,128]{2,1,0:T(8,128)} custom-call(s32[8]{0:T(128)} %bitcast.2, s32[8]{0:T(128)} %bitcast.3, f32[3,1024]{1,0:T(4,128)} %src_hbm.1, f32[2,1024]{1,0:T(2,128)} %cur_hbm.1, f32[8,2,16,128]{3,2,1,0:T(8,128)} %blocks_hbm.1), custom_call_target="tpu_custom_call" | custom-call | flops 1048576 | bytes 1048576 | tf_op jit(solution)/shard_map/pallas_call | solution.py:229
  1.8 0.0 copy-start
  1.8 6.2 %all-to-all-start = ((f32[8,48,128]{2,1,0:T(8,128)}), f32[8,48,128]{2,1,0:T(8,128)S(1)}, u32[]{:S(2)}, u32[]{:S(2)}) async-start(f32[8,48,128]{2,1,0:T(8,128)} %shard_map.64), calls=%async_computation | async-start | bytes 393216 | tf_op jit(solution)/shard_map/all_to_all | solution.py:246
  8.0 0.0 copy-done
  8.0 2.7 %collective-permute-start = (f32[3,16]{1,0:T(4,128)S(1)}, f32[3,16]{1,0:T(4,128)S(1)}, u32[]{:S(2)}, u32[]{:S(2)}) collective-permute-start(f32[3,16]{1,0:T(4,128)S(1)} %copy-done), channel_id=1, source_target_pairs={{0,4},{4,0},{1,5},{5,1},{2,6},{6,2},{3,7},{7,3},{8,12},{12,8},{9,1... | collective-permute-start | bytes 584 | tf_op jit(solution)/shard_map/ppermute | solution.py:209
  10.7 0.0 collective-permute-start.1
  10.7 2.0 %collective-permute-done.partner_ref = f32[3,16]{1,0:T(4,128)S(1)} collective-permute-done((f32[3,16]{1,0:T(4,128)S(1)}, f32[3,16]{1,0:T(4,128)S(1)}, u32[]{:S(2)}, u32[]{:S(2)}) %collective-permute-start) | collective-permute-done | bytes 224 | tf_op jit(solution)/shard_map/ppermute | solution.py:209
  12.7 1.9 %collective-permute-done.1.across_ref = f32[3,16]{1,0:T(4,128)S(1)} collective-permute-done((f32[3,16]{1,0:T(4,128)S(1)}, f32[3,16]{1,0:T(4,128)S(1)}, u32[]{:S(2)}, u32[]{:S(2)}) %collective-permute-start.1) | collective-permute-done | bytes 224 | tf_op jit(solution)/shard_map/ppermute | solution.py:213
  14.6 0.1 shard_map.65.wide_ref
  14.7 0.0 all-to-all-done.messages_ref
  14.7 0.1 collective-permute-start.2
  14.8 1.5 %shard_map.67 = (f32[2,16]{1,0:T(2,128)S(1)}, f32[2,16]{1,0:T(2,128)S(1)}) custom-call(f32[3,3,16,128]{3,2,1,0:T(8,128)S(1)} %shard_map.65.wide_ref, f32[8,48,128]{2,1,0:T(8,128)S(1)} %all-to-all-done.messages_ref), custom_call_target="tpu_custom_call" | custom-call | flops 10485760 | bytes 2097152 | tf_op jit(solution)/shard_map/pallas_call | solution.py:270
  16.3 2.5 %collective-permute-start.3 = (f32[2,16]{1,0:T(2,128)S(1)}, f32[2,16]{1,0:T(2,128)S(1)}, u32[]{:S(2)}, u32[]{:S(2)}) collective-permute-start(f32[2,16]{1,0:T(2,128)S(1)} %get-tuple-element.11), channel_id=1, source_target_pairs={{0,4},{4,0},{1,5},{5,1},{2,6},{6,2},{3,7},{7,3},{8,12},{12,8},{9,1... | collective-permute-start | bytes 392 | tf_op jit(solution)/shard_map/ppermute | solution.py:209
  18.8 0.3 %collective-permute-start.4 = (f32[2,16]{1,0:T(2,128)S(1)}, f32[2,16]{1,0:T(2,128)S(1)}, u32[]{:S(2)}, u32[]{:S(2)}) collective-permute-start(f32[2,16]{1,0:T(2,128)S(1)} %get-tuple-element.12), channel_id=1, source_target_pairs={{0,12},{4,8},{8,4},{12,0},{1,13},{5,9},{9,5},{13,1},{2,14},{6,10},... | collective-permute-start | bytes 392 | tf_op jit(solution)/shard_map/ppermute | solution.py:213
  19.1 0.0 collective-permute-done.2.sibling_ref
  19.1 1.5 %shard_map.66 = f32[2,16]{1,0:T(2,128)S(1)} custom-call(f32[3,3,16,128]{3,2,1,0:T(8,128)S(1)} %shard_map.65.wide_ref, f32[8,48,128]{2,1,0:T(8,128)S(1)} %all-to-all-done.messages_ref, f32[8,48,128]{2,1,0:T(8,128)S(1)} %collective-permute-done.2.sibling_ref), custom_call_target="tpu_custom_call" | custom-call | flops 10485760 | bytes 2097152 | tf_op jit(solution)/shard_map/pallas_call | solution.py:279
  20.6 0.2 collective-permute-done.3
  20.8 1.9 %collective-permute-done.4 = f32[2,16]{1,0:T(2,128)S(1)} collective-permute-done((f32[2,16]{1,0:T(2,128)S(1)}, f32[2,16]{1,0:T(2,128)S(1)}, u32[]{:S(2)}, u32[]{:S(2)}) %collective-permute-start.4) | collective-permute-done | bytes 160 | tf_op jit(solution)/shard_map/ppermute | solution.py:213
  22.7 0.6 %add_add_fusion = f32[2,16]{1,0:T(2,128)} fusion(f32[2,16]{1,0:T(2,128)S(1)} %collective-permute-done.4, f32[2,16]{1,0:T(2,128)S(1)} %shard_map.66, f32[2,16]{1,0:T(2,128)S(1)} %collective-permute-done.3), kind=kLoop, calls=%fused_computation | loop fusion | flops 64 | bytes 512 | tf_op jit(solution)/shard_map/add | solution.py:286
Async XLA Ops:
  1.8 6.2 %copy-start = (f32[3,16]{1,0:T(4,128)S(1)}, f32[3,16]{1,0:T(4,128)}, u32[]{:S(2)}) copy-start(f32[3,16]{1,0:T(4,128)} %tests_ref.1) | copy-start | bytes 580
  1.8 12.9 %all-to-all-start = ((f32[8,48,128]{2,1,0:T(8,128)}), f32[8,48,128]{2,1,0:T(8,128)S(1)}, u32[]{:S(2)}, u32[]{:S(2)}) async-start(f32[8,48,128]{2,1,0:T(8,128)} %shard_map.64), calls=%async_computation | async-start | bytes 393216 | tf_op jit(solution)/shard_map/all_to_all | solution.py:246
  8.0 4.6 %collective-permute-start = (f32[3,16]{1,0:T(4,128)S(1)}, f32[3,16]{1,0:T(4,128)S(1)}, u32[]{:S(2)}, u32[]{:S(2)}) collective-permute-start(f32[3,16]{1,0:T(4,128)S(1)} %copy-done), channel_id=1, source_target_pairs={{0,4},{4,0},{1,5},{5,1},{2,6},{6,2},{3,7},{7,3},{8,12},{12,8},{9,1... | collective-permute-start | bytes 584 | tf_op jit(solution)/shard_map/ppermute | solution.py:209
  10.7 3.9 %collective-permute-start.1 = (f32[3,16]{1,0:T(4,128)S(1)}, f32[3,16]{1,0:T(4,128)S(1)}, u32[]{:S(2)}, u32[]{:S(2)}) collective-permute-start(f32[3,16]{1,0:T(4,128)S(1)} %copy-done), channel_id=1, source_target_pairs={{0,12},{4,8},{8,4},{12,0},{1,13},{5,9},{9,5},{13,1},{2,14},{6,10},... | collective-permute-start | bytes 584 | tf_op jit(solution)/shard_map/ppermute | solution.py:213
  14.7 4.4 %collective-permute-start.2 = (f32[8,48,128]{2,1,0:T(8,128)S(1)}, f32[8,48,128]{2,1,0:T(8,128)S(1)}, u32[]{:S(2)}, u32[]{:S(2)}) collective-permute-start(f32[8,48,128]{2,1,0:T(8,128)S(1)} %all-to-all-done.messages_ref), channel_id=1, source_target_pairs={{0,8},{8,0},{1,9},{9,1},{2,10},{10,2},{3,11},{11,3},{4,12},{12,4},... | collective-permute-start | bytes 589832 | tf_op jit(solution)/shard_map/ppermute | solution.py:209
  16.3 4.5 %collective-permute-start.3 = (f32[2,16]{1,0:T(2,128)S(1)}, f32[2,16]{1,0:T(2,128)S(1)}, u32[]{:S(2)}, u32[]{:S(2)}) collective-permute-start(f32[2,16]{1,0:T(2,128)S(1)} %get-tuple-element.11), channel_id=1, source_target_pairs={{0,4},{4,0},{1,5},{5,1},{2,6},{6,2},{3,7},{7,3},{8,12},{12,8},{9,1... | collective-permute-start | bytes 392 | tf_op jit(solution)/shard_map/ppermute | solution.py:209
  18.8 3.9 %collective-permute-start.4 = (f32[2,16]{1,0:T(2,128)S(1)}, f32[2,16]{1,0:T(2,128)S(1)}, u32[]{:S(2)}, u32[]{:S(2)}) collective-permute-start(f32[2,16]{1,0:T(2,128)S(1)} %get-tuple-element.12), channel_id=1, source_target_pairs={{0,12},{4,8},{8,4},{12,0},{1,13},{5,9},{9,5},{13,1},{2,14},{6,10},... | collective-permute-start | bytes 392 | tf_op jit(solution)/shard_map/ppermute | solution.py:213

commit v9 on v8

--- a/solution.py
+++ b/solution.py
@@ -113,11 +113,11 @@
             copies_ref[base + k, spot : spot + 1, :] = near_all[half * half_columns + k : half * half_columns + k + 1, :]
 
 
-def points_kernel(partner_ref, across_ref, tests_ref, wide_ref):
+def points_kernel(partner_ref, tests_ref, wide_ref):
     row_dev = tests_ref.shape[1]
     lane = lax.broadcasted_iota(jnp.int32, (row_dev, LANES), 1)
     sub = lax.broadcasted_iota(jnp.int32, (row_dev, LANES), 0)
-    for which, ref in enumerate((partner_ref, across_ref, tests_ref)):
+    for which, ref in enumerate((partner_ref, tests_ref)):
         points = jnp.concatenate([ref[...], jnp.zeros((3, LANES - row_dev), jnp.float32)], axis=1) * TURNS
         for c in range(3):
             column = jnp.sum(jnp.where(lane == sub, points[c : c + 1, :], 0.0), axis=1, keepdims=True)
@@ -157,7 +157,7 @@
             sums = tuple(new)
         return sums
 
-    return lax.fori_loop(0, members, step, tuple(sums), unroll=4 // len(tests))
+    return lax.fori_loop(0, members, step, tuple(sums), unroll=8 // len(tests))
 
 
 def rows_of(sums):
@@ -180,26 +180,23 @@
     return total
 
 
-def first_kernel(half_columns, wide_ref, messages_ref, partner_out, across_out):
+def first_kernel(wide_ref, messages_ref, sums_ref):
+    groups = wide_ref.shape[2] // SUB
+    tests = groups_of(wide_ref, 0) + groups_of(wide_ref, 1)
+    zero = jnp.zeros((SUB, LANES), jnp.float32)
+    for k, pair in enumerate(far_loop(tests, [(zero, zero)] * len(tests), messages_ref)):
+        for part in range(2):
+            sums_ref[k // groups, part, pl.ds(k % groups * SUB, SUB), :] = pair[part]
+
+
+def second_kernel(half_columns, other, wide_ref, sums_ref, messages_ref, sibling_ref, out_ref):
     row_dev = wide_ref.shape[2]
-    groups = row_dev // SUB
-    near = near_of(half_columns, True, messages_ref)
-    zero = jnp.zeros((SUB, LANES), jnp.float32)
-    sums = far_loop(groups_of(wide_ref, 0) + groups_of(wide_ref, 1), [(zero, zero)] * (2 * groups), messages_ref)
-    re, im = rows_of(sums[:groups])
-    partner_out[0:1, :] = re[:, :row_dev] + near[:, :row_dev]
-    partner_out[1:2, :] = im[:, :row_dev] + near[:, row_dev : 2 * row_dev]
-    re, im = rows_of(sums[groups:])
-    across_out[0:1, :] = re[:, :row_dev]
-    across_out[1:2, :] = im[:, :row_dev]
-
-
-def second_kernel(half_columns, wide_ref, messages_ref, sibling_ref, out_ref):
-    row_dev = wide_ref.shape[2]
-    near = near_of(half_columns, False, messages_ref)
-    tests = groups_of(wide_ref, 2)
-    zero = jnp.zeros((SUB, LANES), jnp.float32)
-    sums = far_loop(tests, [(zero, zero)] * len(tests), messages_ref)
+    which = 0 if other else 1
+    tests = groups_of(wide_ref, which)
+    near = near_of(half_columns, other, messages_ref)
+    sums = [
+        (sums_ref[which, 0, pl.ds(g * SUB, SUB), :], sums_ref[which, 1, pl.ds(g * SUB, SUB), :]) for g in range(len(tests))
+    ]
     re, im = rows_of(far_loop(tests, sums, sibling_ref))
     out_ref[0:1, :] = re[:, :row_dev] + near[:, :row_dev]
     out_ref[1:2, :] = im[:, :row_dev] + near[:, row_dev : 2 * row_dev]
@@ -207,10 +204,6 @@
 
 def swap(x, axis):
     return lax.ppermute(x, axis, [(0, 1), (1, 0)])
-
-
-def across(x):
-    return lax.ppermute(x, ("core", "half"), [(i, 3 - i) for i in range(4)])
 
 
 def local(rows, half_columns, test_points, src_points, currents, near_blocks, near_dest, near_tile):
@@ -225,7 +218,6 @@
     params = pltpu.CompilerParams(vmem_limit_bytes=24 << 20)
 
     partner_points = swap(test_points, "half")
-    across_points = across(test_points)
     copies = pl.pallas_call(
         functools.partial(pack_kernel, half_columns, gain),
         out_shape=jax.ShapeDtypeStruct((members,) + message, jnp.float32),
@@ -258,32 +250,33 @@
 
     wide = pl.pallas_call(
         points_kernel,
-        out_shape=jax.ShapeDtypeStruct((3, 3, row_dev, LANES), jnp.float32),
-        in_specs=[vmem] * 3,
+        out_shape=jax.ShapeDtypeStruct((2, 3, row_dev, LANES), jnp.float32),
+        in_specs=[vmem] * 2,
         out_specs=vmem,
         **cost(1),
-    )(partner_points, across_points, test_points)
+    )(partner_points, test_points)
 
     messages, wide = lax.optimization_barrier((messages, wide))
     sibling = swap(messages, "core")
-    sums = jax.ShapeDtypeStruct((2, row_dev), jnp.float32)
-    to_partner, to_across = pl.pallas_call(
-        functools.partial(first_kernel, half_columns),
-        out_shape=(sums, sums),
+    sums = pl.pallas_call(
+        first_kernel,
+        out_shape=jax.ShapeDtypeStruct((2, 2, row_dev, LANES), jnp.float32),
         in_specs=[vmem] * 2,
-        out_specs=(vmem, vmem),
+        out_specs=vmem,
         **cost(2),
     )(wide, messages)
-    from_partner = swap(to_partner, "half")
-    from_across = across(to_across)
-    own = pl.pallas_call(
-        functools.partial(second_kernel, half_columns),
-        out_shape=sums,
-        in_specs=[vmem] * 3,
-        out_specs=vmem,
-        **cost(2),
-    )(wide, messages, sibling)
-    return own + from_partner + from_across
+
+    def second(other):
+        return pl.pallas_call(
+            functools.partial(second_kernel, half_columns, other),
+            out_shape=jax.ShapeDtypeStruct((2, row_dev), jnp.float32),
+            in_specs=[vmem] * 4,
+            out_specs=vmem,
+            **cost(1),
+        )(wide, sums, messages, sibling)
+
+    from_partner = swap(second(True), "half")
+    return second(False) + from_partner
 
 
 def solution(mesh):

time: 23.6 us -> 22.3 us (0.945)
  waiting for transfers between devices: 5.99 us -> 5.05 us
    ppermute x2 -> x0, waiting for transfers between devices: 3.8 us -> none  [across(): return lax.ppermute(x, ('core', 'half'), [(i, 3 - i) for i in range(4)])]
    all_to_all x1, waiting for transfers between devices: 0.01 us -> 1.88 us  [local(): lax.all_to_all(copies, ('x', 'column'), split_axis=0, concat_axis=0, tile...]
    ppermute x3, waiting for transfers between devices: 2.19 us -> 3.16 us  [swap(): return lax.ppermute(x, axis, [(0, 1), (1, 0)])]
    ppermute x2 -> x0, starting transfers between devices: 0.27 us -> none  [across(): return lax.ppermute(x, ('core', 'half'), [(i, 3 - i) for i in range(4)])]
    pallas_call x3 -> x4, Pallas kernels: 3.15 us -> 3.04 us  [the longest x2 1.63 us: second(): pl.pallas_call(functools.partial(second_kernel, half_columns, other), out...]
  transfers between devices with their start and end apart: 6 -> 4, of which waited for: 4 -> 4; matrix products, arithmetic and copies ran while one was open for 0% -> 0% of each run, Pallas kernels for 14% -> 10%
where the time goes in v9:
time: 22.3 us; the launch traced here: 22 us
  starting transfers between devices  11.5 us (52%)
  waiting for transfers between devices  5.05 us (23%)
  Pallas kernels  4.84 us (22%)
  other arithmetic  0.56 us (3%)
    all_to_all x1, starting transfers between devices, local(): lax.all_to_all(copies, ('x', 'column'), split_axis=0, concat_axis=0, tile...  6.2 us
    ppermute x3, starting transfers between devices, swap(): return lax.ppermute(x, axis, [(0, 1), (1, 0)])  5.32 us
    ppermute x3, waiting for transfers between devices, swap(): return lax.ppermute(x, axis, [(0, 1), (1, 0)])  3.16 us
    all_to_all x1, waiting for transfers between devices, local(): lax.all_to_all(copies, ('x', 'column'), split_axis=0, concat_axis=0, tile...  1.88 us
    pallas_call x1, Pallas kernels, local(): pl.pallas_call(functools.partial(pack_kernel, half_columns, gain), out_sh...  1.8 us
    pallas_call x2, Pallas kernels, second(): pl.pallas_call(functools.partial(second_kernel, half_columns, other), out...  1.63 us
    pallas_call x1, Pallas kernels, local(): pl.pallas_call(first_kernel, out_shape=jax.ShapeDtypeStruct((2, 2, row_de...  1.32 us
    add x1, other arithmetic, local(): return second(False) + from_partner  0.56 us
  transfers between devices with their start and end apart: 4, of which 4 were waited for; matrix products, arithmetic and copies ran while one was open for 0% of the time, Pallas kernels for 10%

profile of v9, /device:TPU:0, one launch (start us, length us, event | category | flops | bytes accessed | tf_op | source)
XLA Modules:
  0.0 22.0 jit_solution(9925922516265844749)
XLA Ops:
  0.0 1.8 %shard_map.64 = f32[8,48,128]{2,1,0:T(8,128)} custom-call(s32[8]{0:T(128)} %bitcast.2, s32[8]{0:T(128)} %bitcast.3, f32[3,1024]{1,0:T(4,128)} %src_hbm.1, f32[2,1024]{1,0:T(2,128)} %cur_hbm.1, f32[8,2,16,128]{3,2,1,0:T(8,128)} %blocks_hbm.1), custom_call_target="tpu_custom_call" | custom-call | flops 1048576 | bytes 1048576 | tf_op jit(solution)/shard_map/pallas_call | solution.py:221
  1.8 0.0 copy-start
  1.8 6.2 %all-to-all-start = ((f32[8,48,128]{2,1,0:T(8,128)}), f32[8,48,128]{2,1,0:T(8,128)S(1)}, u32[]{:S(2)}, u32[]{:S(2)}) async-start(f32[8,48,128]{2,1,0:T(8,128)} %shard_map.64), calls=%async_computation | async-start | bytes 393216 | tf_op jit(solution)/shard_map/all_to_all | solution.py:238
  8.0 0.0 copy-done
  8.0 2.7 %collective-permute-start = (f32[3,16]{1,0:T(4,128)S(1)}, f32[3,16]{1,0:T(4,128)S(1)}, u32[]{:S(2)}, u32[]{:S(2)}) collective-permute-start(f32[3,16]{1,0:T(4,128)S(1)} %copy-done), channel_id=1, source_target_pairs={{0,4},{4,0},{1,5},{5,1},{2,6},{6,2},{3,7},{7,3},{8,12},{12,8},{9,1... | collective-permute-start | bytes 584 | tf_op jit(solution)/shard_map/ppermute | solution.py:206
  10.7 2.0 %collective-permute-done.partner_ref = f32[3,16]{1,0:T(4,128)S(1)} collective-permute-done((f32[3,16]{1,0:T(4,128)S(1)}, f32[3,16]{1,0:T(4,128)S(1)}, u32[]{:S(2)}, u32[]{:S(2)}) %collective-permute-start) | collective-permute-done | bytes 224 | tf_op jit(solution)/shard_map/ppermute | solution.py:206
  12.7 0.1 shard_map.65.wide_ref
  12.8 1.9 %all-to-all-done.messages_ref = f32[8,48,128]{2,1,0:T(8,128)S(1)} async-done(((f32[8,48,128]{2,1,0:T(8,128)}), f32[8,48,128]{2,1,0:T(8,128)S(1)}, u32[]{:S(2)}, u32[]{:S(2)}) %all-to-all-start) | async-done | bytes 196640 | tf_op jit(solution)/shard_map/all_to_all | solution.py:238
  14.6 0.0 collective-permute-start.1
  14.6 1.3 %shard_map.66.sums_ref = f32[2,2,16,128]{3,2,1,0:T(8,128)S(1)} custom-call(f32[2,3,16,128]{3,2,1,0:T(8,128)S(1)} %shard_map.65.wide_ref, f32[8,48,128]{2,1,0:T(8,128)S(1)} %all-to-all-done.messages_ref), custom_call_target="tpu_custom_call" | custom-call | flops 10485760 | bytes 2097152 | tf_op jit(solution)/shard_map/pallas_call | solution.py:261
  16.0 0.1 collective-permute-done.1.sibling_ref
  16.1 0.8 %shard_map.68 = f32[2,16]{1,0:T(2,128)S(1)} custom-call(f32[2,3,16,128]{3,2,1,0:T(8,128)S(1)} %shard_map.65.wide_ref, f32[2,2,16,128]{3,2,1,0:T(8,128)S(1)} %shard_map.66.sums_ref, f32[8,48,128]{2,1,0:T(8,128)S(1)} %all-to-all-done.messages_ref, f32[8,48,128]{2,1,0:T(8,128)S(1)} %collective-permute-done.1.sibling_ref), custom_call_target="tpu_custom_call" | custom-call | flops 5242880 | bytes 2097152 | tf_op jit(solution)/shard_map/pallas_call | solution.py:270
  16.9 2.7 %collective-permute-start.2 = (f32[2,16]{1,0:T(2,128)S(1)}, f32[2,16]{1,0:T(2,128)S(1)}, u32[]{:S(2)}, u32[]{:S(2)}) collective-permute-start(f32[2,16]{1,0:T(2,128)S(1)} %shard_map.68), channel_id=1, source_target_pairs={{0,4},{4,0},{1,5},{5,1},{2,6},{6,2},{3,7},{7,3},{8,12},{12,8},{9,1... | collective-permute-start | bytes 392 | tf_op jit(solution)/shard_map/ppermute | solution.py:206
  19.6 0.8 %shard_map.67 = f32[2,16]{1,0:T(2,128)S(1)} custom-call(f32[2,3,16,128]{3,2,1,0:T(8,128)S(1)} %shard_map.65.wide_ref, f32[2,2,16,128]{3,2,1,0:T(8,128)S(1)} %shard_map.66.sums_ref, f32[8,48,128]{2,1,0:T(8,128)S(1)} %all-to-all-done.messages_ref, f32[8,48,128]{2,1,0:T(8,128)S(1)} %collective-permute-done.1.sibling_ref), custom_call_target="tpu_custom_call" | custom-call | flops 5242880 | bytes 2097152 | tf_op jit(solution)/shard_map/pallas_call | solution.py:270
  20.4 1.1 %collective-permute-done.2 = f32[2,16]{1,0:T(2,128)S(1)} collective-permute-done((f32[2,16]{1,0:T(2,128)S(1)}, f32[2,16]{1,0:T(2,128)S(1)}, u32[]{:S(2)}, u32[]{:S(2)}) %collective-permute-start.2) | collective-permute-done | bytes 160 | tf_op jit(solution)/shard_map/ppermute | solution.py:206
  21.4 0.6 %add.3 = f32[2,16]{1,0:T(2,128)} add(f32[2,16]{1,0:T(2,128)S(1)} %shard_map.67, f32[2,16]{1,0:T(2,128)S(1)} %collective-permute-done.2) | non-fusion elementwise | flops 32 | bytes 384 | tf_op jit(solution)/shard_map/add | solution.py:279
Async XLA Ops:
  1.8 6.2 %copy-start = (f32[3,16]{1,0:T(4,128)S(1)}, f32[3,16]{1,0:T(4,128)}, u32[]{:S(2)}) copy-start(f32[3,16]{1,0:T(4,128)} %tests_ref.1) | copy-start | bytes 580
  1.8 12.8 %all-to-all-start = ((f32[8,48,128]{2,1,0:T(8,128)}), f32[8,48,128]{2,1,0:T(8,128)S(1)}, u32[]{:S(2)}, u32[]{:S(2)}) async-start(f32[8,48,128]{2,1,0:T(8,128)} %shard_map.64), calls=%async_computation | async-start | bytes 393216 | tf_op jit(solution)/shard_map/all_to_all | solution.py:238
  8.0 4.6 %collective-permute-start = (f32[3,16]{1,0:T(4,128)S(1)}, f32[3,16]{1,0:T(4,128)S(1)}, u32[]{:S(2)}, u32[]{:S(2)}) collective-permute-start(f32[3,16]{1,0:T(4,128)S(1)} %copy-done), channel_id=1, source_target_pairs={{0,4},{4,0},{1,5},{5,1},{2,6},{6,2},{3,7},{7,3},{8,12},{12,8},{9,1... | collective-permute-start | bytes 584 | tf_op jit(solution)/shard_map/ppermute | solution.py:206
  14.6 1.4 %collective-permute-start.1 = (f32[8,48,128]{2,1,0:T(8,128)S(1)}, f32[8,48,128]{2,1,0:T(8,128)S(1)}, u32[]{:S(2)}, u32[]{:S(2)}) collective-permute-start(f32[8,48,128]{2,1,0:T(8,128)S(1)} %all-to-all-done.messages_ref), channel_id=1, source_target_pairs={{0,8},{8,0},{1,9},{9,1},{2,10},{10,2},{3,11},{11,3},{4,12},{12,4},... | collective-permute-start | bytes 589832 | tf_op jit(solution)/shard_map/ppermute | solution.py:206
  16.9 4.5 %collective-permute-start.2 = (f32[2,16]{1,0:T(2,128)S(1)}, f32[2,16]{1,0:T(2,128)S(1)}, u32[]{:S(2)}, u32[]{:S(2)}) collective-permute-start(f32[2,16]{1,0:T(2,128)S(1)} %shard_map.68), channel_id=1, source_target_pairs={{0,4},{4,0},{1,5},{5,1},{2,6},{6,2},{3,7},{7,3},{8,12},{12,8},{9,1... | collective-permute-start | bytes 392 | tf_op jit(solution)/shard_map/ppermute | solution.py:206

commit v10 on v9

--- a/solution.py
+++ b/solution.py
@@ -14,6 +14,7 @@
 TURNS = WAVENUMBER / (2.0 * math.pi)
 LANES = 128
 SUB = 8
+QUAD = 4
 
 
 def even_fit(function, terms, reach):
@@ -66,8 +67,8 @@
     columns = 2 * half_columns
     lane = lax.broadcasted_iota(jnp.int32, (SUB, LANES), 1)
     sub = lax.broadcasted_iota(jnp.int32, (SUB, LANES), 0)
-    for move in moves:
-        move.wait()
+    moves[0].wait()
+    moves[1].wait()
 
     for tile in range(tiles):
         part = pl.ds(tile * LANES, LANES)
@@ -75,10 +76,21 @@
         message[pl.ds(tile, 3, stride=tiles), :] = src_ref[:, part]
     cr = message[3 * tiles : 4 * tiles, :]
     ci = message[4 * tiles : 5 * tiles, :]
-    places = message[: 3 * tiles, :] * TURNS
-    size = jnp.sqrt(cr * cr + ci * ci) * gain
-    turn = phase_of(cr, ci)
-
+    values = [message[c * tiles : (c + 1) * tiles, :] * TURNS for c in range(3)]
+    values += [jnp.sqrt(cr * cr + ci * ci) * gain, phase_of(cr, ci)]
+    pieces = [value[part * QUAD : (part + 1) * QUAD] for value in values for part in range(tiles // QUAD)]
+    last = len(pieces) * LANES
+
+    def copy(member, _):
+        for slot, piece in enumerate(pieces):
+            copies_ref[member, :, slot * LANES : (slot + 1) * LANES] = piece
+        copies_ref[member, :, last:] = jnp.zeros((QUAD, LANES), jnp.float32)
+        return 0
+
+    lax.fori_loop(0, members, copy, 0, unroll=8)
+
+    for move in moves[2:]:
+        move.wait()
     near = [jnp.zeros((SUB, LANES), jnp.float32)] * (columns // SUB)
     for block in range(items):
         tile = pl.multiple_of(tile_ref[block] * LANES, LANES)
@@ -98,19 +110,10 @@
     for group in range(columns // SUB):
         near_all[pl.ds(group * SUB, SUB), :] = near[group]
 
-    def copy(member, _):
-        copies_ref[member, : 3 * tiles, :] = places
-        copies_ref[member, 3 * tiles : 4 * tiles, :] = size
-        copies_ref[member, 4 * tiles : 5 * tiles, :] = turn
-        copies_ref[member, 5 * tiles :, :] = jnp.zeros((SUB, LANES), jnp.float32)
-        return 0
-
-    lax.fori_loop(0, members, copy, 0, unroll=8)
     base = lax.axis_index("x") * half_columns
     for k in range(half_columns):
         for half in range(2):
-            spot = 5 * tiles + half
-            copies_ref[base + k, spot : spot + 1, :] = near_all[half * half_columns + k : half * half_columns + k + 1, :]
+            copies_ref[base + k, half : half + 1, last:] = near_all[half * half_columns + k : half * half_columns + k + 1, :]
 
 
 def points_kernel(partner_ref, tests_ref, wide_ref):
@@ -130,13 +133,15 @@
 
 def far_loop(tests, sums, messages_ref):
     members = messages_ref.shape[0]
-    tiles = (messages_ref.shape[1] - SUB) // 5
+    slots = (messages_ref.shape[2] // LANES - 1) // 5
     soft = (SOFTENING * TURNS) ** 2
 
     def step(member, sums):
-        for tile in range(tiles):
+        for slot, row in [(slot, row) for slot in range(slots) for row in range(QUAD)]:
             sx, sy, sz, size, turn = [
-                jnp.broadcast_to(messages_ref[member, c * tiles + tile : c * tiles + tile + 1, :], (SUB, LANES))
+                jnp.broadcast_to(
+                    messages_ref[member, row : row + 1, (c * slots + slot) * LANES : (c * slots + slot + 1) * LANES], (SUB, LANES)
+                )
                 for c in range(5)
             ]
             new = []
@@ -171,13 +176,13 @@
 
 
 def near_of(half_columns, other, messages_ref):
-    half = lax.axis_index("half")
-    spot = messages_ref.shape[1] - SUB + (1 - half if other else half)
+    last = messages_ref.shape[2] - LANES
     base = lax.axis_index("x") * half_columns
-    total = messages_ref[base, pl.ds(spot, 1), :]
+    total = messages_ref[base, :, last:]
     for k in range(1, half_columns):
-        total = total + messages_ref[base + k, pl.ds(spot, 1), :]
-    return total
+        total = total + messages_ref[base + k, :, last:]
+    first = lax.axis_index("half") == (1 if other else 0)
+    return jnp.where(first, total[0:1], total[1:2])
 
 
 def first_kernel(wide_ref, messages_ref, sums_ref):
@@ -212,7 +217,7 @@
     items = near_blocks.shape[0]
     members = rows // 2 * half_columns
     gain = TURNS / math.sqrt(width * members * 4)
-    message = (5 * width // LANES + SUB, LANES)
+    message = (QUAD, 5 * width // QUAD + LANES)
     vmem = pl.BlockSpec(memory_space=pltpu.VMEM)
     hbm = pl.BlockSpec(memory_space=pltpu.HBM)
     params = pltpu.CompilerParams(vmem_limit_bytes=24 << 20)
@@ -229,7 +234,7 @@
             pltpu.VMEM((3, width), jnp.float32),
             pltpu.VMEM((2, width), jnp.float32),
             pltpu.VMEM(near_blocks.shape, jnp.float32),
-            pltpu.VMEM(message, jnp.float32),
+            pltpu.VMEM((5 * width // LANES, LANES), jnp.float32),
             pltpu.VMEM((2 * half_columns, LANES), jnp.float32),
             pltpu.SemaphoreType.DMA((5,)),
         ],

time: 22.3 us -> 22.2 us (level)
  no operation moved by 1% of the time
where the time goes in v10:
time: 22.2 us; the launch traced here: 21.9 us
  starting transfers between devices  11.5 us (52%)
  waiting for transfers between devices  4.92 us (22%)
  Pallas kernels  4.85 us (22%)
  other arithmetic  0.56 us (3%)
    all_to_all x1, starting transfers between devices, local(): lax.all_to_all(copies, ('x', 'column'), split_axis=0, concat_axis=0, tile...  6.2 us
    ppermute x3, starting transfers between devices, swap(): return lax.ppermute(x, axis, [(0, 1), (1, 0)])  5.32 us
    ppermute x3, waiting for transfers between devices, swap(): return lax.ppermute(x, axis, [(0, 1), (1, 0)])  3.13 us
    pallas_call x1, Pallas kernels, local(): pl.pallas_call(functools.partial(pack_kernel, half_columns, gain), out_sh...  1.8 us
    all_to_all x1, waiting for transfers between devices, local(): lax.all_to_all(copies, ('x', 'column'), split_axis=0, concat_axis=0, tile...  1.79 us
    pallas_call x2, Pallas kernels, second(): pl.pallas_call(functools.partial(second_kernel, half_columns, other), out...  1.64 us
    pallas_call x1, Pallas kernels, local(): pl.pallas_call(first_kernel, out_shape=jax.ShapeDtypeStruct((2, 2, row_de...  1.33 us
    add x1, other arithmetic, local(): return second(False) + from_partner  0.56 us
  transfers between devices with their start and end apart: 4, of which 4 were waited for; matrix products, arithmetic and copies ran while one was open for 0% of the time, Pallas kernels for 10%

profile of v10, /device:TPU:0, one launch (start us, length us, event | category | flops | bytes accessed | tf_op | source)
XLA Modules:
  0.0 21.9 jit_solution(445852620975008906)
XLA Ops:
  0.0 1.8 %shard_map.64 = f32[8,4,1408]{2,1,0:T(4,128)} custom-call(s32[8]{0:T(128)} %bitcast.2, s32[8]{0:T(128)} %bitcast.3, f32[3,1024]{1,0:T(4,128)} %src_hbm.1, f32[2,1024]{1,0:T(2,128)} %cur_hbm.1, f32[8,2,16,128]{3,2,1,0:T(8,128)} %blocks_hbm.1), custom_call_target="tpu_custom_call" | custom-call | flops 1048576 | bytes 1048576 | tf_op jit(solution)/shard_map/pallas_call | solution.py:226
  1.8 0.0 copy-start
  1.8 6.2 %all-to-all-start = ((f32[8,4,1408]{2,1,0:T(4,128)}), f32[8,4,1408]{2,1,0:T(4,128)S(1)}, u32[]{:S(2)}, u32[]{:S(2)}) async-start(f32[8,4,1408]{2,1,0:T(4,128)} %shard_map.64), calls=%async_computation | async-start | bytes 360448 | tf_op jit(solution)/shard_map/all_to_all | solution.py:243
  8.0 0.0 copy-done
  8.0 2.7 %collective-permute-start = (f32[3,16]{1,0:T(4,128)S(1)}, f32[3,16]{1,0:T(4,128)S(1)}, u32[]{:S(2)}, u32[]{:S(2)}) collective-permute-start(f32[3,16]{1,0:T(4,128)S(1)} %copy-done), channel_id=1, source_target_pairs={{0,4},{4,0},{1,5},{5,1},{2,6},{6,2},{3,7},{7,3},{8,12},{12,8},{9,1... | collective-permute-start | bytes 584 | tf_op jit(solution)/shard_map/ppermute | solution.py:211
  10.7 2.0 %collective-permute-done.partner_ref = f32[3,16]{1,0:T(4,128)S(1)} collective-permute-done((f32[3,16]{1,0:T(4,128)S(1)}, f32[3,16]{1,0:T(4,128)S(1)}, u32[]{:S(2)}, u32[]{:S(2)}) %collective-permute-start) | collective-permute-done | bytes 224 | tf_op jit(solution)/shard_map/ppermute | solution.py:211
  12.7 0.1 shard_map.65.wide_ref
  12.8 1.8 %all-to-all-done.messages_ref = f32[8,4,1408]{2,1,0:T(4,128)S(1)} async-done(((f32[8,4,1408]{2,1,0:T(4,128)}), f32[8,4,1408]{2,1,0:T(4,128)S(1)}, u32[]{:S(2)}, u32[]{:S(2)}) %all-to-all-start) | async-done | bytes 180256 | tf_op jit(solution)/shard_map/all_to_all | solution.py:243
  14.5 0.0 collective-permute-start.1
  14.6 1.3 %shard_map.66.sums_ref = f32[2,2,16,128]{3,2,1,0:T(8,128)S(1)} custom-call(f32[2,3,16,128]{3,2,1,0:T(8,128)S(1)} %shard_map.65.wide_ref, f32[8,4,1408]{2,1,0:T(4,128)S(1)} %all-to-all-done.messages_ref), custom_call_target="tpu_custom_call" | custom-call | flops 10485760 | bytes 2097152 | tf_op jit(solution)/shard_map/pallas_call | solution.py:266
  15.9 0.1 collective-permute-done.1.sibling_ref
  16.0 0.8 %shard_map.68 = f32[2,16]{1,0:T(2,128)S(1)} custom-call(f32[2,3,16,128]{3,2,1,0:T(8,128)S(1)} %shard_map.65.wide_ref, f32[2,2,16,128]{3,2,1,0:T(8,128)S(1)} %shard_map.66.sums_ref, f32[8,4,1408]{2,1,0:T(4,128)S(1)} %all-to-all-done.messages_ref, f32[8,4,1408]{2,1,0:T(4,128)S(1)} %collective-permute-done.1.sibling_ref), custom_call_target="tpu_custom_call" | custom-call | flops 5242880 | bytes 2097152 | tf_op jit(solution)/shard_map/pallas_call | solution.py:275
  16.8 2.7 %collective-permute-start.2 = (f32[2,16]{1,0:T(2,128)S(1)}, f32[2,16]{1,0:T(2,128)S(1)}, u32[]{:S(2)}, u32[]{:S(2)}) collective-permute-start(f32[2,16]{1,0:T(2,128)S(1)} %shard_map.68), channel_id=1, source_target_pairs={{0,4},{4,0},{1,5},{5,1},{2,6},{6,2},{3,7},{7,3},{8,12},{12,8},{9,1... | collective-permute-start | bytes 392 | tf_op jit(solution)/shard_map/ppermute | solution.py:211
  19.4 0.8 %shard_map.67 = f32[2,16]{1,0:T(2,128)S(1)} custom-call(f32[2,3,16,128]{3,2,1,0:T(8,128)S(1)} %shard_map.65.wide_ref, f32[2,2,16,128]{3,2,1,0:T(8,128)S(1)} %shard_map.66.sums_ref, f32[8,4,1408]{2,1,0:T(4,128)S(1)} %all-to-all-done.messages_ref, f32[8,4,1408]{2,1,0:T(4,128)S(1)} %collective-permute-done.1.sibling_ref), custom_call_target="tpu_custom_call" | custom-call | flops 5242880 | bytes 2097152 | tf_op jit(solution)/shard_map/pallas_call | solution.py:275
  20.3 1.1 %collective-permute-done.2 = f32[2,16]{1,0:T(2,128)S(1)} collective-permute-done((f32[2,16]{1,0:T(2,128)S(1)}, f32[2,16]{1,0:T(2,128)S(1)}, u32[]{:S(2)}, u32[]{:S(2)}) %collective-permute-start.2) | collective-permute-done | bytes 160 | tf_op jit(solution)/shard_map/ppermute | solution.py:211
  21.3 0.6 %add.3 = f32[2,16]{1,0:T(2,128)} add(f32[2,16]{1,0:T(2,128)S(1)} %shard_map.67, f32[2,16]{1,0:T(2,128)S(1)} %collective-permute-done.2) | non-fusion elementwise | flops 32 | bytes 384 | tf_op jit(solution)/shard_map/add | solution.py:284
Async XLA Ops:
  1.8 6.2 %copy-start = (f32[3,16]{1,0:T(4,128)S(1)}, f32[3,16]{1,0:T(4,128)}, u32[]{:S(2)}) copy-start(f32[3,16]{1,0:T(4,128)} %tests_ref.1) | copy-start | bytes 580
  1.8 12.7 %all-to-all-start = ((f32[8,4,1408]{2,1,0:T(4,128)}), f32[8,4,1408]{2,1,0:T(4,128)S(1)}, u32[]{:S(2)}, u32[]{:S(2)}) async-start(f32[8,4,1408]{2,1,0:T(4,128)} %shard_map.64), calls=%async_computation | async-start | bytes 360448 | tf_op jit(solution)/shard_map/all_to_all | solution.py:243
  8.0 4.6 %collective-permute-start = (f32[3,16]{1,0:T(4,128)S(1)}, f32[3,16]{1,0:T(4,128)S(1)}, u32[]{:S(2)}, u32[]{:S(2)}) collective-permute-start(f32[3,16]{1,0:T(4,128)S(1)} %copy-done), channel_id=1, source_target_pairs={{0,4},{4,0},{1,5},{5,1},{2,6},{6,2},{3,7},{7,3},{8,12},{12,8},{9,1... | collective-permute-start | bytes 584 | tf_op jit(solution)/shard_map/ppermute | solution.py:211
  14.5 1.4 %collective-permute-start.1 = (f32[8,4,1408]{2,1,0:T(4,128)S(1)}, f32[8,4,1408]{2,1,0:T(4,128)S(1)}, u32[]{:S(2)}, u32[]{:S(2)}) collective-permute-start(f32[8,4,1408]{2,1,0:T(4,128)S(1)} %all-to-all-done.messages_ref), channel_id=1, source_target_pairs={{0,8},{8,0},{1,9},{9,1},{2,10},{10,2},{3,11},{11,3},{4,12},{12,4},... | collective-permute-start | bytes 540680 | tf_op jit(solution)/shard_map/ppermute | solution.py:211
  16.8 4.5 %collective-permute-start.2 = (f32[2,16]{1,0:T(2,128)S(1)}, f32[2,16]{1,0:T(2,128)S(1)}, u32[]{:S(2)}, u32[]{:S(2)}) collective-permute-start(f32[2,16]{1,0:T(2,128)S(1)} %shard_map.68), channel_id=1, source_target_pairs={{0,4},{4,0},{1,5},{5,1},{2,6},{6,2},{3,7},{7,3},{8,12},{12,8},{9,1... | collective-permute-start | bytes 392 | tf_op jit(solution)/shard_map/ppermute | solution.py:211

commit v11 on v10

--- a/solution.py
+++ b/solution.py
@@ -198,7 +198,7 @@
     row_dev = wide_ref.shape[2]
     which = 0 if other else 1
     tests = groups_of(wide_ref, which)
-    near = near_of(half_columns, other, messages_ref)
+    near = near_of(half_columns, other, sibling_ref if other else messages_ref)
     sums = [
         (sums_ref[which, 0, pl.ds(g * SUB, SUB), :], sums_ref[which, 1, pl.ds(g * SUB, SUB), :]) for g in range(len(tests))
     ]
@@ -207,8 +207,8 @@
     out_ref[1:2, :] = im[:, :row_dev] + near[:, row_dev : 2 * row_dev]
 
 
-def swap(x, axis):
-    return lax.ppermute(x, axis, [(0, 1), (1, 0)])
+def across(x):
+    return lax.ppermute(x, ("core", "half"), [(i, 3 - i) for i in range(4)])
 
 
 def local(rows, half_columns, test_points, src_points, currents, near_blocks, near_dest, near_tile):
@@ -222,7 +222,7 @@
     hbm = pl.BlockSpec(memory_space=pltpu.HBM)
     params = pltpu.CompilerParams(vmem_limit_bytes=24 << 20)
 
-    partner_points = swap(test_points, "half")
+    partner_points = across(test_points)
     copies = pl.pallas_call(
         functools.partial(pack_kernel, half_columns, gain),
         out_shape=jax.ShapeDtypeStruct((members,) + message, jnp.float32),
@@ -262,7 +262,7 @@
     )(partner_points, test_points)
 
     messages, wide = lax.optimization_barrier((messages, wide))
-    sibling = swap(messages, "core")
+    sibling = lax.ppermute(messages, "core", [(0, 1), (1, 0)])
     sums = pl.pallas_call(
         first_kernel,
         out_shape=jax.ShapeDtypeStruct((2, 2, row_dev, LANES), jnp.float32),
@@ -280,7 +280,7 @@
             **cost(1),
         )(wide, sums, messages, sibling)
 
-    from_partner = swap(second(True), "half")
+    from_partner = across(second(True))
     return second(False) + from_partner
 
 

time: 22.2 us -> 21.6 us (0.973)
  starting transfers between devices: 11.5 us -> 10.7 us
  waiting for transfers between devices: 4.92 us -> 5.23 us
    ppermute x3, starting transfers between devices: 5.32 us -> 4.49 us  [the longest x2 4.49 us: across(): return lax.ppermute(x, ('core', 'half'), [(i, 3 - i) for i in range(4)])]
    all_to_all x1, waiting for transfers between devices: 1.79 us -> 2.41 us  [local(): lax.all_to_all(copies, ('x', 'column'), split_axis=0, concat_axis=0, tile...]
    ppermute x3, waiting for transfers between devices: 3.13 us -> 2.82 us  [the longest x2 2.75 us: across(): return lax.ppermute(x, ('core', 'half'), [(i, 3 - i) for i in range(4)])]
where the time goes in v11:
time: 21.6 us; the launch traced here: 21.4 us
  starting transfers between devices  10.7 us (50%)
  waiting for transfers between devices  5.23 us (24%)
  Pallas kernels  4.85 us (22%)
  other arithmetic  0.56 us (3%)
    all_to_all x1, starting transfers between devices, local(): lax.all_to_all(copies, ('x', 'column'), split_axis=0, concat_axis=0, tile...  6.2 us
    ppermute x2, starting transfers between devices, across(): return lax.ppermute(x, ('core', 'half'), [(i, 3 - i) for i in range(4)])  4.49 us
    ppermute x2, waiting for transfers between devices, across(): return lax.ppermute(x, ('core', 'half'), [(i, 3 - i) for i in range(4)])  2.75 us
    all_to_all x1, waiting for transfers between devices, local(): lax.all_to_all(copies, ('x', 'column'), split_axis=0, concat_axis=0, tile...  2.41 us
    pallas_call x1, Pallas kernels, local(): pl.pallas_call(functools.partial(pack_kernel, half_columns, gain), out_sh...  1.8 us
    pallas_call x2, Pallas kernels, second(): pl.pallas_call(functools.partial(second_kernel, half_columns, other), out...  1.64 us
    pallas_call x1, Pallas kernels, local(): pl.pallas_call(first_kernel, out_shape=jax.ShapeDtypeStruct((2, 2, row_de...  1.33 us
    add x1, other arithmetic, local(): return second(False) + from_partner  0.56 us
  transfers between devices with their start and end apart: 4, of which 4 were waited for; matrix products, arithmetic and copies ran while one was open for 0% of the time, Pallas kernels for 10%

profile of v11, /device:TPU:0, one launch (start us, length us, event | category | flops | bytes accessed | tf_op | source)
XLA Modules:
  0.0 21.4 jit_solution(11985630531785270015)
XLA Ops:
  0.0 1.8 %shard_map.64 = f32[8,4,1408]{2,1,0:T(4,128)} custom-call(s32[8]{0:T(128)} %bitcast.2, s32[8]{0:T(128)} %bitcast.3, f32[3,1024]{1,0:T(4,128)} %src_hbm.1, f32[2,1024]{1,0:T(2,128)} %cur_hbm.1, f32[8,2,16,128]{3,2,1,0:T(8,128)} %blocks_hbm.1), custom_call_target="tpu_custom_call" | custom-call | flops 1048576 | bytes 1048576 | tf_op jit(solution)/shard_map/pallas_call | solution.py:226
  1.8 0.0 copy-start
  1.8 6.2 %all-to-all-start = ((f32[8,4,1408]{2,1,0:T(4,128)}), f32[8,4,1408]{2,1,0:T(4,128)S(1)}, u32[]{:S(2)}, u32[]{:S(2)}) async-start(f32[8,4,1408]{2,1,0:T(4,128)} %shard_map.64), calls=%async_computation | async-start | bytes 360448 | tf_op jit(solution)/shard_map/all_to_all | solution.py:243
  8.0 0.0 copy-done
  8.0 1.8 %collective-permute-start = (f32[3,16]{1,0:T(4,128)S(1)}, f32[3,16]{1,0:T(4,128)S(1)}, u32[]{:S(2)}, u32[]{:S(2)}) collective-permute-start(f32[3,16]{1,0:T(4,128)S(1)} %copy-done), channel_id=1, source_target_pairs={{0,12},{4,8},{8,4},{12,0},{1,13},{5,9},{9,5},{13,1},{2,14},{6,10},... | collective-permute-start | bytes 584 | tf_op jit(solution)/shard_map/ppermute | solution.py:211
  9.8 2.3 %collective-permute-done.partner_ref = f32[3,16]{1,0:T(4,128)S(1)} collective-permute-done((f32[3,16]{1,0:T(4,128)S(1)}, f32[3,16]{1,0:T(4,128)S(1)}, u32[]{:S(2)}, u32[]{:S(2)}) %collective-permute-start) | collective-permute-done | bytes 224 | tf_op jit(solution)/shard_map/ppermute | solution.py:211
  12.1 0.1 shard_map.65.wide_ref
  12.2 2.4 %all-to-all-done.messages_ref = f32[8,4,1408]{2,1,0:T(4,128)S(1)} async-done(((f32[8,4,1408]{2,1,0:T(4,128)}), f32[8,4,1408]{2,1,0:T(4,128)S(1)}, u32[]{:S(2)}, u32[]{:S(2)}) %all-to-all-start) | async-done | bytes 180256 | tf_op jit(solution)/shard_map/all_to_all | solution.py:243
  14.6 0.0 collective-permute-start.1
  14.6 1.3 %shard_map.66.sums_ref = f32[2,2,16,128]{3,2,1,0:T(8,128)S(1)} custom-call(f32[2,3,16,128]{3,2,1,0:T(8,128)S(1)} %shard_map.65.wide_ref, f32[8,4,1408]{2,1,0:T(4,128)S(1)} %all-to-all-done.messages_ref), custom_call_target="tpu_custom_call" | custom-call | flops 10485760 | bytes 2097152 | tf_op jit(solution)/shard_map/pallas_call | solution.py:266
  15.9 0.1 collective-permute-done.1.sibling_ref
  16.0 0.8 %shard_map.68 = f32[2,16]{1,0:T(2,128)S(1)} custom-call(f32[2,3,16,128]{3,2,1,0:T(8,128)S(1)} %shard_map.65.wide_ref, f32[2,2,16,128]{3,2,1,0:T(8,128)S(1)} %shard_map.66.sums_ref, f32[8,4,1408]{2,1,0:T(4,128)S(1)} %all-to-all-done.messages_ref, f32[8,4,1408]{2,1,0:T(4,128)S(1)} %collective-permute-done.1.sibling_ref), custom_call_target="tpu_custom_call" | custom-call | flops 5242880 | bytes 2097152 | tf_op jit(solution)/shard_map/pallas_call | solution.py:275
  16.8 2.7 %collective-permute-start.2 = (f32[2,16]{1,0:T(2,128)S(1)}, f32[2,16]{1,0:T(2,128)S(1)}, u32[]{:S(2)}, u32[]{:S(2)}) collective-permute-start(f32[2,16]{1,0:T(2,128)S(1)} %shard_map.68), channel_id=1, source_target_pairs={{0,12},{4,8},{8,4},{12,0},{1,13},{5,9},{9,5},{13,1},{2,14},{6,10},... | collective-permute-start | bytes 392 | tf_op jit(solution)/shard_map/ppermute | solution.py:211
  19.5 0.8 %shard_map.67 = f32[2,16]{1,0:T(2,128)S(1)} custom-call(f32[2,3,16,128]{3,2,1,0:T(8,128)S(1)} %shard_map.65.wide_ref, f32[2,2,16,128]{3,2,1,0:T(8,128)S(1)} %shard_map.66.sums_ref, f32[8,4,1408]{2,1,0:T(4,128)S(1)} %all-to-all-done.messages_ref, f32[8,4,1408]{2,1,0:T(4,128)S(1)} %collective-permute-done.1.sibling_ref), custom_call_target="tpu_custom_call" | custom-call | flops 5242880 | bytes 2097152 | tf_op jit(solution)/shard_map/pallas_call | solution.py:275
  20.3 0.5 %collective-permute-done.2 = f32[2,16]{1,0:T(2,128)S(1)} collective-permute-done((f32[2,16]{1,0:T(2,128)S(1)}, f32[2,16]{1,0:T(2,128)S(1)}, u32[]{:S(2)}, u32[]{:S(2)}) %collective-permute-start.2) | collective-permute-done | bytes 160 | tf_op jit(solution)/shard_map/ppermute | solution.py:211
  20.8 0.6 %add.3 = f32[2,16]{1,0:T(2,128)} add(f32[2,16]{1,0:T(2,128)S(1)} %shard_map.67, f32[2,16]{1,0:T(2,128)S(1)} %collective-permute-done.2) | non-fusion elementwise | flops 32 | bytes 384 | tf_op jit(solution)/shard_map/add | solution.py:284
Async XLA Ops:
  1.8 6.2 %copy-start = (f32[3,16]{1,0:T(4,128)S(1)}, f32[3,16]{1,0:T(4,128)}, u32[]{:S(2)}) copy-start(f32[3,16]{1,0:T(4,128)} %tests_ref.1) | copy-start | bytes 580
  1.8 12.8 %all-to-all-start = ((f32[8,4,1408]{2,1,0:T(4,128)}), f32[8,4,1408]{2,1,0:T(4,128)S(1)}, u32[]{:S(2)}, u32[]{:S(2)}) async-start(f32[8,4,1408]{2,1,0:T(4,128)} %shard_map.64), calls=%async_computation | async-start | bytes 360448 | tf_op jit(solution)/shard_map/all_to_all | solution.py:243
  8.0 4.1 %collective-permute-start = (f32[3,16]{1,0:T(4,128)S(1)}, f32[3,16]{1,0:T(4,128)S(1)}, u32[]{:S(2)}, u32[]{:S(2)}) collective-permute-start(f32[3,16]{1,0:T(4,128)S(1)} %copy-done), channel_id=1, source_target_pairs={{0,12},{4,8},{8,4},{12,0},{1,13},{5,9},{9,5},{13,1},{2,14},{6,10},... | collective-permute-start | bytes 584 | tf_op jit(solution)/shard_map/ppermute | solution.py:211
  14.6 1.4 %collective-permute-start.1 = (f32[8,4,1408]{2,1,0:T(4,128)S(1)}, f32[8,4,1408]{2,1,0:T(4,128)S(1)}, u32[]{:S(2)}, u32[]{:S(2)}) collective-permute-start(f32[8,4,1408]{2,1,0:T(4,128)S(1)} %all-to-all-done.messages_ref), channel_id=1, source_target_pairs={{0,8},{8,0},{1,9},{9,1},{2,10},{10,2},{3,11},{11,3},{4,12},{12,4},... | collective-permute-start | bytes 540680 | tf_op jit(solution)/shard_map/ppermute | solution.py:265
  16.8 4.0 %collective-permute-start.2 = (f32[2,16]{1,0:T(2,128)S(1)}, f32[2,16]{1,0:T(2,128)S(1)}, u32[]{:S(2)}, u32[]{:S(2)}) collective-permute-start(f32[2,16]{1,0:T(2,128)S(1)} %shard_map.68), channel_id=1, source_target_pairs={{0,12},{4,8},{8,4},{12,0},{1,13},{5,9},{9,5},{13,1},{2,14},{6,10},... | collective-permute-start | bytes 392 | tf_op jit(solution)/shard_map/ppermute | solution.py:211

commit v12 on v11

--- a/solution.py
+++ b/solution.py
@@ -175,12 +175,17 @@
     return rows
 
 
-def near_of(half_columns, other, messages_ref):
+def near_of(half_columns, other, messages_ref, sibling_ref):
     last = messages_ref.shape[2] - LANES
     base = lax.axis_index("x") * half_columns
-    total = messages_ref[base, :, last:]
-    for k in range(1, half_columns):
-        total = total + messages_ref[base + k, :, last:]
+    middle = half_columns // 2
+    straight = crossed = jnp.zeros((QUAD, LANES), jnp.float32)
+    for k in range(half_columns):
+        own, sibling = messages_ref[base + k, :, last:], sibling_ref[base + k, :, last:]
+        straight = straight + (own if k < middle else sibling)
+        crossed = crossed + (sibling if k < middle else own)
+    upper = lax.axis_index("column") >= middle
+    total = jnp.where(upper, straight, crossed) if other else jnp.where(upper, crossed, straight)
     first = lax.axis_index("half") == (1 if other else 0)
     return jnp.where(first, total[0:1], total[1:2])
 
@@ -198,7 +203,7 @@
     row_dev = wide_ref.shape[2]
     which = 0 if other else 1
     tests = groups_of(wide_ref, which)
-    near = near_of(half_columns, other, sibling_ref if other else messages_ref)
+    near = near_of(half_columns, other, messages_ref, sibling_ref)
     sums = [
         (sums_ref[which, 0, pl.ds(g * SUB, SUB), :], sums_ref[which, 1, pl.ds(g * SUB, SUB), :]) for g in range(len(tests))
     ]
@@ -209,6 +214,17 @@
 
 def across(x):
     return lax.ppermute(x, ("core", "half"), [(i, 3 - i) for i in range(4)])
+
+
+def groups_for(xs, half_columns):
+    def place(x, core, half, column):
+        return ((x * 2 + core) * 2 + half) * half_columns + column
+
+    return [
+        [place(x, g ^ (column >= half_columns // 2), half, column) for x in range(xs) for column in range(half_columns)]
+        for half in range(2)
+        for g in range(2)
+    ]
 
 
 def local(rows, half_columns, test_points, src_points, currents, near_blocks, near_dest, near_tile):
@@ -240,7 +256,10 @@
         ],
         cost_estimate=pl.CostEstimate(flops=1 << 20, bytes_accessed=1 << 20, transcendentals=0),
     )(near_dest.reshape(-1), near_tile.reshape(-1), src_points, currents, near_blocks)
-    messages = lax.all_to_all(copies, ("x", "column"), split_axis=0, concat_axis=0, tiled=True)
+    messages = lax.all_to_all(
+        copies, ("x", "core", "half", "column"), split_axis=0, concat_axis=0, tiled=True,
+        axis_index_groups=groups_for(rows // 2, half_columns),
+    )
 
 
     evaluations = width * members * row_dev

time: 21.6 us -> 21.2 us (0.981)
  waiting for transfers between devices: 5.23 us -> 3.9 us
  starting transfers between devices: 10.7 us -> 11.6 us
    ppermute x2, starting transfers between devices: 4.49 us -> 5.25 us  [across(): return lax.ppermute(x, ('core', 'half'), [(i, 3 - i) for i in range(4)])]
    all_to_all x1, waiting for transfers between devices: 2.41 us -> 1.7 us  [local(): lax.all_to_all(copies, ('x', 'core', 'half', 'column'), split_axis=0, con...]
    ppermute x1, starting transfers between devices: 0.01 us -> 0.69 us  [local(): sibling = lax.ppermute(messages, 'core', [(0, 1), (1, 0)])]
    all_to_all x1, starting transfers between devices: 6.2 us -> 5.63 us  [local(): lax.all_to_all(copies, ('x', 'core', 'half', 'column'), split_axis=0, con...]
    ppermute x2, waiting for transfers between devices: 2.75 us -> 2.2 us  [across(): return lax.ppermute(x, ('core', 'half'), [(i, 3 - i) for i in range(4)])]
  transfers between devices with their start and end apart: 4 -> 4, of which waited for: 4 -> 3; matrix products, arithmetic and copies ran while one was open for 0% -> 0% of each run, Pallas kernels for 10% -> 11%
where the time goes in v12:
time: 21.2 us; the launch traced here: 20.9 us
  starting transfers between devices  11.6 us (55%)
  Pallas kernels  4.87 us (23%)
  waiting for transfers between devices  3.9 us (18%)
  other arithmetic  0.56 us (3%)
    all_to_all x1, starting transfers between devices, local(): lax.all_to_all(copies, ('x', 'core', 'half', 'column'), split_axis=0, con...  5.63 us
    ppermute x2, starting transfers between devices, across(): return lax.ppermute(x, ('core', 'half'), [(i, 3 - i) for i in range(4)])  5.25 us
    ppermute x2, waiting for transfers between devices, across(): return lax.ppermute(x, ('core', 'half'), [(i, 3 - i) for i in range(4)])  2.2 us
    pallas_call x1, Pallas kernels, local(): pl.pallas_call(functools.partial(pack_kernel, half_columns, gain), out_sh...  1.8 us
    all_to_all x1, waiting for transfers between devices, local(): lax.all_to_all(copies, ('x', 'core', 'half', 'column'), split_axis=0, con...  1.7 us
    pallas_call x2, Pallas kernels, second(): pl.pallas_call(functools.partial(second_kernel, half_columns, other), out...  1.65 us
    pallas_call x1, Pallas kernels, local(): pl.pallas_call(first_kernel, out_shape=jax.ShapeDtypeStruct((2, 2, row_de...  1.33 us
    ppermute x1, starting transfers between devices, local(): sibling = lax.ppermute(messages, 'core', [(0, 1), (1, 0)])  0.69 us
  transfers between devices with their start and end apart: 4, of which 3 were waited for; matrix products, arithmetic and copies ran while one was open for 0% of the time, Pallas kernels for 11%

profile of v12, /device:TPU:0, one launch (start us, length us, event | category | flops | bytes accessed | tf_op | source)
XLA Modules:
  0.0 20.9 jit_solution(18193683025340466477)
XLA Ops:
  0.0 1.8 %shard_map.64 = f32[8,4,1408]{2,1,0:T(4,128)} custom-call(s32[8]{0:T(128)} %bitcast.2, s32[8]{0:T(128)} %bitcast.3, f32[3,1024]{1,0:T(4,128)} %src_hbm.1, f32[2,1024]{1,0:T(2,128)} %cur_hbm.1, f32[8,2,16,128]{3,2,1,0:T(8,128)} %blocks_hbm.1), custom_call_target="tpu_custom_call" | custom-call | flops 1048576 | bytes 1048576 | tf_op jit(solution)/shard_map/pallas_call | solution.py:242
  1.8 0.0 copy-start
  1.8 5.6 %all-to-all-start = ((f32[8,4,1408]{2,1,0:T(4,128)}), f32[8,4,1408]{2,1,0:T(4,128)S(1)}, u32[]{:S(2)}, u32[]{:S(2)}) async-start(f32[8,4,1408]{2,1,0:T(4,128)} %shard_map.64), calls=%async_computation | async-start | bytes 360448 | tf_op jit(solution)/shard_map/all_to_all | solution.py:259
  7.5 0.0 copy-done
  7.5 2.9 %collective-permute-start = (f32[3,16]{1,0:T(4,128)S(1)}, f32[3,16]{1,0:T(4,128)S(1)}, u32[]{:S(2)}, u32[]{:S(2)}) collective-permute-start(f32[3,16]{1,0:T(4,128)S(1)} %copy-done), channel_id=1, source_target_pairs={{0,12},{4,8},{8,4},{12,0},{1,13},{5,9},{9,5},{13,1},{2,14},{6,10},... | collective-permute-start | bytes 584 | tf_op jit(solution)/shard_map/ppermute | solution.py:216
  10.4 1.4 %collective-permute-done.partner_ref = f32[3,16]{1,0:T(4,128)S(1)} collective-permute-done((f32[3,16]{1,0:T(4,128)S(1)}, f32[3,16]{1,0:T(4,128)S(1)}, u32[]{:S(2)}, u32[]{:S(2)}) %collective-permute-start) | collective-permute-done | bytes 224 | tf_op jit(solution)/shard_map/ppermute | solution.py:216
  11.8 0.1 shard_map.65.wide_ref
  11.8 1.7 %all-to-all-done.messages_ref = f32[8,4,1408]{2,1,0:T(4,128)S(1)} async-done(((f32[8,4,1408]{2,1,0:T(4,128)}), f32[8,4,1408]{2,1,0:T(4,128)S(1)}, u32[]{:S(2)}, u32[]{:S(2)}) %all-to-all-start) | async-done | bytes 180256 | tf_op jit(solution)/shard_map/all_to_all | solution.py:259
  13.5 0.7 %collective-permute-start.1 = (f32[8,4,1408]{2,1,0:T(4,128)S(1)}, f32[8,4,1408]{2,1,0:T(4,128)S(1)}, u32[]{:S(2)}, u32[]{:S(2)}) collective-permute-start(f32[8,4,1408]{2,1,0:T(4,128)S(1)} %all-to-all-done.messages_ref), channel_id=1, source_target_pairs={{0,8},{8,0},{1,9},{9,1},{2,10},{10,2},{3,11},{11,3},{4,12},{12,4},... | collective-permute-start | bytes 540680 | tf_op jit(solution)/shard_map/ppermute | solution.py:284
  14.2 1.3 %shard_map.66.sums_ref = f32[2,2,16,128]{3,2,1,0:T(8,128)S(1)} custom-call(f32[2,3,16,128]{3,2,1,0:T(8,128)S(1)} %shard_map.65.wide_ref, f32[8,4,1408]{2,1,0:T(4,128)S(1)} %all-to-all-done.messages_ref), custom_call_target="tpu_custom_call" | custom-call | flops 10485760 | bytes 2097152 | tf_op jit(solution)/shard_map/pallas_call | solution.py:285
  15.6 0.0 collective-permute-done.1.sibling_ref
  15.6 0.8 %shard_map.68 = f32[2,16]{1,0:T(2,128)S(1)} custom-call(f32[2,3,16,128]{3,2,1,0:T(8,128)S(1)} %shard_map.65.wide_ref, f32[2,2,16,128]{3,2,1,0:T(8,128)S(1)} %shard_map.66.sums_ref, f32[8,4,1408]{2,1,0:T(4,128)S(1)} %all-to-all-done.messages_ref, f32[8,4,1408]{2,1,0:T(4,128)S(1)} %collective-permute-done.1.sibling_ref), custom_call_target="tpu_custom_call" | custom-call | flops 5242880 | bytes 2097152 | tf_op jit(solution)/shard_map/pallas_call | solution.py:294
  16.4 2.3 %collective-permute-start.2 = (f32[2,16]{1,0:T(2,128)S(1)}, f32[2,16]{1,0:T(2,128)S(1)}, u32[]{:S(2)}, u32[]{:S(2)}) collective-permute-start(f32[2,16]{1,0:T(2,128)S(1)} %shard_map.68), channel_id=1, source_target_pairs={{0,12},{4,8},{8,4},{12,0},{1,13},{5,9},{9,5},{13,1},{2,14},{6,10},... | collective-permute-start | bytes 392 | tf_op jit(solution)/shard_map/ppermute | solution.py:216
  18.7 0.8 %shard_map.67 = f32[2,16]{1,0:T(2,128)S(1)} custom-call(f32[2,3,16,128]{3,2,1,0:T(8,128)S(1)} %shard_map.65.wide_ref, f32[2,2,16,128]{3,2,1,0:T(8,128)S(1)} %shard_map.66.sums_ref, f32[8,4,1408]{2,1,0:T(4,128)S(1)} %all-to-all-done.messages_ref, f32[8,4,1408]{2,1,0:T(4,128)S(1)} %collective-permute-done.1.sibling_ref), custom_call_target="tpu_custom_call" | custom-call | flops 5242880 | bytes 2097152 | tf_op jit(solution)/shard_map/pallas_call | solution.py:294
  19.5 0.8 %collective-permute-done.2 = f32[2,16]{1,0:T(2,128)S(1)} collective-permute-done((f32[2,16]{1,0:T(2,128)S(1)}, f32[2,16]{1,0:T(2,128)S(1)}, u32[]{:S(2)}, u32[]{:S(2)}) %collective-permute-start.2) | collective-permute-done | bytes 160 | tf_op jit(solution)/shard_map/ppermute | solution.py:216
  20.4 0.6 %add.3 = f32[2,16]{1,0:T(2,128)} add(f32[2,16]{1,0:T(2,128)S(1)} %shard_map.67, f32[2,16]{1,0:T(2,128)S(1)} %collective-permute-done.2) | non-fusion elementwise | flops 32 | bytes 384 | tf_op jit(solution)/shard_map/add | solution.py:303
Async XLA Ops:
  1.8 5.6 %copy-start = (f32[3,16]{1,0:T(4,128)S(1)}, f32[3,16]{1,0:T(4,128)}, u32[]{:S(2)}) copy-start(f32[3,16]{1,0:T(4,128)} %tests_ref.1) | copy-start | bytes 580
  1.8 11.7 %all-to-all-start = ((f32[8,4,1408]{2,1,0:T(4,128)}), f32[8,4,1408]{2,1,0:T(4,128)S(1)}, u32[]{:S(2)}, u32[]{:S(2)}) async-start(f32[8,4,1408]{2,1,0:T(4,128)} %shard_map.64), calls=%async_computation | async-start | bytes 360448 | tf_op jit(solution)/shard_map/all_to_all | solution.py:259
  7.5 4.3 %collective-permute-start = (f32[3,16]{1,0:T(4,128)S(1)}, f32[3,16]{1,0:T(4,128)S(1)}, u32[]{:S(2)}, u32[]{:S(2)}) collective-permute-start(f32[3,16]{1,0:T(4,128)S(1)} %copy-done), channel_id=1, source_target_pairs={{0,12},{4,8},{8,4},{12,0},{1,13},{5,9},{9,5},{13,1},{2,14},{6,10},... | collective-permute-start | bytes 584 | tf_op jit(solution)/shard_map/ppermute | solution.py:216
  13.5 2.0 %collective-permute-start.1 = (f32[8,4,1408]{2,1,0:T(4,128)S(1)}, f32[8,4,1408]{2,1,0:T(4,128)S(1)}, u32[]{:S(2)}, u32[]{:S(2)}) collective-permute-start(f32[8,4,1408]{2,1,0:T(4,128)S(1)} %all-to-all-done.messages_ref), channel_id=1, source_target_pairs={{0,8},{8,0},{1,9},{9,1},{2,10},{10,2},{3,11},{11,3},{4,12},{12,4},... | collective-permute-start | bytes 540680 | tf_op jit(solution)/shard_map/ppermute | solution.py:284
  16.4 4.0 %collective-permute-start.2 = (f32[2,16]{1,0:T(2,128)S(1)}, f32[2,16]{1,0:T(2,128)S(1)}, u32[]{:S(2)}, u32[]{:S(2)}) collective-permute-start(f32[2,16]{1,0:T(2,128)S(1)} %shard_map.68), channel_id=1, source_target_pairs={{0,12},{4,8},{8,4},{12,0},{1,13},{5,9},{9,5},{13,1},{2,14},{6,10},... | collective-permute-start | bytes 392 | tf_op jit(solution)/shard_map/ppermute | solution.py:216

commit v13 on v12

--- a/solution.py
+++ b/solution.py
@@ -53,22 +53,21 @@
     half_columns, gain, dest_hbm, tile_hbm, src_hbm, cur_hbm, blocks_hbm, copies_ref,
     dest_ref, tile_ref, src_ref, cur_ref, blocks_ref, message, near_all, sems
 ):
-    moves = [
-        pltpu.make_async_copy(source, target, sems.at[k])
-        for k, (source, target) in enumerate((
-            (src_hbm, src_ref), (cur_hbm, cur_ref), (blocks_hbm, blocks_ref), (dest_hbm, dest_ref), (tile_hbm, tile_ref)
-        ))
-    ]
+    items = blocks_ref.shape[0]
+    parts = [pl.ds(part * items // 2, items // 2) for part in range(2)]
+    pairs = [(blocks_hbm.at[part], blocks_ref.at[part]) for part in parts]
+    pairs += [(cur_hbm, cur_ref), (src_hbm, src_ref), (dest_hbm, dest_ref), (tile_hbm, tile_ref)]
+    moves = [pltpu.make_async_copy(source, target, sems.at[k]) for k, (source, target) in enumerate(pairs)]
     for move in moves:
         move.start()
     members = copies_ref.shape[0]
     tiles = src_ref.shape[1] // LANES
-    items, _, row_dev, _ = blocks_ref.shape
+    row_dev = blocks_ref.shape[2]
     columns = 2 * half_columns
     lane = lax.broadcasted_iota(jnp.int32, (SUB, LANES), 1)
     sub = lax.broadcasted_iota(jnp.int32, (SUB, LANES), 0)
-    moves[0].wait()
-    moves[1].wait()
+    moves[2].wait()
+    moves[3].wait()
 
     for tile in range(tiles):
         part = pl.ds(tile * LANES, LANES)
@@ -89,10 +88,12 @@
 
     lax.fori_loop(0, members, copy, 0, unroll=8)
 
-    for move in moves[2:]:
-        move.wait()
+    moves[4].wait()
+    moves[5].wait()
     near = [jnp.zeros((SUB, LANES), jnp.float32)] * (columns // SUB)
     for block in range(items):
+        if block % (items // 2) == 0:
+            moves[block // (items // 2)].wait()
         tile = pl.multiple_of(tile_ref[block] * LANES, LANES)
         cr = cur_ref[0:1, pl.ds(tile, LANES)]
         ci = cur_ref[1:2, pl.ds(tile, LANES)]
@@ -252,7 +253,7 @@
             pltpu.VMEM(near_blocks.shape, jnp.float32),
             pltpu.VMEM((5 * width // LANES, LANES), jnp.float32),
             pltpu.VMEM((2 * half_columns, LANES), jnp.float32),
-            pltpu.SemaphoreType.DMA((5,)),
+            pltpu.SemaphoreType.DMA((6,)),
         ],
         cost_estimate=pl.CostEstimate(flops=1 << 20, bytes_accessed=1 << 20, transcendentals=0),
     )(near_dest.reshape(-1), near_tile.reshape(-1), src_points, currents, near_blocks)

time: 21.2 us -> 21.2 us (level)
  no operation moved by 1% of the time
where the time goes in v13:
time: 21.2 us; the launch traced here: 21 us
  starting transfers between devices  11.6 us (55%)
  Pallas kernels  4.87 us (23%)
  waiting for transfers between devices  3.9 us (18%)
  other arithmetic  0.56 us (3%)
    all_to_all x1, starting transfers between devices, local(): lax.all_to_all(copies, ('x', 'core', 'half', 'column'), split_axis=0, con...  5.63 us
    ppermute x2, starting transfers between devices, across(): return lax.ppermute(x, ('core', 'half'), [(i, 3 - i) for i in range(4)])  5.25 us
    ppermute x2, waiting for transfers between devices, across(): return lax.ppermute(x, ('core', 'half'), [(i, 3 - i) for i in range(4)])  2.2 us
    pallas_call x1, Pallas kernels, local(): pl.pallas_call(functools.partial(pack_kernel, half_columns, gain), out_sh...  1.81 us
    all_to_all x1, waiting for transfers between devices, local(): lax.all_to_all(copies, ('x', 'core', 'half', 'column'), split_axis=0, con...  1.7 us
    pallas_call x2, Pallas kernels, second(): pl.pallas_call(functools.partial(second_kernel, half_columns, other), out...  1.65 us
    pallas_call x1, Pallas kernels, local(): pl.pallas_call(first_kernel, out_shape=jax.ShapeDtypeStruct((2, 2, row_de...  1.33 us
    ppermute x1, starting transfers between devices, local(): sibling = lax.ppermute(messages, 'core', [(0, 1), (1, 0)])  0.69 us
  transfers between devices with their start and end apart: 4, of which 3 were waited for; matrix products, arithmetic and copies ran while one was open for 0% of the time, Pallas kernels for 11%

profile of v13, /device:TPU:0, one launch (start us, length us, event | category | flops | bytes accessed | tf_op | source)
XLA Modules:
  0.0 21.0 jit_solution(9058510437774137329)
XLA Ops:
  0.0 1.8 %shard_map.64 = f32[8,4,1408]{2,1,0:T(4,128)} custom-call(s32[8]{0:T(128)} %bitcast.2, s32[8]{0:T(128)} %bitcast.3, f32[3,1024]{1,0:T(4,128)} %src_hbm.1, f32[2,1024]{1,0:T(2,128)} %cur_hbm.1, f32[8,2,16,128]{3,2,1,0:T(8,128)} %blocks_hbm.1), custom_call_target="tpu_custom_call" | custom-call | flops 1048576 | bytes 1048576 | tf_op jit(solution)/shard_map/pallas_call | solution.py:243
  1.8 0.0 copy-start
  1.8 5.6 %all-to-all-start = ((f32[8,4,1408]{2,1,0:T(4,128)}), f32[8,4,1408]{2,1,0:T(4,128)S(1)}, u32[]{:S(2)}, u32[]{:S(2)}) async-start(f32[8,4,1408]{2,1,0:T(4,128)} %shard_map.64), calls=%async_computation | async-start | bytes 360448 | tf_op jit(solution)/shard_map/all_to_all | solution.py:260
  7.5 0.0 copy-done
  7.5 2.9 %collective-permute-start = (f32[3,16]{1,0:T(4,128)S(1)}, f32[3,16]{1,0:T(4,128)S(1)}, u32[]{:S(2)}, u32[]{:S(2)}) collective-permute-start(f32[3,16]{1,0:T(4,128)S(1)} %copy-done), channel_id=1, source_target_pairs={{0,12},{4,8},{8,4},{12,0},{1,13},{5,9},{9,5},{13,1},{2,14},{6,10},... | collective-permute-start | bytes 584 | tf_op jit(solution)/shard_map/ppermute | solution.py:217
  10.4 1.4 %collective-permute-done.partner_ref = f32[3,16]{1,0:T(4,128)S(1)} collective-permute-done((f32[3,16]{1,0:T(4,128)S(1)}, f32[3,16]{1,0:T(4,128)S(1)}, u32[]{:S(2)}, u32[]{:S(2)}) %collective-permute-start) | collective-permute-done | bytes 224 | tf_op jit(solution)/shard_map/ppermute | solution.py:217
  11.8 0.1 shard_map.65.wide_ref
  11.9 1.7 %all-to-all-done.messages_ref = f32[8,4,1408]{2,1,0:T(4,128)S(1)} async-done(((f32[8,4,1408]{2,1,0:T(4,128)}), f32[8,4,1408]{2,1,0:T(4,128)S(1)}, u32[]{:S(2)}, u32[]{:S(2)}) %all-to-all-start) | async-done | bytes 180256 | tf_op jit(solution)/shard_map/all_to_all | solution.py:260
  13.6 0.7 %collective-permute-start.1 = (f32[8,4,1408]{2,1,0:T(4,128)S(1)}, f32[8,4,1408]{2,1,0:T(4,128)S(1)}, u32[]{:S(2)}, u32[]{:S(2)}) collective-permute-start(f32[8,4,1408]{2,1,0:T(4,128)S(1)} %all-to-all-done.messages_ref), channel_id=1, source_target_pairs={{0,8},{8,0},{1,9},{9,1},{2,10},{10,2},{3,11},{11,3},{4,12},{12,4},... | collective-permute-start | bytes 540680 | tf_op jit(solution)/shard_map/ppermute | solution.py:285
  14.2 1.3 %shard_map.66.sums_ref = f32[2,2,16,128]{3,2,1,0:T(8,128)S(1)} custom-call(f32[2,3,16,128]{3,2,1,0:T(8,128)S(1)} %shard_map.65.wide_ref, f32[8,4,1408]{2,1,0:T(4,128)S(1)} %all-to-all-done.messages_ref), custom_call_target="tpu_custom_call" | custom-call | flops 10485760 | bytes 2097152 | tf_op jit(solution)/shard_map/pallas_call | solution.py:286
  15.6 0.0 collective-permute-done.1.sibling_ref
  15.6 0.8 %shard_map.68 = f32[2,16]{1,0:T(2,128)S(1)} custom-call(f32[2,3,16,128]{3,2,1,0:T(8,128)S(1)} %shard_map.65.wide_ref, f32[2,2,16,128]{3,2,1,0:T(8,128)S(1)} %shard_map.66.sums_ref, f32[8,4,1408]{2,1,0:T(4,128)S(1)} %all-to-all-done.messages_ref, f32[8,4,1408]{2,1,0:T(4,128)S(1)} %collective-permute-done.1.sibling_ref), custom_call_target="tpu_custom_call" | custom-call | flops 5242880 | bytes 2097152 | tf_op jit(solution)/shard_map/pallas_call | solution.py:295
  16.4 2.3 %collective-permute-start.2 = (f32[2,16]{1,0:T(2,128)S(1)}, f32[2,16]{1,0:T(2,128)S(1)}, u32[]{:S(2)}, u32[]{:S(2)}) collective-permute-start(f32[2,16]{1,0:T(2,128)S(1)} %shard_map.68), channel_id=1, source_target_pairs={{0,12},{4,8},{8,4},{12,0},{1,13},{5,9},{9,5},{13,1},{2,14},{6,10},... | collective-permute-start | bytes 392 | tf_op jit(solution)/shard_map/ppermute | solution.py:217
  18.7 0.8 %shard_map.67 = f32[2,16]{1,0:T(2,128)S(1)} custom-call(f32[2,3,16,128]{3,2,1,0:T(8,128)S(1)} %shard_map.65.wide_ref, f32[2,2,16,128]{3,2,1,0:T(8,128)S(1)} %shard_map.66.sums_ref, f32[8,4,1408]{2,1,0:T(4,128)S(1)} %all-to-all-done.messages_ref, f32[8,4,1408]{2,1,0:T(4,128)S(1)} %collective-permute-done.1.sibling_ref), custom_call_target="tpu_custom_call" | custom-call | flops 5242880 | bytes 2097152 | tf_op jit(solution)/shard_map/pallas_call | solution.py:295
  19.6 0.8 %collective-permute-done.2 = f32[2,16]{1,0:T(2,128)S(1)} collective-permute-done((f32[2,16]{1,0:T(2,128)S(1)}, f32[2,16]{1,0:T(2,128)S(1)}, u32[]{:S(2)}, u32[]{:S(2)}) %collective-permute-start.2) | collective-permute-done | bytes 160 | tf_op jit(solution)/shard_map/ppermute | solution.py:217
  20.4 0.6 %add.3 = f32[2,16]{1,0:T(2,128)} add(f32[2,16]{1,0:T(2,128)S(1)} %shard_map.67, f32[2,16]{1,0:T(2,128)S(1)} %collective-permute-done.2) | non-fusion elementwise | flops 32 | bytes 384 | tf_op jit(solution)/shard_map/add | solution.py:304
Async XLA Ops:
  1.8 5.6 %copy-start = (f32[3,16]{1,0:T(4,128)S(1)}, f32[3,16]{1,0:T(4,128)}, u32[]{:S(2)}) copy-start(f32[3,16]{1,0:T(4,128)} %tests_ref.1) | copy-start | bytes 580
  1.8 11.7 %all-to-all-start = ((f32[8,4,1408]{2,1,0:T(4,128)}), f32[8,4,1408]{2,1,0:T(4,128)S(1)}, u32[]{:S(2)}, u32[]{:S(2)}) async-start(f32[8,4,1408]{2,1,0:T(4,128)} %shard_map.64), calls=%async_computation | async-start | bytes 360448 | tf_op jit(solution)/shard_map/all_to_all | solution.py:260
  7.5 4.3 %collective-permute-start = (f32[3,16]{1,0:T(4,128)S(1)}, f32[3,16]{1,0:T(4,128)S(1)}, u32[]{:S(2)}, u32[]{:S(2)}) collective-permute-start(f32[3,16]{1,0:T(4,128)S(1)} %copy-done), channel_id=1, source_target_pairs={{0,12},{4,8},{8,4},{12,0},{1,13},{5,9},{9,5},{13,1},{2,14},{6,10},... | collective-permute-start | bytes 584 | tf_op jit(solution)/shard_map/ppermute | solution.py:217
  13.6 2.0 %collective-permute-start.1 = (f32[8,4,1408]{2,1,0:T(4,128)S(1)}, f32[8,4,1408]{2,1,0:T(4,128)S(1)}, u32[]{:S(2)}, u32[]{:S(2)}) collective-permute-start(f32[8,4,1408]{2,1,0:T(4,128)S(1)} %all-to-all-done.messages_ref), channel_id=1, source_target_pairs={{0,8},{8,0},{1,9},{9,1},{2,10},{10,2},{3,11},{11,3},{4,12},{12,4},... | collective-permute-start | bytes 540680 | tf_op jit(solution)/shard_map/ppermute | solution.py:285
  16.4 4.0 %collective-permute-start.2 = (f32[2,16]{1,0:T(2,128)S(1)}, f32[2,16]{1,0:T(2,128)S(1)}, u32[]{:S(2)}, u32[]{:S(2)}) collective-permute-start(f32[2,16]{1,0:T(2,128)S(1)} %shard_map.68), channel_id=1, source_target_pairs={{0,12},{4,8},{8,4},{12,0},{1,13},{5,9},{9,5},{13,1},{2,14},{6,10},... | collective-permute-start | bytes 392 | tf_op jit(solution)/shard_map/ppermute | solution.py:217

commit v14 on v12

--- a/solution.py
+++ b/solution.py
@@ -175,6 +175,10 @@
     return rows
 
 
+def side_of(column, half_columns):
+    return (column // (half_columns // 2) + column % 2) % 2
+
+
 def near_of(half_columns, other, messages_ref, sibling_ref):
     last = messages_ref.shape[2] - LANES
     base = lax.axis_index("x") * half_columns
@@ -182,9 +186,11 @@
     straight = crossed = jnp.zeros((QUAD, LANES), jnp.float32)
     for k in range(half_columns):
         own, sibling = messages_ref[base + k, :, last:], sibling_ref[base + k, :, last:]
-        straight = straight + (own if k < middle else sibling)
-        crossed = crossed + (sibling if k < middle else own)
-    upper = lax.axis_index("column") >= middle
+        side = side_of(k, half_columns)
+        straight = straight + (sibling if side else own)
+        crossed = crossed + (own if side else sibling)
+    column = lax.axis_index("column")
+    upper = (column // middle + column % 2) % 2 == 1
     total = jnp.where(upper, straight, crossed) if other else jnp.where(upper, crossed, straight)
     first = lax.axis_index("half") == (1 if other else 0)
     return jnp.where(first, total[0:1], total[1:2])
@@ -221,7 +227,7 @@
         return ((x * 2 + core) * 2 + half) * half_columns + column
 
     return [
-        [place(x, g ^ (column >= half_columns // 2), half, column) for x in range(xs) for column in range(half_columns)]
+        [place(x, g ^ side_of(column, half_columns), half, column) for x in range(xs) for column in range(half_columns)]
         for half in range(2)
         for g in range(2)
     ]

time: 21.2 us -> 21.7 us (1.024)
  waiting for transfers between devices: 3.9 us -> 5.22 us
  starting transfers between devices: 11.6 us -> 10.7 us
    ppermute x2, starting transfers between devices: 5.25 us -> 4.51 us  [across(): return lax.ppermute(x, ('core', 'half'), [(i, 3 - i) for i in range(4)])]
    all_to_all x1, waiting for transfers between devices: 1.7 us -> 2.4 us  [local(): lax.all_to_all(copies, ('x', 'core', 'half', 'column'), split_axis=0, con...]
    ppermute x1, starting transfers between devices: 0.69 us -> 0.01 us  [local(): sibling = lax.ppermute(messages, 'core', [(0, 1), (1, 0)])]
    all_to_all x1, starting transfers between devices: 5.63 us -> 6.2 us  [local(): lax.all_to_all(copies, ('x', 'core', 'half', 'column'), split_axis=0, con...]
    ppermute x2, waiting for transfers between devices: 2.2 us -> 2.74 us  [across(): return lax.ppermute(x, ('core', 'half'), [(i, 3 - i) for i in range(4)])]
  transfers between devices with their start and end apart: 4 -> 4, of which waited for: 3 -> 4; matrix products, arithmetic and copies ran while one was open for 0% -> 0% of each run, Pallas kernels for 11% -> 10%
where the time goes in v14:
time: 21.7 us; the launch traced here: 21.4 us
  starting transfers between devices  10.7 us (49%)
  waiting for transfers between devices  5.22 us (24%)
  Pallas kernels  4.85 us (22%)
  other arithmetic  0.56 us (3%)
    all_to_all x1, starting transfers between devices, local(): lax.all_to_all(copies, ('x', 'core', 'half', 'column'), split_axis=0, con...  6.2 us
    ppermute x2, starting transfers between devices, across(): return lax.ppermute(x, ('core', 'half'), [(i, 3 - i) for i in range(4)])  4.51 us
    ppermute x2, waiting for transfers between devices, across(): return lax.ppermute(x, ('core', 'half'), [(i, 3 - i) for i in range(4)])  2.74 us
    all_to_all x1, waiting for transfers between devices, local(): lax.all_to_all(copies, ('x', 'core', 'half', 'column'), split_axis=0, con...  2.4 us
    pallas_call x1, Pallas kernels, local(): pl.pallas_call(functools.partial(pack_kernel, half_columns, gain), out_sh...  1.8 us
    pallas_call x2, Pallas kernels, second(): pl.pallas_call(functools.partial(second_kernel, half_columns, other), out...  1.64 us
    pallas_call x1, Pallas kernels, local(): pl.pallas_call(first_kernel, out_shape=jax.ShapeDtypeStruct((2, 2, row_de...  1.33 us
    add x1, other arithmetic, local(): return second(False) + from_partner  0.56 us
  transfers between devices with their start and end apart: 4, of which 4 were waited for; matrix products, arithmetic and copies ran while one was open for 0% of the time, Pallas kernels for 10%

profile of v14, /device:TPU:0, one launch (start us, length us, event | category | flops | bytes accessed | tf_op | source)
XLA Modules:
  0.0 21.4 jit_solution(2023787116185539318)
XLA Ops:
  0.0 1.8 %shard_map.64 = f32[8,4,1408]{2,1,0:T(4,128)} custom-call(s32[8]{0:T(128)} %bitcast.2, s32[8]{0:T(128)} %bitcast.3, f32[3,1024]{1,0:T(4,128)} %src_hbm.1, f32[2,1024]{1,0:T(2,128)} %cur_hbm.1, f32[8,2,16,128]{3,2,1,0:T(8,128)} %blocks_hbm.1), custom_call_target="tpu_custom_call" | custom-call | flops 1048576 | bytes 1048576 | tf_op jit(solution)/shard_map/pallas_call | solution.py:248
  1.8 0.0 copy-start
  1.8 6.2 %all-to-all-start = ((f32[8,4,1408]{2,1,0:T(4,128)}), f32[8,4,1408]{2,1,0:T(4,128)S(1)}, u32[]{:S(2)}, u32[]{:S(2)}) async-start(f32[8,4,1408]{2,1,0:T(4,128)} %shard_map.64), calls=%async_computation | async-start | bytes 360448 | tf_op jit(solution)/shard_map/all_to_all | solution.py:265
  8.0 0.0 copy-done
  8.0 1.8 %collective-permute-start = (f32[3,16]{1,0:T(4,128)S(1)}, f32[3,16]{1,0:T(4,128)S(1)}, u32[]{:S(2)}, u32[]{:S(2)}) collective-permute-start(f32[3,16]{1,0:T(4,128)S(1)} %copy-done), channel_id=1, source_target_pairs={{0,12},{4,8},{8,4},{12,0},{1,13},{5,9},{9,5},{13,1},{2,14},{6,10},... | collective-permute-start | bytes 584 | tf_op jit(solution)/shard_map/ppermute | solution.py:222
  9.8 2.3 %collective-permute-done.partner_ref = f32[3,16]{1,0:T(4,128)S(1)} collective-permute-done((f32[3,16]{1,0:T(4,128)S(1)}, f32[3,16]{1,0:T(4,128)S(1)}, u32[]{:S(2)}, u32[]{:S(2)}) %collective-permute-start) | collective-permute-done | bytes 224 | tf_op jit(solution)/shard_map/ppermute | solution.py:222
  12.1 0.1 shard_map.65.wide_ref
  12.2 2.4 %all-to-all-done.messages_ref = f32[8,4,1408]{2,1,0:T(4,128)S(1)} async-done(((f32[8,4,1408]{2,1,0:T(4,128)}), f32[8,4,1408]{2,1,0:T(4,128)S(1)}, u32[]{:S(2)}, u32[]{:S(2)}) %all-to-all-start) | async-done | bytes 180256 | tf_op jit(solution)/shard_map/all_to_all | solution.py:265
  14.6 0.0 collective-permute-start.1
  14.6 1.3 %shard_map.66.sums_ref = f32[2,2,16,128]{3,2,1,0:T(8,128)S(1)} custom-call(f32[2,3,16,128]{3,2,1,0:T(8,128)S(1)} %shard_map.65.wide_ref, f32[8,4,1408]{2,1,0:T(4,128)S(1)} %all-to-all-done.messages_ref), custom_call_target="tpu_custom_call" | custom-call | flops 10485760 | bytes 2097152 | tf_op jit(solution)/shard_map/pallas_call | solution.py:291
  15.9 0.1 collective-permute-done.1.sibling_ref
  16.0 0.8 %shard_map.68 = f32[2,16]{1,0:T(2,128)S(1)} custom-call(f32[2,3,16,128]{3,2,1,0:T(8,128)S(1)} %shard_map.65.wide_ref, f32[2,2,16,128]{3,2,1,0:T(8,128)S(1)} %shard_map.66.sums_ref, f32[8,4,1408]{2,1,0:T(4,128)S(1)} %all-to-all-done.messages_ref, f32[8,4,1408]{2,1,0:T(4,128)S(1)} %collective-permute-done.1.sibling_ref), custom_call_target="tpu_custom_call" | custom-call | flops 5242880 | bytes 2097152 | tf_op jit(solution)/shard_map/pallas_call | solution.py:300
  16.8 2.7 %collective-permute-start.2 = (f32[2,16]{1,0:T(2,128)S(1)}, f32[2,16]{1,0:T(2,128)S(1)}, u32[]{:S(2)}, u32[]{:S(2)}) collective-permute-start(f32[2,16]{1,0:T(2,128)S(1)} %shard_map.68), channel_id=1, source_target_pairs={{0,12},{4,8},{8,4},{12,0},{1,13},{5,9},{9,5},{13,1},{2,14},{6,10},... | collective-permute-start | bytes 392 | tf_op jit(solution)/shard_map/ppermute | solution.py:222
  19.5 0.8 %shard_map.67 = f32[2,16]{1,0:T(2,128)S(1)} custom-call(f32[2,3,16,128]{3,2,1,0:T(8,128)S(1)} %shard_map.65.wide_ref, f32[2,2,16,128]{3,2,1,0:T(8,128)S(1)} %shard_map.66.sums_ref, f32[8,4,1408]{2,1,0:T(4,128)S(1)} %all-to-all-done.messages_ref, f32[8,4,1408]{2,1,0:T(4,128)S(1)} %collective-permute-done.1.sibling_ref), custom_call_target="tpu_custom_call" | custom-call | flops 5242880 | bytes 2097152 | tf_op jit(solution)/shard_map/pallas_call | solution.py:300
  20.3 0.5 %collective-permute-done.2 = f32[2,16]{1,0:T(2,128)S(1)} collective-permute-done((f32[2,16]{1,0:T(2,128)S(1)}, f32[2,16]{1,0:T(2,128)S(1)}, u32[]{:S(2)}, u32[]{:S(2)}) %collective-permute-start.2) | collective-permute-done | bytes 160 | tf_op jit(solution)/shard_map/ppermute | solution.py:222
  20.8 0.6 %add.3 = f32[2,16]{1,0:T(2,128)} add(f32[2,16]{1,0:T(2,128)S(1)} %shard_map.67, f32[2,16]{1,0:T(2,128)S(1)} %collective-permute-done.2) | non-fusion elementwise | flops 32 | bytes 384 | tf_op jit(solution)/shard_map/add | solution.py:309
Async XLA Ops:
  1.8 6.2 %copy-start = (f32[3,16]{1,0:T(4,128)S(1)}, f32[3,16]{1,0:T(4,128)}, u32[]{:S(2)}) copy-start(f32[3,16]{1,0:T(4,128)} %tests_ref.1) | copy-start | bytes 580
  1.8 12.8 %all-to-all-start = ((f32[8,4,1408]{2,1,0:T(4,128)}), f32[8,4,1408]{2,1,0:T(4,128)S(1)}, u32[]{:S(2)}, u32[]{:S(2)}) async-start(f32[8,4,1408]{2,1,0:T(4,128)} %shard_map.64), calls=%async_computation | async-start | bytes 360448 | tf_op jit(solution)/shard_map/all_to_all | solution.py:265
  8.0 4.1 %collective-permute-start = (f32[3,16]{1,0:T(4,128)S(1)}, f32[3,16]{1,0:T(4,128)S(1)}, u32[]{:S(2)}, u32[]{:S(2)}) collective-permute-start(f32[3,16]{1,0:T(4,128)S(1)} %copy-done), channel_id=1, source_target_pairs={{0,12},{4,8},{8,4},{12,0},{1,13},{5,9},{9,5},{13,1},{2,14},{6,10},... | collective-permute-start | bytes 584 | tf_op jit(solution)/shard_map/ppermute | solution.py:222
  14.6 1.4 %collective-permute-start.1 = (f32[8,4,1408]{2,1,0:T(4,128)S(1)}, f32[8,4,1408]{2,1,0:T(4,128)S(1)}, u32[]{:S(2)}, u32[]{:S(2)}) collective-permute-start(f32[8,4,1408]{2,1,0:T(4,128)S(1)} %all-to-all-done.messages_ref), channel_id=1, source_target_pairs={{0,8},{8,0},{1,9},{9,1},{2,10},{10,2},{3,11},{11,3},{4,12},{12,4},... | collective-permute-start | bytes 540680 | tf_op jit(solution)/shard_map/ppermute | solution.py:290
  16.8 4.0 %collective-permute-start.2 = (f32[2,16]{1,0:T(2,128)S(1)}, f32[2,16]{1,0:T(2,128)S(1)}, u32[]{:S(2)}, u32[]{:S(2)}) collective-permute-start(f32[2,16]{1,0:T(2,128)S(1)} %shard_map.68), channel_id=1, source_target_pairs={{0,12},{4,8},{8,4},{12,0},{1,13},{5,9},{9,5},{13,1},{2,14},{6,10},... | collective-permute-start | bytes 392 | tf_op jit(solution)/shard_map/ppermute | solution.py:222

commit v15 on v14

--- a/solution.py
+++ b/solution.py
@@ -175,22 +175,20 @@
     return rows
 
 
-def side_of(column, half_columns):
-    return (column // (half_columns // 2) + column % 2) % 2
+def side_of(column):
+    return column % 2
 
 
 def near_of(half_columns, other, messages_ref, sibling_ref):
     last = messages_ref.shape[2] - LANES
     base = lax.axis_index("x") * half_columns
-    middle = half_columns // 2
     straight = crossed = jnp.zeros((QUAD, LANES), jnp.float32)
     for k in range(half_columns):
         own, sibling = messages_ref[base + k, :, last:], sibling_ref[base + k, :, last:]
-        side = side_of(k, half_columns)
+        side = side_of(k)
         straight = straight + (sibling if side else own)
         crossed = crossed + (own if side else sibling)
-    column = lax.axis_index("column")
-    upper = (column // middle + column % 2) % 2 == 1
+    upper = side_of(lax.axis_index("column")) == 1
     total = jnp.where(upper, straight, crossed) if other else jnp.where(upper, crossed, straight)
     first = lax.axis_index("half") == (1 if other else 0)
     return jnp.where(first, total[0:1], total[1:2])
@@ -227,7 +225,7 @@
         return ((x * 2 + core) * 2 + half) * half_columns + column
 
     return [
-        [place(x, g ^ side_of(column, half_columns), half, column) for x in range(xs) for column in range(half_columns)]
+        [place(x, g ^ side_of(column), half, column) for x in range(xs) for column in range(half_columns)]
         for half in range(2)
         for g in range(2)
     ]

time: 21.7 us -> 21.2 us (0.977)
  waiting for transfers between devices: 5.22 us -> 4.16 us
  starting transfers between devices: 10.7 us -> 11.3 us
    ppermute x2, starting transfers between devices: 4.51 us -> 5.25 us  [across(): return lax.ppermute(x, ('core', 'half'), [(i, 3 - i) for i in range(4)])]
    all_to_all x1, starting transfers between devices: 6.2 us -> 5.63 us  [local(): lax.all_to_all(copies, ('x', 'core', 'half', 'column'), split_axis=0, con...]
    ppermute x2, waiting for transfers between devices: 2.74 us -> 2.2 us  [across(): return lax.ppermute(x, ('core', 'half'), [(i, 3 - i) for i in range(4)])]
    all_to_all x1, waiting for transfers between devices: 2.4 us -> 1.95 us  [local(): lax.all_to_all(copies, ('x', 'core', 'half', 'column'), split_axis=0, con...]
    ppermute x1, starting transfers between devices: 0.01 us -> 0.44 us  [local(): sibling = lax.ppermute(messages, 'core', [(0, 1), (1, 0)])]
  transfers between devices with their start and end apart: 4 -> 4, of which waited for: 4 -> 3; matrix products, arithmetic and copies ran while one was open for 0% -> 0% of each run, Pallas kernels for 10% -> 11%
where the time goes in v15:
time: 21.2 us; the launch traced here: 21 us
  starting transfers between devices  11.3 us (53%)
  Pallas kernels  4.87 us (23%)
  waiting for transfers between devices  4.16 us (20%)
  other arithmetic  0.56 us (3%)
    all_to_all x1, starting transfers between devices, local(): lax.all_to_all(copies, ('x', 'core', 'half', 'column'), split_axis=0, con...  5.63 us
    ppermute x2, starting transfers between devices, across(): return lax.ppermute(x, ('core', 'half'), [(i, 3 - i) for i in range(4)])  5.25 us
    ppermute x2, waiting for transfers between devices, across(): return lax.ppermute(x, ('core', 'half'), [(i, 3 - i) for i in range(4)])  2.2 us
    all_to_all x1, waiting for transfers between devices, local(): lax.all_to_all(copies, ('x', 'core', 'half', 'column'), split_axis=0, con...  1.95 us
    pallas_call x1, Pallas kernels, local(): pl.pallas_call(functools.partial(pack_kernel, half_columns, gain), out_sh...  1.8 us
    pallas_call x2, Pallas kernels, second(): pl.pallas_call(functools.partial(second_kernel, half_columns, other), out...  1.66 us
    pallas_call x1, Pallas kernels, local(): pl.pallas_call(first_kernel, out_shape=jax.ShapeDtypeStruct((2, 2, row_de...  1.33 us
    add x1, other arithmetic, local(): return second(False) + from_partner  0.56 us
  transfers between devices with their start and end apart: 4, of which 3 were waited for; matrix products, arithmetic and copies ran while one was open for 0% of the time, Pallas kernels for 11%

profile of v15, /device:TPU:0, one launch (start us, length us, event | category | flops | bytes accessed | tf_op | source)
XLA Modules:
  0.0 21.0 jit_solution(7073187186851737661)
XLA Ops:
  0.0 1.8 %shard_map.64 = f32[8,4,1408]{2,1,0:T(4,128)} custom-call(s32[8]{0:T(128)} %bitcast.2, s32[8]{0:T(128)} %bitcast.3, f32[3,1024]{1,0:T(4,128)} %src_hbm.1, f32[2,1024]{1,0:T(2,128)} %cur_hbm.1, f32[8,2,16,128]{3,2,1,0:T(8,128)} %blocks_hbm.1), custom_call_target="tpu_custom_call" | custom-call | flops 1048576 | bytes 1048576 | tf_op jit(solution)/shard_map/pallas_call | solution.py:246
  1.8 0.0 copy-start
  1.8 5.6 %all-to-all-start = ((f32[8,4,1408]{2,1,0:T(4,128)}), f32[8,4,1408]{2,1,0:T(4,128)S(1)}, u32[]{:S(2)}, u32[]{:S(2)}) async-start(f32[8,4,1408]{2,1,0:T(4,128)} %shard_map.64), calls=%async_computation | async-start | bytes 360448 | tf_op jit(solution)/shard_map/all_to_all | solution.py:263
  7.5 0.0 copy-done
  7.5 2.9 %collective-permute-start = (f32[3,16]{1,0:T(4,128)S(1)}, f32[3,16]{1,0:T(4,128)S(1)}, u32[]{:S(2)}, u32[]{:S(2)}) collective-permute-start(f32[3,16]{1,0:T(4,128)S(1)} %copy-done), channel_id=1, source_target_pairs={{0,12},{4,8},{8,4},{12,0},{1,13},{5,9},{9,5},{13,1},{2,14},{6,10},... | collective-permute-start | bytes 584 | tf_op jit(solution)/shard_map/ppermute | solution.py:220
  10.4 1.4 %collective-permute-done.partner_ref = f32[3,16]{1,0:T(4,128)S(1)} collective-permute-done((f32[3,16]{1,0:T(4,128)S(1)}, f32[3,16]{1,0:T(4,128)S(1)}, u32[]{:S(2)}, u32[]{:S(2)}) %collective-permute-start) | collective-permute-done | bytes 224 | tf_op jit(solution)/shard_map/ppermute | solution.py:220
  11.8 0.1 shard_map.65.wide_ref
  11.8 2.0 %all-to-all-done.messages_ref = f32[8,4,1408]{2,1,0:T(4,128)S(1)} async-done(((f32[8,4,1408]{2,1,0:T(4,128)}), f32[8,4,1408]{2,1,0:T(4,128)S(1)}, u32[]{:S(2)}, u32[]{:S(2)}) %all-to-all-start) | async-done | bytes 180256 | tf_op jit(solution)/shard_map/all_to_all | solution.py:263
  13.8 0.4 %collective-permute-start.1 = (f32[8,4,1408]{2,1,0:T(4,128)S(1)}, f32[8,4,1408]{2,1,0:T(4,128)S(1)}, u32[]{:S(2)}, u32[]{:S(2)}) collective-permute-start(f32[8,4,1408]{2,1,0:T(4,128)S(1)} %all-to-all-done.messages_ref), channel_id=1, source_target_pairs={{0,8},{8,0},{1,9},{9,1},{2,10},{10,2},{3,11},{11,3},{4,12},{12,4},... | collective-permute-start | bytes 540680 | tf_op jit(solution)/shard_map/ppermute | solution.py:288
  14.2 1.3 %shard_map.66.sums_ref = f32[2,2,16,128]{3,2,1,0:T(8,128)S(1)} custom-call(f32[2,3,16,128]{3,2,1,0:T(8,128)S(1)} %shard_map.65.wide_ref, f32[8,4,1408]{2,1,0:T(4,128)S(1)} %all-to-all-done.messages_ref), custom_call_target="tpu_custom_call" | custom-call | flops 10485760 | bytes 2097152 | tf_op jit(solution)/shard_map/pallas_call | solution.py:289
  15.6 0.0 collective-permute-done.1.sibling_ref
  15.6 0.8 %shard_map.68 = f32[2,16]{1,0:T(2,128)S(1)} custom-call(f32[2,3,16,128]{3,2,1,0:T(8,128)S(1)} %shard_map.65.wide_ref, f32[2,2,16,128]{3,2,1,0:T(8,128)S(1)} %shard_map.66.sums_ref, f32[8,4,1408]{2,1,0:T(4,128)S(1)} %all-to-all-done.messages_ref, f32[8,4,1408]{2,1,0:T(4,128)S(1)} %collective-permute-done.1.sibling_ref), custom_call_target="tpu_custom_call" | custom-call | flops 5242880 | bytes 2097152 | tf_op jit(solution)/shard_map/pallas_call | solution.py:298
  16.4 2.3 %collective-permute-start.2 = (f32[2,16]{1,0:T(2,128)S(1)}, f32[2,16]{1,0:T(2,128)S(1)}, u32[]{:S(2)}, u32[]{:S(2)}) collective-permute-start(f32[2,16]{1,0:T(2,128)S(1)} %shard_map.68), channel_id=1, source_target_pairs={{0,12},{4,8},{8,4},{12,0},{1,13},{5,9},{9,5},{13,1},{2,14},{6,10},... | collective-permute-start | bytes 392 | tf_op jit(solution)/shard_map/ppermute | solution.py:220
  18.7 0.8 %shard_map.67 = f32[2,16]{1,0:T(2,128)S(1)} custom-call(f32[2,3,16,128]{3,2,1,0:T(8,128)S(1)} %shard_map.65.wide_ref, f32[2,2,16,128]{3,2,1,0:T(8,128)S(1)} %shard_map.66.sums_ref, f32[8,4,1408]{2,1,0:T(4,128)S(1)} %all-to-all-done.messages_ref, f32[8,4,1408]{2,1,0:T(4,128)S(1)} %collective-permute-done.1.sibling_ref), custom_call_target="tpu_custom_call" | custom-call | flops 5242880 | bytes 2097152 | tf_op jit(solution)/shard_map/pallas_call | solution.py:298
  19.6 0.8 %collective-permute-done.2 = f32[2,16]{1,0:T(2,128)S(1)} collective-permute-done((f32[2,16]{1,0:T(2,128)S(1)}, f32[2,16]{1,0:T(2,128)S(1)}, u32[]{:S(2)}, u32[]{:S(2)}) %collective-permute-start.2) | collective-permute-done | bytes 160 | tf_op jit(solution)/shard_map/ppermute | solution.py:220
  20.4 0.6 %add.3 = f32[2,16]{1,0:T(2,128)} add(f32[2,16]{1,0:T(2,128)S(1)} %shard_map.67, f32[2,16]{1,0:T(2,128)S(1)} %collective-permute-done.2) | non-fusion elementwise | flops 32 | bytes 384 | tf_op jit(solution)/shard_map/add | solution.py:307
Async XLA Ops:
  1.8 5.6 %copy-start = (f32[3,16]{1,0:T(4,128)S(1)}, f32[3,16]{1,0:T(4,128)}, u32[]{:S(2)}) copy-start(f32[3,16]{1,0:T(4,128)} %tests_ref.1) | copy-start | bytes 580
  1.8 12.0 %all-to-all-start = ((f32[8,4,1408]{2,1,0:T(4,128)}), f32[8,4,1408]{2,1,0:T(4,128)S(1)}, u32[]{:S(2)}, u32[]{:S(2)}) async-start(f32[8,4,1408]{2,1,0:T(4,128)} %shard_map.64), calls=%async_computation | async-start | bytes 360448 | tf_op jit(solution)/shard_map/all_to_all | solution.py:263
  7.5 4.3 %collective-permute-start = (f32[3,16]{1,0:T(4,128)S(1)}, f32[3,16]{1,0:T(4,128)S(1)}, u32[]{:S(2)}, u32[]{:S(2)}) collective-permute-start(f32[3,16]{1,0:T(4,128)S(1)} %copy-done), channel_id=1, source_target_pairs={{0,12},{4,8},{8,4},{12,0},{1,13},{5,9},{9,5},{13,1},{2,14},{6,10},... | collective-permute-start | bytes 584 | tf_op jit(solution)/shard_map/ppermute | solution.py:220
  13.8 1.8 %collective-permute-start.1 = (f32[8,4,1408]{2,1,0:T(4,128)S(1)}, f32[8,4,1408]{2,1,0:T(4,128)S(1)}, u32[]{:S(2)}, u32[]{:S(2)}) collective-permute-start(f32[8,4,1408]{2,1,0:T(4,128)S(1)} %all-to-all-done.messages_ref), channel_id=1, source_target_pairs={{0,8},{8,0},{1,9},{9,1},{2,10},{10,2},{3,11},{11,3},{4,12},{12,4},... | collective-permute-start | bytes 540680 | tf_op jit(solution)/shard_map/ppermute | solution.py:288
  16.4 4.0 %collective-permute-start.2 = (f32[2,16]{1,0:T(2,128)S(1)}, f32[2,16]{1,0:T(2,128)S(1)}, u32[]{:S(2)}, u32[]{:S(2)}) collective-permute-start(f32[2,16]{1,0:T(2,128)S(1)} %shard_map.68), channel_id=1, source_target_pairs={{0,12},{4,8},{8,4},{12,0},{1,13},{5,9},{9,5},{13,1},{2,14},{6,10},... | collective-permute-start | bytes 392 | tf_op jit(solution)/shard_map/ppermute | solution.py:220

commit v16 on v12

--- a/solution.py
+++ b/solution.py
@@ -110,10 +110,10 @@
     for group in range(columns // SUB):
         near_all[pl.ds(group * SUB, SUB), :] = near[group]
 
-    base = lax.axis_index("x") * half_columns
+    xs = members // half_columns
     for k in range(half_columns):
         for half in range(2):
-            copies_ref[base + k, half : half + 1, last:] = near_all[half * half_columns + k : half * half_columns + k + 1, :]
+            copies_ref[k * xs + lax.axis_index("x"), half : half + 1, last:] = near_all[half * half_columns + k : half * half_columns + k + 1, :]
 
 
 def points_kernel(partner_ref, tests_ref, wide_ref):
@@ -177,11 +177,12 @@
 
 def near_of(half_columns, other, messages_ref, sibling_ref):
     last = messages_ref.shape[2] - LANES
-    base = lax.axis_index("x") * half_columns
+    xs = messages_ref.shape[0] // half_columns
     middle = half_columns // 2
     straight = crossed = jnp.zeros((QUAD, LANES), jnp.float32)
     for k in range(half_columns):
-        own, sibling = messages_ref[base + k, :, last:], sibling_ref[base + k, :, last:]
+        member = k * xs + lax.axis_index("x")
+        own, sibling = messages_ref[member, :, last:], sibling_ref[member, :, last:]
         straight = straight + (own if k < middle else sibling)
         crossed = crossed + (sibling if k < middle else own)
     upper = lax.axis_index("column") >= middle
@@ -221,7 +222,7 @@
         return ((x * 2 + core) * 2 + half) * half_columns + column
 
     return [
-        [place(x, g ^ (column >= half_columns // 2), half, column) for x in range(xs) for column in range(half_columns)]
+        [place(x, g ^ (column >= half_columns // 2), half, column) for column in range(half_columns) for x in range(xs)]
         for half in range(2)
         for g in range(2)
     ]

time: 21.2 us -> 21 us (level)
  no operation moved by 1% of the time
where the time goes in v16:
time: 21 us; the launch traced here: 20.7 us
  starting transfers between devices  11.4 us (54%)
  Pallas kernels  4.87 us (23%)
  waiting for transfers between devices  3.82 us (18%)
  other arithmetic  0.56 us (3%)
    all_to_all x1, starting transfers between devices, local(): lax.all_to_all(copies, ('x', 'core', 'half', 'column'), split_axis=0, con...  5.63 us
    ppermute x2, starting transfers between devices, across(): return lax.ppermute(x, ('core', 'half'), [(i, 3 - i) for i in range(4)])  5.26 us
    ppermute x2, waiting for transfers between devices, across(): return lax.ppermute(x, ('core', 'half'), [(i, 3 - i) for i in range(4)])  2.19 us
    pallas_call x1, Pallas kernels, local(): pl.pallas_call(functools.partial(pack_kernel, half_columns, gain), out_sh...  1.8 us
    pallas_call x2, Pallas kernels, second(): pl.pallas_call(functools.partial(second_kernel, half_columns, other), out...  1.65 us
    all_to_all x1, waiting for transfers between devices, local(): lax.all_to_all(copies, ('x', 'core', 'half', 'column'), split_axis=0, con...  1.63 us
    pallas_call x1, Pallas kernels, local(): pl.pallas_call(first_kernel, out_shape=jax.ShapeDtypeStruct((2, 2, row_de...  1.33 us
    add x1, other arithmetic, local(): return second(False) + from_partner  0.56 us
  transfers between devices with their start and end apart: 4, of which 3 were waited for; matrix products, arithmetic and copies ran while one was open for 0% of the time, Pallas kernels for 11%

profile of v16, /device:TPU:0, one launch (start us, length us, event | category | flops | bytes accessed | tf_op | source)
XLA Modules:
  0.0 20.7 jit_solution(6197936230211353563)
XLA Ops:
  0.0 1.8 %shard_map.64 = f32[8,4,1408]{2,1,0:T(4,128)} custom-call(s32[8]{0:T(128)} %bitcast.2, s32[8]{0:T(128)} %bitcast.3, f32[3,1024]{1,0:T(4,128)} %src_hbm.1, f32[2,1024]{1,0:T(2,128)} %cur_hbm.1, f32[8,2,16,128]{3,2,1,0:T(8,128)} %blocks_hbm.1), custom_call_target="tpu_custom_call" | custom-call | flops 1048576 | bytes 1048576 | tf_op jit(solution)/shard_map/pallas_call | solution.py:243
  1.8 0.0 copy-start
  1.8 5.6 %all-to-all-start = ((f32[8,4,1408]{2,1,0:T(4,128)}), f32[8,4,1408]{2,1,0:T(4,128)S(1)}, u32[]{:S(2)}, u32[]{:S(2)}) async-start(f32[8,4,1408]{2,1,0:T(4,128)} %shard_map.64), calls=%async_computation | async-start | bytes 360448 | tf_op jit(solution)/shard_map/all_to_all | solution.py:260
  7.5 0.0 copy-done
  7.5 2.9 %collective-permute-start = (f32[3,16]{1,0:T(4,128)S(1)}, f32[3,16]{1,0:T(4,128)S(1)}, u32[]{:S(2)}, u32[]{:S(2)}) collective-permute-start(f32[3,16]{1,0:T(4,128)S(1)} %copy-done), channel_id=1, source_target_pairs={{0,12},{4,8},{8,4},{12,0},{1,13},{5,9},{9,5},{13,1},{2,14},{6,10},... | collective-permute-start | bytes 584 | tf_op jit(solution)/shard_map/ppermute | solution.py:217
  10.4 1.4 %collective-permute-done.partner_ref = f32[3,16]{1,0:T(4,128)S(1)} collective-permute-done((f32[3,16]{1,0:T(4,128)S(1)}, f32[3,16]{1,0:T(4,128)S(1)}, u32[]{:S(2)}, u32[]{:S(2)}) %collective-permute-start) | collective-permute-done | bytes 224 | tf_op jit(solution)/shard_map/ppermute | solution.py:217
  11.8 0.1 shard_map.65.wide_ref
  11.8 1.6 %all-to-all-done.messages_ref = f32[8,4,1408]{2,1,0:T(4,128)S(1)} async-done(((f32[8,4,1408]{2,1,0:T(4,128)}), f32[8,4,1408]{2,1,0:T(4,128)S(1)}, u32[]{:S(2)}, u32[]{:S(2)}) %all-to-all-start) | async-done | bytes 180256 | tf_op jit(solution)/shard_map/all_to_all | solution.py:260
  13.5 0.5 %collective-permute-start.1 = (f32[8,4,1408]{2,1,0:T(4,128)S(1)}, f32[8,4,1408]{2,1,0:T(4,128)S(1)}, u32[]{:S(2)}, u32[]{:S(2)}) collective-permute-start(f32[8,4,1408]{2,1,0:T(4,128)S(1)} %all-to-all-done.messages_ref), channel_id=1, source_target_pairs={{0,8},{8,0},{1,9},{9,1},{2,10},{10,2},{3,11},{11,3},{4,12},{12,4},... | collective-permute-start | bytes 540680 | tf_op jit(solution)/shard_map/ppermute | solution.py:285
  14.0 1.3 %shard_map.66.sums_ref = f32[2,2,16,128]{3,2,1,0:T(8,128)S(1)} custom-call(f32[2,3,16,128]{3,2,1,0:T(8,128)S(1)} %shard_map.65.wide_ref, f32[8,4,1408]{2,1,0:T(4,128)S(1)} %all-to-all-done.messages_ref), custom_call_target="tpu_custom_call" | custom-call | flops 10485760 | bytes 2097152 | tf_op jit(solution)/shard_map/pallas_call | solution.py:286
  15.3 0.0 collective-permute-done.1.sibling_ref
  15.3 0.8 %shard_map.68 = f32[2,16]{1,0:T(2,128)S(1)} custom-call(f32[2,3,16,128]{3,2,1,0:T(8,128)S(1)} %shard_map.65.wide_ref, f32[2,2,16,128]{3,2,1,0:T(8,128)S(1)} %shard_map.66.sums_ref, f32[8,4,1408]{2,1,0:T(4,128)S(1)} %all-to-all-done.messages_ref, f32[8,4,1408]{2,1,0:T(4,128)S(1)} %collective-permute-done.1.sibling_ref), custom_call_target="tpu_custom_call" | custom-call | flops 5242880 | bytes 2097152 | tf_op jit(solution)/shard_map/pallas_call | solution.py:295
  16.2 2.3 %collective-permute-start.2 = (f32[2,16]{1,0:T(2,128)S(1)}, f32[2,16]{1,0:T(2,128)S(1)}, u32[]{:S(2)}, u32[]{:S(2)}) collective-permute-start(f32[2,16]{1,0:T(2,128)S(1)} %shard_map.68), channel_id=1, source_target_pairs={{0,12},{4,8},{8,4},{12,0},{1,13},{5,9},{9,5},{13,1},{2,14},{6,10},... | collective-permute-start | bytes 392 | tf_op jit(solution)/shard_map/ppermute | solution.py:217
  18.5 0.8 %shard_map.67 = f32[2,16]{1,0:T(2,128)S(1)} custom-call(f32[2,3,16,128]{3,2,1,0:T(8,128)S(1)} %shard_map.65.wide_ref, f32[2,2,16,128]{3,2,1,0:T(8,128)S(1)} %shard_map.66.sums_ref, f32[8,4,1408]{2,1,0:T(4,128)S(1)} %all-to-all-done.messages_ref, f32[8,4,1408]{2,1,0:T(4,128)S(1)} %collective-permute-done.1.sibling_ref), custom_call_target="tpu_custom_call" | custom-call | flops 5242880 | bytes 2097152 | tf_op jit(solution)/shard_map/pallas_call | solution.py:295
  19.3 0.8 %collective-permute-done.2 = f32[2,16]{1,0:T(2,128)S(1)} collective-permute-done((f32[2,16]{1,0:T(2,128)S(1)}, f32[2,16]{1,0:T(2,128)S(1)}, u32[]{:S(2)}, u32[]{:S(2)}) %collective-permute-start.2) | collective-permute-done | bytes 160 | tf_op jit(solution)/shard_map/ppermute | solution.py:217
  20.1 0.6 %add.3 = f32[2,16]{1,0:T(2,128)} add(f32[2,16]{1,0:T(2,128)S(1)} %shard_map.67, f32[2,16]{1,0:T(2,128)S(1)} %collective-permute-done.2) | non-fusion elementwise | flops 32 | bytes 384 | tf_op jit(solution)/shard_map/add | solution.py:304
Async XLA Ops:
  1.8 5.6 %copy-start = (f32[3,16]{1,0:T(4,128)S(1)}, f32[3,16]{1,0:T(4,128)}, u32[]{:S(2)}) copy-start(f32[3,16]{1,0:T(4,128)} %tests_ref.1) | copy-start | bytes 580
  1.8 11.7 %all-to-all-start = ((f32[8,4,1408]{2,1,0:T(4,128)}), f32[8,4,1408]{2,1,0:T(4,128)S(1)}, u32[]{:S(2)}, u32[]{:S(2)}) async-start(f32[8,4,1408]{2,1,0:T(4,128)} %shard_map.64), calls=%async_computation | async-start | bytes 360448 | tf_op jit(solution)/shard_map/all_to_all | solution.py:260
  7.5 4.3 %collective-permute-start = (f32[3,16]{1,0:T(4,128)S(1)}, f32[3,16]{1,0:T(4,128)S(1)}, u32[]{:S(2)}, u32[]{:S(2)}) collective-permute-start(f32[3,16]{1,0:T(4,128)S(1)} %copy-done), channel_id=1, source_target_pairs={{0,12},{4,8},{8,4},{12,0},{1,13},{5,9},{9,5},{13,1},{2,14},{6,10},... | collective-permute-start | bytes 584 | tf_op jit(solution)/shard_map/ppermute | solution.py:217
  13.5 1.8 %collective-permute-start.1 = (f32[8,4,1408]{2,1,0:T(4,128)S(1)}, f32[8,4,1408]{2,1,0:T(4,128)S(1)}, u32[]{:S(2)}, u32[]{:S(2)}) collective-permute-start(f32[8,4,1408]{2,1,0:T(4,128)S(1)} %all-to-all-done.messages_ref), channel_id=1, source_target_pairs={{0,8},{8,0},{1,9},{9,1},{2,10},{10,2},{3,11},{11,3},{4,12},{12,4},... | collective-permute-start | bytes 540680 | tf_op jit(solution)/shard_map/ppermute | solution.py:285
  16.2 4.0 %collective-permute-start.2 = (f32[2,16]{1,0:T(2,128)S(1)}, f32[2,16]{1,0:T(2,128)S(1)}, u32[]{:S(2)}, u32[]{:S(2)}) collective-permute-start(f32[2,16]{1,0:T(2,128)S(1)} %shard_map.68), channel_id=1, source_target_pairs={{0,12},{4,8},{8,4},{12,0},{1,13},{5,9},{9,5},{13,1},{2,14},{6,10},... | collective-permute-start | bytes 392 | tf_op jit(solution)/shard_map/ppermute | solution.py:217

commit v17 on v16

--- a/solution.py
+++ b/solution.py
@@ -113,7 +113,7 @@
     xs = members // half_columns
     for k in range(half_columns):
         for half in range(2):
-            copies_ref[k * xs + lax.axis_index("x"), half : half + 1, last:] = near_all[half * half_columns + k : half * half_columns + k + 1, :]
+            copies_ref[members - 1 - k * xs - lax.axis_index("x"), half : half + 1, last:] = near_all[half * half_columns + k : half * half_columns + k + 1, :]
 
 
 def points_kernel(partner_ref, tests_ref, wide_ref):
@@ -181,7 +181,7 @@
     middle = half_columns // 2
     straight = crossed = jnp.zeros((QUAD, LANES), jnp.float32)
     for k in range(half_columns):
-        member = k * xs + lax.axis_index("x")
+        member = messages_ref.shape[0] - 1 - k * xs - lax.axis_index("x")
         own, sibling = messages_ref[member, :, last:], sibling_ref[member, :, last:]
         straight = straight + (own if k < middle else sibling)
         crossed = crossed + (sibling if k < middle else own)
@@ -222,7 +222,7 @@
         return ((x * 2 + core) * 2 + half) * half_columns + column
 
     return [
-        [place(x, g ^ (column >= half_columns // 2), half, column) for column in range(half_columns) for x in range(xs)]
+        [place(x, g ^ (column >= half_columns // 2), half, column) for column in reversed(range(half_columns)) for x in reversed(range(xs))]
         for half in range(2)
         for g in range(2)
     ]

time: 21 us -> 21.2 us (level)
  starting transfers between devices: 11.4 us -> 13.3 us
  waiting for transfers between devices: 3.82 us -> 2.14 us
    all_to_all x1, starting transfers between devices: 5.63 us -> 7.69 us  [local(): lax.all_to_all(copies, ('x', 'core', 'half', 'column'), split_axis=0, con...]
    all_to_all x1, waiting for transfers between devices: 1.63 us -> 0.01 us  [local(): lax.all_to_all(copies, ('x', 'core', 'half', 'column'), split_axis=0, con...]
  transfers between devices with their start and end apart: 4 -> 4, of which waited for: 3 -> 2; matrix products, arithmetic and copies ran while one was open for 0% -> 0% of each run, Pallas kernels for 11% -> 11%
where the time goes in v17:
time: 21.2 us; the launch traced here: 21 us
  starting transfers between devices  13.3 us (63%)
  Pallas kernels  4.87 us (23%)
  waiting for transfers between devices  2.14 us (10%)
  other arithmetic  0.56 us (3%)
    all_to_all x1, starting transfers between devices, local(): lax.all_to_all(copies, ('x', 'core', 'half', 'column'), split_axis=0, con...  7.69 us
    ppermute x2, starting transfers between devices, across(): return lax.ppermute(x, ('core', 'half'), [(i, 3 - i) for i in range(4)])  5.19 us
    ppermute x2, waiting for transfers between devices, across(): return lax.ppermute(x, ('core', 'half'), [(i, 3 - i) for i in range(4)])  2.13 us
    pallas_call x1, Pallas kernels, local(): pl.pallas_call(functools.partial(pack_kernel, half_columns, gain), out_sh...  1.8 us
    pallas_call x2, Pallas kernels, second(): pl.pallas_call(functools.partial(second_kernel, half_columns, other), out...  1.66 us
    pallas_call x1, Pallas kernels, local(): pl.pallas_call(first_kernel, out_shape=jax.ShapeDtypeStruct((2, 2, row_de...  1.33 us
    add x1, other arithmetic, local(): return second(False) + from_partner  0.56 us
    ppermute x1, starting transfers between devices, local(): sibling = lax.ppermute(messages, 'core', [(0, 1), (1, 0)])  0.47 us
  transfers between devices with their start and end apart: 4, of which 2 were waited for; matrix products, arithmetic and copies ran while one was open for 0% of the time, Pallas kernels for 11%

profile of v17, /device:TPU:0, one launch (start us, length us, event | category | flops | bytes accessed | tf_op | source)
XLA Modules:
  0.0 21.0 jit_solution(6149226406771711321)
XLA Ops:
  0.0 1.8 %shard_map.64 = f32[8,4,1408]{2,1,0:T(4,128)} custom-call(s32[8]{0:T(128)} %bitcast.2, s32[8]{0:T(128)} %bitcast.3, f32[3,1024]{1,0:T(4,128)} %src_hbm.1, f32[2,1024]{1,0:T(2,128)} %cur_hbm.1, f32[8,2,16,128]{3,2,1,0:T(8,128)} %blocks_hbm.1), custom_call_target="tpu_custom_call" | custom-call | flops 1048576 | bytes 1048576 | tf_op jit(solution)/shard_map/pallas_call | solution.py:243
  1.8 0.0 copy-start
  1.8 7.7 %all-to-all-start = ((f32[8,4,1408]{2,1,0:T(4,128)}), f32[8,4,1408]{2,1,0:T(4,128)S(1)}, u32[]{:S(2)}, u32[]{:S(2)}) async-start(f32[8,4,1408]{2,1,0:T(4,128)} %shard_map.64), calls=%async_computation | async-start | bytes 360448 | tf_op jit(solution)/shard_map/all_to_all | solution.py:260
  9.5 0.0 copy-done
  9.5 2.9 %collective-permute-start = (f32[3,16]{1,0:T(4,128)S(1)}, f32[3,16]{1,0:T(4,128)S(1)}, u32[]{:S(2)}, u32[]{:S(2)}) collective-permute-start(f32[3,16]{1,0:T(4,128)S(1)} %copy-done), channel_id=1, source_target_pairs={{0,12},{4,8},{8,4},{12,0},{1,13},{5,9},{9,5},{13,1},{2,14},{6,10},... | collective-permute-start | bytes 584 | tf_op jit(solution)/shard_map/ppermute | solution.py:217
  12.4 1.3 %collective-permute-done.partner_ref = f32[3,16]{1,0:T(4,128)S(1)} collective-permute-done((f32[3,16]{1,0:T(4,128)S(1)}, f32[3,16]{1,0:T(4,128)S(1)}, u32[]{:S(2)}, u32[]{:S(2)}) %collective-permute-start) | collective-permute-done | bytes 224 | tf_op jit(solution)/shard_map/ppermute | solution.py:217
  13.7 0.1 shard_map.65.wide_ref
  13.8 0.0 all-to-all-done.messages_ref
  13.8 0.5 %collective-permute-start.1 = (f32[8,4,1408]{2,1,0:T(4,128)S(1)}, f32[8,4,1408]{2,1,0:T(4,128)S(1)}, u32[]{:S(2)}, u32[]{:S(2)}) collective-permute-start(f32[8,4,1408]{2,1,0:T(4,128)S(1)} %all-to-all-done.messages_ref), channel_id=1, source_target_pairs={{0,8},{8,0},{1,9},{9,1},{2,10},{10,2},{3,11},{11,3},{4,12},{12,4},... | collective-permute-start | bytes 540680 | tf_op jit(solution)/shard_map/ppermute | solution.py:285
  14.2 1.3 %shard_map.66.sums_ref = f32[2,2,16,128]{3,2,1,0:T(8,128)S(1)} custom-call(f32[2,3,16,128]{3,2,1,0:T(8,128)S(1)} %shard_map.65.wide_ref, f32[8,4,1408]{2,1,0:T(4,128)S(1)} %all-to-all-done.messages_ref), custom_call_target="tpu_custom_call" | custom-call | flops 10485760 | bytes 2097152 | tf_op jit(solution)/shard_map/pallas_call | solution.py:286
  15.6 0.0 collective-permute-done.1.sibling_ref
  15.6 0.8 %shard_map.68 = f32[2,16]{1,0:T(2,128)S(1)} custom-call(f32[2,3,16,128]{3,2,1,0:T(8,128)S(1)} %shard_map.65.wide_ref, f32[2,2,16,128]{3,2,1,0:T(8,128)S(1)} %shard_map.66.sums_ref, f32[8,4,1408]{2,1,0:T(4,128)S(1)} %all-to-all-done.messages_ref, f32[8,4,1408]{2,1,0:T(4,128)S(1)} %collective-permute-done.1.sibling_ref), custom_call_target="tpu_custom_call" | custom-call | flops 5242880 | bytes 2097152 | tf_op jit(solution)/shard_map/pallas_call | solution.py:295
  16.4 2.3 %collective-permute-start.2 = (f32[2,16]{1,0:T(2,128)S(1)}, f32[2,16]{1,0:T(2,128)S(1)}, u32[]{:S(2)}, u32[]{:S(2)}) collective-permute-start(f32[2,16]{1,0:T(2,128)S(1)} %shard_map.68), channel_id=1, source_target_pairs={{0,12},{4,8},{8,4},{12,0},{1,13},{5,9},{9,5},{13,1},{2,14},{6,10},... | collective-permute-start | bytes 392 | tf_op jit(solution)/shard_map/ppermute | solution.py:217
  18.8 0.8 %shard_map.67 = f32[2,16]{1,0:T(2,128)S(1)} custom-call(f32[2,3,16,128]{3,2,1,0:T(8,128)S(1)} %shard_map.65.wide_ref, f32[2,2,16,128]{3,2,1,0:T(8,128)S(1)} %shard_map.66.sums_ref, f32[8,4,1408]{2,1,0:T(4,128)S(1)} %all-to-all-done.messages_ref, f32[8,4,1408]{2,1,0:T(4,128)S(1)} %collective-permute-done.1.sibling_ref), custom_call_target="tpu_custom_call" | custom-call | flops 5242880 | bytes 2097152 | tf_op jit(solution)/shard_map/pallas_call | solution.py:295
  19.6 0.8 %collective-permute-done.2 = f32[2,16]{1,0:T(2,128)S(1)} collective-permute-done((f32[2,16]{1,0:T(2,128)S(1)}, f32[2,16]{1,0:T(2,128)S(1)}, u32[]{:S(2)}, u32[]{:S(2)}) %collective-permute-start.2) | collective-permute-done | bytes 160 | tf_op jit(solution)/shard_map/ppermute | solution.py:217
  20.4 0.6 %add.3 = f32[2,16]{1,0:T(2,128)} add(f32[2,16]{1,0:T(2,128)S(1)} %shard_map.67, f32[2,16]{1,0:T(2,128)S(1)} %collective-permute-done.2) | non-fusion elementwise | flops 32 | bytes 384 | tf_op jit(solution)/shard_map/add | solution.py:304
Async XLA Ops:
  1.8 7.7 %copy-start = (f32[3,16]{1,0:T(4,128)S(1)}, f32[3,16]{1,0:T(4,128)}, u32[]{:S(2)}) copy-start(f32[3,16]{1,0:T(4,128)} %tests_ref.1) | copy-start | bytes 580
  1.8 12.0 %all-to-all-start = ((f32[8,4,1408]{2,1,0:T(4,128)}), f32[8,4,1408]{2,1,0:T(4,128)S(1)}, u32[]{:S(2)}, u32[]{:S(2)}) async-start(f32[8,4,1408]{2,1,0:T(4,128)} %shard_map.64), calls=%async_computation | async-start | bytes 360448 | tf_op jit(solution)/shard_map/all_to_all | solution.py:260
  9.5 4.2 %collective-permute-start = (f32[3,16]{1,0:T(4,128)S(1)}, f32[3,16]{1,0:T(4,128)S(1)}, u32[]{:S(2)}, u32[]{:S(2)}) collective-permute-start(f32[3,16]{1,0:T(4,128)S(1)} %copy-done), channel_id=1, source_target_pairs={{0,12},{4,8},{8,4},{12,0},{1,13},{5,9},{9,5},{13,1},{2,14},{6,10},... | collective-permute-start | bytes 584 | tf_op jit(solution)/shard_map/ppermute | solution.py:217
  13.8 1.8 %collective-permute-start.1 = (f32[8,4,1408]{2,1,0:T(4,128)S(1)}, f32[8,4,1408]{2,1,0:T(4,128)S(1)}, u32[]{:S(2)}, u32[]{:S(2)}) collective-permute-start(f32[8,4,1408]{2,1,0:T(4,128)S(1)} %all-to-all-done.messages_ref), channel_id=1, source_target_pairs={{0,8},{8,0},{1,9},{9,1},{2,10},{10,2},{3,11},{11,3},{4,12},{12,4},... | collective-permute-start | bytes 540680 | tf_op jit(solution)/shard_map/ppermute | solution.py:285
  16.4 4.0 %collective-permute-start.2 = (f32[2,16]{1,0:T(2,128)S(1)}, f32[2,16]{1,0:T(2,128)S(1)}, u32[]{:S(2)}, u32[]{:S(2)}) collective-permute-start(f32[2,16]{1,0:T(2,128)S(1)} %shard_map.68), channel_id=1, source_target_pairs={{0,12},{4,8},{8,4},{12,0},{1,13},{5,9},{9,5},{13,1},{2,14},{6,10},... | collective-permute-start | bytes 392 | tf_op jit(solution)/shard_map/ppermute | solution.py:217

commit v18 on v16

--- a/solution.py
+++ b/solution.py
@@ -162,7 +162,7 @@
             sums = tuple(new)
         return sums
 
-    return lax.fori_loop(0, members, step, tuple(sums), unroll=8 // len(tests))
+    return lax.fori_loop(0, members, step, tuple(sums), unroll=16 // len(tests))
 
 
 def rows_of(sums):

time: 21 us -> 20.9 us (level)
  no operation moved by 1% of the time
where the time goes in v18:
time: 20.9 us; the launch traced here: 20.6 us
  starting transfers between devices  11.4 us (55%)
  Pallas kernels  4.8 us (23%)
  waiting for transfers between devices  3.81 us (18%)
  other arithmetic  0.56 us (3%)
    all_to_all x1, starting transfers between devices, local(): lax.all_to_all(copies, ('x', 'core', 'half', 'column'), split_axis=0, con...  5.63 us
    ppermute x2, starting transfers between devices, across(): return lax.ppermute(x, ('core', 'half'), [(i, 3 - i) for i in range(4)])  5.24 us
    ppermute x2, waiting for transfers between devices, across(): return lax.ppermute(x, ('core', 'half'), [(i, 3 - i) for i in range(4)])  2.18 us
    pallas_call x1, Pallas kernels, local(): pl.pallas_call(functools.partial(pack_kernel, half_columns, gain), out_sh...  1.8 us
    all_to_all x1, waiting for transfers between devices, local(): lax.all_to_all(copies, ('x', 'core', 'half', 'column'), split_axis=0, con...  1.63 us
    pallas_call x2, Pallas kernels, second(): pl.pallas_call(functools.partial(second_kernel, half_columns, other), out...  1.6 us
    pallas_call x1, Pallas kernels, local(): pl.pallas_call(first_kernel, out_shape=jax.ShapeDtypeStruct((2, 2, row_de...  1.31 us
    add x1, other arithmetic, local(): return second(False) + from_partner  0.56 us
  transfers between devices with their start and end apart: 4, of which 3 were waited for; matrix products, arithmetic and copies ran while one was open for 0% of the time, Pallas kernels for 11%

profile of v18, /device:TPU:0, one launch (start us, length us, event | category | flops | bytes accessed | tf_op | source)
XLA Modules:
  0.0 20.6 jit_solution(3812355616287821973)
XLA Ops:
  0.0 1.8 %shard_map.64 = f32[8,4,1408]{2,1,0:T(4,128)} custom-call(s32[8]{0:T(128)} %bitcast.2, s32[8]{0:T(128)} %bitcast.3, f32[3,1024]{1,0:T(4,128)} %src_hbm.1, f32[2,1024]{1,0:T(2,128)} %cur_hbm.1, f32[8,2,16,128]{3,2,1,0:T(8,128)} %blocks_hbm.1), custom_call_target="tpu_custom_call" | custom-call | flops 1048576 | bytes 1048576 | tf_op jit(solution)/shard_map/pallas_call | solution.py:243
  1.8 0.0 copy-start
  1.8 5.6 %all-to-all-start = ((f32[8,4,1408]{2,1,0:T(4,128)}), f32[8,4,1408]{2,1,0:T(4,128)S(1)}, u32[]{:S(2)}, u32[]{:S(2)}) async-start(f32[8,4,1408]{2,1,0:T(4,128)} %shard_map.64), calls=%async_computation | async-start | bytes 360448 | tf_op jit(solution)/shard_map/all_to_all | solution.py:260
  7.5 0.0 copy-done
  7.5 2.9 %collective-permute-start = (f32[3,16]{1,0:T(4,128)S(1)}, f32[3,16]{1,0:T(4,128)S(1)}, u32[]{:S(2)}, u32[]{:S(2)}) collective-permute-start(f32[3,16]{1,0:T(4,128)S(1)} %copy-done), channel_id=1, source_target_pairs={{0,12},{4,8},{8,4},{12,0},{1,13},{5,9},{9,5},{13,1},{2,14},{6,10},... | collective-permute-start | bytes 584 | tf_op jit(solution)/shard_map/ppermute | solution.py:217
  10.4 1.4 %collective-permute-done.partner_ref = f32[3,16]{1,0:T(4,128)S(1)} collective-permute-done((f32[3,16]{1,0:T(4,128)S(1)}, f32[3,16]{1,0:T(4,128)S(1)}, u32[]{:S(2)}, u32[]{:S(2)}) %collective-permute-start) | collective-permute-done | bytes 224 | tf_op jit(solution)/shard_map/ppermute | solution.py:217
  11.8 0.1 shard_map.65.wide_ref
  11.8 1.6 %all-to-all-done.messages_ref = f32[8,4,1408]{2,1,0:T(4,128)S(1)} async-done(((f32[8,4,1408]{2,1,0:T(4,128)}), f32[8,4,1408]{2,1,0:T(4,128)S(1)}, u32[]{:S(2)}, u32[]{:S(2)}) %all-to-all-start) | async-done | bytes 180256 | tf_op jit(solution)/shard_map/all_to_all | solution.py:260
  13.5 0.5 %collective-permute-start.1 = (f32[8,4,1408]{2,1,0:T(4,128)S(1)}, f32[8,4,1408]{2,1,0:T(4,128)S(1)}, u32[]{:S(2)}, u32[]{:S(2)}) collective-permute-start(f32[8,4,1408]{2,1,0:T(4,128)S(1)} %all-to-all-done.messages_ref), channel_id=1, source_target_pairs={{0,8},{8,0},{1,9},{9,1},{2,10},{10,2},{3,11},{11,3},{4,12},{12,4},... | collective-permute-start | bytes 540680 | tf_op jit(solution)/shard_map/ppermute | solution.py:285
  14.0 1.3 %shard_map.66.sums_ref = f32[2,2,16,128]{3,2,1,0:T(8,128)S(1)} custom-call(f32[2,3,16,128]{3,2,1,0:T(8,128)S(1)} %shard_map.65.wide_ref, f32[8,4,1408]{2,1,0:T(4,128)S(1)} %all-to-all-done.messages_ref), custom_call_target="tpu_custom_call" | custom-call | flops 10485760 | bytes 2097152 | tf_op jit(solution)/shard_map/pallas_call | solution.py:286
  15.3 0.0 collective-permute-done.1.sibling_ref
  15.3 0.8 %shard_map.68 = f32[2,16]{1,0:T(2,128)S(1)} custom-call(f32[2,3,16,128]{3,2,1,0:T(8,128)S(1)} %shard_map.65.wide_ref, f32[2,2,16,128]{3,2,1,0:T(8,128)S(1)} %shard_map.66.sums_ref, f32[8,4,1408]{2,1,0:T(4,128)S(1)} %all-to-all-done.messages_ref, f32[8,4,1408]{2,1,0:T(4,128)S(1)} %collective-permute-done.1.sibling_ref), custom_call_target="tpu_custom_call" | custom-call | flops 5242880 | bytes 2097152 | tf_op jit(solution)/shard_map/pallas_call | solution.py:295
  16.1 2.3 %collective-permute-start.2 = (f32[2,16]{1,0:T(2,128)S(1)}, f32[2,16]{1,0:T(2,128)S(1)}, u32[]{:S(2)}, u32[]{:S(2)}) collective-permute-start(f32[2,16]{1,0:T(2,128)S(1)} %shard_map.68), channel_id=1, source_target_pairs={{0,12},{4,8},{8,4},{12,0},{1,13},{5,9},{9,5},{13,1},{2,14},{6,10},... | collective-permute-start | bytes 392 | tf_op jit(solution)/shard_map/ppermute | solution.py:217
  18.4 0.8 %shard_map.67 = f32[2,16]{1,0:T(2,128)S(1)} custom-call(f32[2,3,16,128]{3,2,1,0:T(8,128)S(1)} %shard_map.65.wide_ref, f32[2,2,16,128]{3,2,1,0:T(8,128)S(1)} %shard_map.66.sums_ref, f32[8,4,1408]{2,1,0:T(4,128)S(1)} %all-to-all-done.messages_ref, f32[8,4,1408]{2,1,0:T(4,128)S(1)} %collective-permute-done.1.sibling_ref), custom_call_target="tpu_custom_call" | custom-call | flops 5242880 | bytes 2097152 | tf_op jit(solution)/shard_map/pallas_call | solution.py:295
  19.2 0.8 %collective-permute-done.2 = f32[2,16]{1,0:T(2,128)S(1)} collective-permute-done((f32[2,16]{1,0:T(2,128)S(1)}, f32[2,16]{1,0:T(2,128)S(1)}, u32[]{:S(2)}, u32[]{:S(2)}) %collective-permute-start.2) | collective-permute-done | bytes 160 | tf_op jit(solution)/shard_map/ppermute | solution.py:217
  20.0 0.6 %add.3 = f32[2,16]{1,0:T(2,128)} add(f32[2,16]{1,0:T(2,128)S(1)} %shard_map.67, f32[2,16]{1,0:T(2,128)S(1)} %collective-permute-done.2) | non-fusion elementwise | flops 32 | bytes 384 | tf_op jit(solution)/shard_map/add | solution.py:304
Async XLA Ops:
  1.8 5.6 %copy-start = (f32[3,16]{1,0:T(4,128)S(1)}, f32[3,16]{1,0:T(4,128)}, u32[]{:S(2)}) copy-start(f32[3,16]{1,0:T(4,128)} %tests_ref.1) | copy-start | bytes 580
  1.8 11.7 %all-to-all-start = ((f32[8,4,1408]{2,1,0:T(4,128)}), f32[8,4,1408]{2,1,0:T(4,128)S(1)}, u32[]{:S(2)}, u32[]{:S(2)}) async-start(f32[8,4,1408]{2,1,0:T(4,128)} %shard_map.64), calls=%async_computation | async-start | bytes 360448 | tf_op jit(solution)/shard_map/all_to_all | solution.py:260
  7.5 4.3 %collective-permute-start = (f32[3,16]{1,0:T(4,128)S(1)}, f32[3,16]{1,0:T(4,128)S(1)}, u32[]{:S(2)}, u32[]{:S(2)}) collective-permute-start(f32[3,16]{1,0:T(4,128)S(1)} %copy-done), channel_id=1, source_target_pairs={{0,12},{4,8},{8,4},{12,0},{1,13},{5,9},{9,5},{13,1},{2,14},{6,10},... | collective-permute-start | bytes 584 | tf_op jit(solution)/shard_map/ppermute | solution.py:217
  13.5 1.8 %collective-permute-start.1 = (f32[8,4,1408]{2,1,0:T(4,128)S(1)}, f32[8,4,1408]{2,1,0:T(4,128)S(1)}, u32[]{:S(2)}, u32[]{:S(2)}) collective-permute-start(f32[8,4,1408]{2,1,0:T(4,128)S(1)} %all-to-all-done.messages_ref), channel_id=1, source_target_pairs={{0,8},{8,0},{1,9},{9,1},{2,10},{10,2},{3,11},{11,3},{4,12},{12,4},... | collective-permute-start | bytes 540680 | tf_op jit(solution)/shard_map/ppermute | solution.py:285
  16.1 3.9 %collective-permute-start.2 = (f32[2,16]{1,0:T(2,128)S(1)}, f32[2,16]{1,0:T(2,128)S(1)}, u32[]{:S(2)}, u32[]{:S(2)}) collective-permute-start(f32[2,16]{1,0:T(2,128)S(1)} %shard_map.68), channel_id=1, source_target_pairs={{0,12},{4,8},{8,4},{12,0},{1,13},{5,9},{9,5},{13,1},{2,14},{6,10},... | collective-permute-start | bytes 392 | tf_op jit(solution)/shard_map/ppermute | solution.py:217

commit v19 on v16

--- a/solution.py
+++ b/solution.py
@@ -59,7 +59,7 @@
             (src_hbm, src_ref), (cur_hbm, cur_ref), (blocks_hbm, blocks_ref), (dest_hbm, dest_ref), (tile_hbm, tile_ref)
         ))
     ]
-    for move in moves:
+    for move in (*moves[3:], *moves[:3]):
         move.start()
     members = copies_ref.shape[0]
     tiles = src_ref.shape[1] // LANES

time: 21 us -> 20.9 us (level)
  no operation moved by 1% of the time
where the time goes in v19:
time: 20.9 us; the launch traced here: 20.7 us
  starting transfers between devices  11.4 us (55%)
  Pallas kernels  4.87 us (23%)
  waiting for transfers between devices  3.82 us (18%)
  other arithmetic  0.56 us (3%)
    all_to_all x1, starting transfers between devices, local(): lax.all_to_all(copies, ('x', 'core', 'half', 'column'), split_axis=0, con...  5.63 us
    ppermute x2, starting transfers between devices, across(): return lax.ppermute(x, ('core', 'half'), [(i, 3 - i) for i in range(4)])  5.26 us
    ppermute x2, waiting for transfers between devices, across(): return lax.ppermute(x, ('core', 'half'), [(i, 3 - i) for i in range(4)])  2.19 us
    pallas_call x1, Pallas kernels, local(): pl.pallas_call(functools.partial(pack_kernel, half_columns, gain), out_sh...  1.8 us
    pallas_call x2, Pallas kernels, second(): pl.pallas_call(functools.partial(second_kernel, half_columns, other), out...  1.65 us
    all_to_all x1, waiting for transfers between devices, local(): lax.all_to_all(copies, ('x', 'core', 'half', 'column'), split_axis=0, con...  1.63 us
    pallas_call x1, Pallas kernels, local(): pl.pallas_call(first_kernel, out_shape=jax.ShapeDtypeStruct((2, 2, row_de...  1.33 us
    add x1, other arithmetic, local(): return second(False) + from_partner  0.56 us
  transfers between devices with their start and end apart: 4, of which 3 were waited for; matrix products, arithmetic and copies ran while one was open for 0% of the time, Pallas kernels for 11%

profile of v19, /device:TPU:0, one launch (start us, length us, event | category | flops | bytes accessed | tf_op | source)
XLA Modules:
  0.0 20.7 jit_solution(14882231010222981591)
XLA Ops:
  0.0 1.8 %shard_map.64 = f32[8,4,1408]{2,1,0:T(4,128)} custom-call(s32[8]{0:T(128)} %bitcast.2, s32[8]{0:T(128)} %bitcast.3, f32[3,1024]{1,0:T(4,128)} %src_hbm.1, f32[2,1024]{1,0:T(2,128)} %cur_hbm.1, f32[8,2,16,128]{3,2,1,0:T(8,128)} %blocks_hbm.1), custom_call_target="tpu_custom_call" | custom-call | flops 1048576 | bytes 1048576 | tf_op jit(solution)/shard_map/pallas_call | solution.py:243
  1.8 0.0 copy-start
  1.8 5.6 %all-to-all-start = ((f32[8,4,1408]{2,1,0:T(4,128)}), f32[8,4,1408]{2,1,0:T(4,128)S(1)}, u32[]{:S(2)}, u32[]{:S(2)}) async-start(f32[8,4,1408]{2,1,0:T(4,128)} %shard_map.64), calls=%async_computation | async-start | bytes 360448 | tf_op jit(solution)/shard_map/all_to_all | solution.py:260
  7.5 0.0 copy-done
  7.5 2.9 %collective-permute-start = (f32[3,16]{1,0:T(4,128)S(1)}, f32[3,16]{1,0:T(4,128)S(1)}, u32[]{:S(2)}, u32[]{:S(2)}) collective-permute-start(f32[3,16]{1,0:T(4,128)S(1)} %copy-done), channel_id=1, source_target_pairs={{0,12},{4,8},{8,4},{12,0},{1,13},{5,9},{9,5},{13,1},{2,14},{6,10},... | collective-permute-start | bytes 584 | tf_op jit(solution)/shard_map/ppermute | solution.py:217
  10.4 1.4 %collective-permute-done.partner_ref = f32[3,16]{1,0:T(4,128)S(1)} collective-permute-done((f32[3,16]{1,0:T(4,128)S(1)}, f32[3,16]{1,0:T(4,128)S(1)}, u32[]{:S(2)}, u32[]{:S(2)}) %collective-permute-start) | collective-permute-done | bytes 224 | tf_op jit(solution)/shard_map/ppermute | solution.py:217
  11.8 0.1 shard_map.65.wide_ref
  11.8 1.6 %all-to-all-done.messages_ref = f32[8,4,1408]{2,1,0:T(4,128)S(1)} async-done(((f32[8,4,1408]{2,1,0:T(4,128)}), f32[8,4,1408]{2,1,0:T(4,128)S(1)}, u32[]{:S(2)}, u32[]{:S(2)}) %all-to-all-start) | async-done | bytes 180256 | tf_op jit(solution)/shard_map/all_to_all | solution.py:260
  13.5 0.5 %collective-permute-start.1 = (f32[8,4,1408]{2,1,0:T(4,128)S(1)}, f32[8,4,1408]{2,1,0:T(4,128)S(1)}, u32[]{:S(2)}, u32[]{:S(2)}) collective-permute-start(f32[8,4,1408]{2,1,0:T(4,128)S(1)} %all-to-all-done.messages_ref), channel_id=1, source_target_pairs={{0,8},{8,0},{1,9},{9,1},{2,10},{10,2},{3,11},{11,3},{4,12},{12,4},... | collective-permute-start | bytes 540680 | tf_op jit(solution)/shard_map/ppermute | solution.py:285
  14.0 1.3 %shard_map.66.sums_ref = f32[2,2,16,128]{3,2,1,0:T(8,128)S(1)} custom-call(f32[2,3,16,128]{3,2,1,0:T(8,128)S(1)} %shard_map.65.wide_ref, f32[8,4,1408]{2,1,0:T(4,128)S(1)} %all-to-all-done.messages_ref), custom_call_target="tpu_custom_call" | custom-call | flops 10485760 | bytes 2097152 | tf_op jit(solution)/shard_map/pallas_call | solution.py:286
  15.3 0.0 collective-permute-done.1.sibling_ref
  15.3 0.8 %shard_map.68 = f32[2,16]{1,0:T(2,128)S(1)} custom-call(f32[2,3,16,128]{3,2,1,0:T(8,128)S(1)} %shard_map.65.wide_ref, f32[2,2,16,128]{3,2,1,0:T(8,128)S(1)} %shard_map.66.sums_ref, f32[8,4,1408]{2,1,0:T(4,128)S(1)} %all-to-all-done.messages_ref, f32[8,4,1408]{2,1,0:T(4,128)S(1)} %collective-permute-done.1.sibling_ref), custom_call_target="tpu_custom_call" | custom-call | flops 5242880 | bytes 2097152 | tf_op jit(solution)/shard_map/pallas_call | solution.py:295
  16.2 2.3 %collective-permute-start.2 = (f32[2,16]{1,0:T(2,128)S(1)}, f32[2,16]{1,0:T(2,128)S(1)}, u32[]{:S(2)}, u32[]{:S(2)}) collective-permute-start(f32[2,16]{1,0:T(2,128)S(1)} %shard_map.68), channel_id=1, source_target_pairs={{0,12},{4,8},{8,4},{12,0},{1,13},{5,9},{9,5},{13,1},{2,14},{6,10},... | collective-permute-start | bytes 392 | tf_op jit(solution)/shard_map/ppermute | solution.py:217
  18.5 0.8 %shard_map.67 = f32[2,16]{1,0:T(2,128)S(1)} custom-call(f32[2,3,16,128]{3,2,1,0:T(8,128)S(1)} %shard_map.65.wide_ref, f32[2,2,16,128]{3,2,1,0:T(8,128)S(1)} %shard_map.66.sums_ref, f32[8,4,1408]{2,1,0:T(4,128)S(1)} %all-to-all-done.messages_ref, f32[8,4,1408]{2,1,0:T(4,128)S(1)} %collective-permute-done.1.sibling_ref), custom_call_target="tpu_custom_call" | custom-call | flops 5242880 | bytes 2097152 | tf_op jit(solution)/shard_map/pallas_call | solution.py:295
  19.3 0.8 %collective-permute-done.2 = f32[2,16]{1,0:T(2,128)S(1)} collective-permute-done((f32[2,16]{1,0:T(2,128)S(1)}, f32[2,16]{1,0:T(2,128)S(1)}, u32[]{:S(2)}, u32[]{:S(2)}) %collective-permute-start.2) | collective-permute-done | bytes 160 | tf_op jit(solution)/shard_map/ppermute | solution.py:217
  20.1 0.6 %add.3 = f32[2,16]{1,0:T(2,128)} add(f32[2,16]{1,0:T(2,128)S(1)} %shard_map.67, f32[2,16]{1,0:T(2,128)S(1)} %collective-permute-done.2) | non-fusion elementwise | flops 32 | bytes 384 | tf_op jit(solution)/shard_map/add | solution.py:304
Async XLA Ops:
  1.8 5.6 %copy-start = (f32[3,16]{1,0:T(4,128)S(1)}, f32[3,16]{1,0:T(4,128)}, u32[]{:S(2)}) copy-start(f32[3,16]{1,0:T(4,128)} %tests_ref.1) | copy-start | bytes 580
  1.8 11.7 %all-to-all-start = ((f32[8,4,1408]{2,1,0:T(4,128)}), f32[8,4,1408]{2,1,0:T(4,128)S(1)}, u32[]{:S(2)}, u32[]{:S(2)}) async-start(f32[8,4,1408]{2,1,0:T(4,128)} %shard_map.64), calls=%async_computation | async-start | bytes 360448 | tf_op jit(solution)/shard_map/all_to_all | solution.py:260
  7.5 4.3 %collective-permute-start = (f32[3,16]{1,0:T(4,128)S(1)}, f32[3,16]{1,0:T(4,128)S(1)}, u32[]{:S(2)}, u32[]{:S(2)}) collective-permute-start(f32[3,16]{1,0:T(4,128)S(1)} %copy-done), channel_id=1, source_target_pairs={{0,12},{4,8},{8,4},{12,0},{1,13},{5,9},{9,5},{13,1},{2,14},{6,10},... | collective-permute-start | bytes 584 | tf_op jit(solution)/shard_map/ppermute | solution.py:217
  13.5 1.8 %collective-permute-start.1 = (f32[8,4,1408]{2,1,0:T(4,128)S(1)}, f32[8,4,1408]{2,1,0:T(4,128)S(1)}, u32[]{:S(2)}, u32[]{:S(2)}) collective-permute-start(f32[8,4,1408]{2,1,0:T(4,128)S(1)} %all-to-all-done.messages_ref), channel_id=1, source_target_pairs={{0,8},{8,0},{1,9},{9,1},{2,10},{10,2},{3,11},{11,3},{4,12},{12,4},... | collective-permute-start | bytes 540680 | tf_op jit(solution)/shard_map/ppermute | solution.py:285
  16.2 4.0 %collective-permute-start.2 = (f32[2,16]{1,0:T(2,128)S(1)}, f32[2,16]{1,0:T(2,128)S(1)}, u32[]{:S(2)}, u32[]{:S(2)}) collective-permute-start(f32[2,16]{1,0:T(2,128)S(1)} %shard_map.68), channel_id=1, source_target_pairs={{0,12},{4,8},{8,4},{12,0},{1,13},{5,9},{9,5},{13,1},{2,14},{6,10},... | collective-permute-start | bytes 392 | tf_op jit(solution)/shard_map/ppermute | solution.py:217
